TPU v7x, 32 devices: a whole 2x2x4 slice. The times are simulated.
32 devices in a mesh: dp: 8 (over y, x, core), tensor: 4 (over z).
Axes of the slice: x: 2, y: 2, z: 4, core: 2. Of those that a mesh axis runs over, the one named last changes fastest.
Arguments:
- residual: bfloat16 [16384, 1024], P(('dp', 'tensor')), may hold values from -6 to 6
- mixer_in: bfloat16 [1024, 2, 1536], P('dp', None, 'tensor'), may hold values from -0.1875 to 0.1875
- step_in: bfloat16 [1024, 24], P('dp', 'tensor'), may hold values from -0.1875 to 0.1875
- shared_in: bfloat16 [1024, 256], P('dp', 'tensor'), may hold values from -0.1875 to 0.1875
- query_in: bfloat16 [1024, 512], P('dp', 'tensor'), may hold values from -0.1875 to 0.1875
- keyval_in: bfloat16 [1024, 256], P('dp', 'tensor'), may hold values from -0.1875 to 0.1875
- mixer_proj: bfloat16 [1536, 1024], P('tensor', 'dp'), may hold values from -0.15625 to 0.15625
- attn_proj: bfloat16 [512, 1024], P('tensor', 'dp'), may hold values from -1 to 1
- gate_up: bfloat16 [1024, 2, 2048], P('dp', None, 'tensor'), may hold values from -0.1875 to 0.1875
- down_proj: bfloat16 [2048, 1024], P('tensor', 'dp'), may hold values from -0.125 to 0.125
- norm_gain: float32 [1024], replicated, may hold values from 0.5 to 1.5
- mlp_gain: float32 [1024], replicated, may hold values from 0.5 to 1.5
- conv_filter: float32 [4, 1792], replicated, may hold values from -3 to 3
- decay_log: float32 [24], replicated, may hold values from -2 to 1.5
- skip_gain: float32 [24], replicated, may hold values from 0.5 to 1.5
- step_bias: float32 [24], replicated, may hold values from -5 to -1
- gated_gain: float32 [1536], replicated, may hold values from 0.5 to 1.5
- cotangent: bfloat16 [16384, 1024], P(('dp', 'tensor')), may hold values from -6 to 6
Outputs:
- output: float32 [16384, 1024], P(('dp', 'tensor'))
- residual_grad: float32 [16384, 1024], P(('dp', 'tensor'))
- mixer_in_grad: float32 [1024, 2, 1536], P('dp', None, 'tensor')
- step_in_grad: float32 [1024, 24], P('dp', 'tensor')
- shared_in_grad: float32 [1024, 256], P('dp', 'tensor')
- query_in_grad: float32 [1024, 512], P('dp', 'tensor')
- keyval_in_grad: float32 [1024, 256], P('dp', 'tensor')
- mixer_proj_grad: float32 [1536, 1024], P('tensor', 'dp')
- attn_proj_grad: float32 [512, 1024], P('tensor', 'dp')
- gate_up_grad: float32 [1024, 2, 2048], P('dp', None, 'tensor')
- down_proj_grad: float32 [2048, 1024], P('tensor', 'dp')
- norm_gain_grad: float32 [1024], replicated
- mlp_gain_grad: float32 [1024], replicated
- conv_filter_grad: float32 [4, 1792], replicated
- decay_log_grad: float32 [24], replicated
- skip_gain_grad: float32 [24], replicated
- step_bias_grad: float32 [24], replicated
- gated_gain_grad: float32 [1536], replicated
All inputs are finite; a program needn't handle non-finite values.
Results may differ from a plain program's by a relative error of at most 0.019.
Values may be sent and summed in bfloat16 or wider, within the bound.
No kernel may reach another device: no remote copies, remote signals or barrier semaphores. Data moves between devices by JAX's collectives and lax.ppermute only.
A program may use at most 192 MiB of HBM per device.

v0:
```python
import jax
import jax.numpy as jnp
from jax import lax
from jax.sharding import PartitionSpec as P

PH = 64
NS = 128
KC = 4
AH = 8
KVH = 2
HD = 64
LEN = 1024
SBLK = 256
QBLK = 512


epsilon = 1e-05
rope_base = 100000000000.0
masked_fill = -1e30
highest = lax.Precision.HIGHEST


def matmul(left, right):
    return jnp.dot(left, right, preferred_element_type=jnp.float32)


def rows_of(array, first_row, row_count):
    return lax.dynamic_slice_in_dim(array, first_row, row_count, 0)


def state_scan(block_item):
    head_in, step_size, log_decay, matrix_b, matrix_c = block_item
    local_heads = head_in.shape[1]
    block_count = LEN // SBLK
    weighted = (head_in * step_size[:, :, None]).reshape(block_count, SBLK, local_heads, PH)
    decay_blocks = log_decay.reshape(block_count, SBLK, local_heads)
    b_blocks = matrix_b.reshape(block_count, SBLK, NS)
    c_blocks = matrix_c.reshape(block_count, SBLK, NS)
    cumulated = jnp.cumsum(decay_blocks, axis=1)
    position = jnp.arange(SBLK, dtype=jnp.int32)
    causal = position[:, None] >= position[None, :]
    gaps = cumulated[:, :, None, :] - cumulated[:, None, :, :]
    decays = jnp.exp(jnp.where(causal[None, :, :, None], gaps, masked_fill))
    affinity = jnp.einsum("bin,bjn->bij", c_blocks, b_blocks, precision=highest)
    inside = jnp.einsum(
        "bijh,bjhp->bihp", affinity[:, :, :, None] * decays, weighted, precision=highest
    )
    to_end = jnp.exp(cumulated[:, -1:, :] - cumulated)
    states = jnp.einsum("bjh,bjhp,bjn->bhpn", to_end, weighted, b_blocks, precision=highest)
    block_fall = jnp.exp(cumulated[:, -1, :])

    def carry_step(state_now, pair_item):
        fall_now, added = pair_item
        return (fall_now[:, None, None] * state_now + added, state_now)

    _, entering = lax.scan(
        carry_step, jnp.zeros((local_heads, PH, NS), jnp.float32), (block_fall, states)
    )
    carried = (
        jnp.einsum("bin,bhpn->bihp", c_blocks, entering, precision=highest)
        * jnp.exp(cumulated)[:, :, :, None]
    )
    return (inside + carried).reshape(LEN, local_heads, PH)


def mamba_inner(
    gate_mix, value_mix, shared_proj, step_proj, conv_filter, step_bias, decay_log, skip_gain
):
    row_total, local_width = value_mix.shape
    local_heads = step_proj.shape[1]
    seq_count = row_total // LEN
    joined = jnp.concatenate([value_mix, shared_proj], axis=1).reshape(
        seq_count, LEN, local_width + 2 * NS
    )
    padded = jnp.pad(joined, ((0, 0), (KC - 1, 0), (0, 0)))
    convolved = padded[:, 0:LEN, :] * conv_filter[0]
    for offset in range(1, KC):
        convolved = convolved + padded[:, offset : offset + LEN, :] * conv_filter[offset]
    activated = jax.nn.silu(convolved)
    head_in = activated[:, :, :local_width].reshape(seq_count, LEN, local_heads, PH)
    matrix_b = activated[:, :, local_width : local_width + NS]
    matrix_c = activated[:, :, local_width + NS :]
    step_size = jax.nn.softplus(step_proj.reshape(seq_count, LEN, local_heads) + step_bias)
    log_decay = -jnp.exp(decay_log) * step_size
    scanned = lax.map(
        jax.checkpoint(state_scan), (head_in, step_size, log_decay, matrix_b, matrix_c)
    )
    scanned = scanned + skip_gain[:, None] * head_in
    return scanned.reshape(row_total, local_width) * jax.nn.silu(gate_mix)


def rotary(tensor_in):
    half_size = HD // 2
    frequency = rope_base ** (-2.0 * jnp.arange(half_size, dtype=jnp.float32) / HD)
    angles = jnp.arange(LEN, dtype=jnp.float32)[:, None] * frequency[None, :]
    cosine = jnp.cos(angles)[None, :, None, :]
    sine = jnp.sin(angles)[None, :, None, :]
    front_half = tensor_in[..., :half_size]
    back_half = tensor_in[..., half_size:]
    return jnp.concatenate(
        [front_half * cosine - back_half * sine, back_half * cosine + front_half * sine], axis=-1
    )


def attend(query_proj, keyval_proj):
    row_total = query_proj.shape[0]
    seq_count = row_total // LEN
    query_heads = query_proj.shape[1] // HD
    key_heads = keyval_proj.shape[1] // (2 * HD)
    group_size = query_heads // key_heads
    queries = rotary(query_proj.reshape(seq_count, LEN, query_heads, HD))
    key_value = keyval_proj.reshape(seq_count, LEN, key_heads, 2, HD)
    keys_rot = jnp.repeat(rotary(key_value[:, :, :, 0]), group_size, axis=2)
    values = jnp.repeat(key_value[:, :, :, 1], group_size, axis=2)
    score_scale = HD ** (-0.5)

    def one_seq(seq_item):
        seq_queries, seq_keys, seq_values = seq_item

        def one_block(first_row):
            block_queries = lax.dynamic_slice_in_dim(seq_queries, first_row, QBLK, 0)
            scores = (
                jnp.einsum("qhd,khd->hqk", block_queries, seq_keys, precision=highest) * score_scale
            )
            visible = (first_row + jnp.arange(QBLK, dtype=jnp.int32))[:, None] >= jnp.arange(
                LEN, dtype=jnp.int32
            )[None, :]
            scores = jnp.where(visible[None], scores, masked_fill)
            row_max = jnp.max(scores, axis=-1, keepdims=True)
            weights = jnp.exp(scores - row_max)
            weights = weights / jnp.sum(weights, axis=-1, keepdims=True)
            return jnp.einsum("hqk,khd->qhd", weights, seq_values, precision=highest)

        starts = jnp.arange(LEN // QBLK, dtype=jnp.int32) * QBLK
        return lax.map(jax.checkpoint(one_block), starts).reshape(LEN, query_heads, HD)

    attended = lax.map(one_seq, (queries, keys_rot, values))
    return attended.reshape(row_total, query_heads * HD)


def shards(
    residual,
    mixer_in,
    step_in,
    shared_in,
    query_in,
    keyval_in,
    mixer_proj,
    attn_proj,
    gate_up,
    down_proj,
    norm_gain,
    mlp_gain,
    conv_filter,
    decay_log,
    skip_gain,
    step_bias,
    gated_gain,
    cotangent,
):
    tensor_idx = lax.axis_index("tensor")
    tensor_count = lax.axis_size("tensor")
    gathered = (
        lax.all_gather(mixer_in, "dp", axis=0, tiled=True),
        lax.all_gather(step_in, "dp", axis=0, tiled=True),
        lax.all_gather(shared_in, "dp", axis=0, tiled=True),
        lax.all_gather(query_in, "dp", axis=0, tiled=True),
        lax.all_gather(keyval_in, "dp", axis=0, tiled=True),
        lax.all_gather(mixer_proj, "dp", axis=1, tiled=True),
        lax.all_gather(attn_proj, "dp", axis=1, tiled=True),
        lax.all_gather(gate_up, "dp", axis=0, tiled=True),
        lax.all_gather(down_proj, "dp", axis=1, tiled=True),
    )
    (
        mixer_full,
        step_full,
        shared_piece,
        query_full,
        keyval_piece,
        mixer_out_w,
        attn_out_w,
        gate_up_full,
        down_full,
    ) = gathered
    rows_low, shared_full, keyval_full = (
        lax.all_gather(residual, "tensor", axis=0, tiled=True),
        lax.all_gather(shared_piece, "tensor", axis=1, tiled=True),
        lax.all_gather(keyval_piece, "tensor", axis=1, tiled=True),
    )
    share_rows = residual.shape[0]
    group_rows = rows_low.astype(jnp.float32)
    inv_first = lax.rsqrt(jnp.mean(group_rows * group_rows, axis=-1, keepdims=True) + epsilon)
    normed_first = group_rows * inv_first
    normed_in = (normed_first * norm_gain).astype(jnp.bfloat16)
    mixed_proj = jnp.einsum(
        "rd,dkc->rkc", normed_in, mixer_full, preferred_element_type=jnp.float32
    )
    gate_mix = mixed_proj[:, 0]
    value_mix = mixed_proj[:, 1]
    shared_proj = matmul(normed_in, shared_full)
    step_proj = matmul(normed_in, step_full)
    query_proj = matmul(normed_in, query_full)
    local_width = value_mix.shape[1]
    local_heads = step_proj.shape[1]
    local_queries = query_proj.shape[1] // HD
    kv_head = tensor_idx * local_queries // (AH // KVH)
    keyval_cols = lax.dynamic_slice_in_dim(keyval_full, kv_head * 2 * HD, 2 * HD, 1)
    keyval_proj = matmul(normed_in, keyval_cols)
    ssm_width = conv_filter.shape[1] - 2 * NS
    filter_local = jnp.concatenate(
        [
            lax.dynamic_slice_in_dim(conv_filter, tensor_idx * local_width, local_width, 1),
            conv_filter[:, ssm_width:],
        ],
        axis=1,
    )
    bias_local = lax.dynamic_slice_in_dim(step_bias, tensor_idx * local_heads, local_heads, 0)
    decay_local = lax.dynamic_slice_in_dim(decay_log, tensor_idx * local_heads, local_heads, 0)
    skip_local = lax.dynamic_slice_in_dim(skip_gain, tensor_idx * local_heads, local_heads, 0)
    gated_local = lax.dynamic_slice_in_dim(gated_gain, tensor_idx * local_width, local_width, 0)
    gated_pre, mamba_back = jax.vjp(
        mamba_inner,
        gate_mix,
        value_mix,
        shared_proj,
        step_proj,
        filter_local,
        bias_local,
        decay_local,
        skip_local,
    )
    square_sum = lax.psum(jnp.sum(gated_pre * gated_pre, axis=-1), "tensor")
    inv_gated = lax.rsqrt(square_sum / (local_width * tensor_count) + epsilon)[:, None]
    gated_normed = gated_pre * inv_gated
    mixer_heads = (gated_normed * gated_local).astype(jnp.bfloat16)
    attn_f32, attend_back = jax.vjp(attend, query_proj, keyval_proj)
    attn_heads = attn_f32.astype(jnp.bfloat16)
    first_row = jnp.int32(0)
    branch = lax.psum_scatter(
        (
            matmul(
                rows_of(mixer_heads, first_row, share_rows * lax.axis_size("tensor")), mixer_out_w
            )
            + matmul(
                rows_of(attn_heads, first_row, share_rows * lax.axis_size("tensor")), attn_out_w
            )
        ).astype(jnp.bfloat16),
        "tensor",
        scatter_dimension=0,
        tiled=True,
    ).astype(jnp.float32)
    middle = residual.astype(jnp.float32) + branch
    inv_second = lax.rsqrt(jnp.mean(middle * middle, axis=-1, keepdims=True) + epsilon)
    second_normed = middle * inv_second
    mlp_share = (second_normed * mlp_gain).astype(jnp.bfloat16)
    mlp_rows = lax.all_gather(mlp_share, "tensor", axis=0, tiled=True)
    gate_both = jnp.einsum(
        "rd,dkf->rkf", mlp_rows, gate_up_full, preferred_element_type=jnp.float32
    )
    gate_val = gate_both[:, 0]
    up_val = gate_both[:, 1]
    sig_gate = jax.nn.sigmoid(gate_val)
    silu_gate = gate_val * sig_gate
    hidden = (silu_gate * up_val).astype(jnp.bfloat16)
    output = middle + lax.psum_scatter(
        matmul(
            rows_of(hidden, jnp.int32(0), share_rows * lax.axis_size("tensor")), down_full
        ).astype(jnp.bfloat16),
        "tensor",
        scatter_dimension=0,
        tiled=True,
    ).astype(jnp.float32)
    grad_rows = lax.all_gather(cotangent, "tensor", axis=0, tiled=True)
    refetched = (
        lax.all_gather(mixer_in, "dp", axis=0, tiled=True),
        lax.all_gather(step_in, "dp", axis=0, tiled=True),
        lax.all_gather(query_in, "dp", axis=0, tiled=True),
        lax.all_gather(mixer_proj, "dp", axis=1, tiled=True),
        lax.all_gather(attn_proj, "dp", axis=1, tiled=True),
        lax.all_gather(gate_up, "dp", axis=0, tiled=True),
        lax.all_gather(down_proj, "dp", axis=1, tiled=True),
    )
    mixer_full, step_full, query_full, mixer_out_w, attn_out_w, gate_up_full, down_full = refetched
    down_grad = jnp.einsum("rf,rd->fd", hidden, grad_rows, preferred_element_type=jnp.float32)
    hidden_grad = jnp.einsum("rd,fd->rf", grad_rows, down_full, preferred_element_type=jnp.float32)
    gate_grad = hidden_grad * up_val * sig_gate * (1.0 + gate_val * (1.0 - sig_gate))
    up_grad = hidden_grad * silu_gate
    both_grad = jnp.stack([gate_grad, up_grad], axis=1).astype(jnp.bfloat16)
    gate_up_grad = jnp.einsum(
        "rd,rkf->dkf", mlp_rows, both_grad, preferred_element_type=jnp.float32
    )
    mlp_in_grad = lax.psum_scatter(
        jnp.einsum(
            "rkf,dkf->rd",
            rows_of(both_grad, jnp.int32(0), share_rows * lax.axis_size("tensor")),
            gate_up_full,
            preferred_element_type=jnp.float32,
        ).astype(jnp.bfloat16),
        "tensor",
        scatter_dimension=0,
        tiled=True,
    ).astype(jnp.float32)
    mlp_gain_part = jnp.sum(mlp_in_grad * second_normed, axis=0)
    scaled_second = mlp_in_grad * mlp_gain
    middle_grad = cotangent.astype(jnp.float32) + inv_second * (
        scaled_second
        - second_normed * jnp.mean(scaled_second * second_normed, axis=-1, keepdims=True)
    )
    branch_grad = lax.all_gather(middle_grad.astype(jnp.bfloat16), "tensor", axis=0, tiled=True)
    mixer_proj_grad = jnp.einsum(
        "rc,rd->cd", mixer_heads, branch_grad, preferred_element_type=jnp.float32
    )
    attn_proj_grad = jnp.einsum(
        "rc,rd->cd", attn_heads, branch_grad, preferred_element_type=jnp.float32
    )
    heads_grad = jnp.einsum(
        "rd,cd->rc", branch_grad, mixer_out_w, preferred_element_type=jnp.float32
    )
    attn_grad = jnp.einsum("rd,cd->rc", branch_grad, attn_out_w, preferred_element_type=jnp.float32)
    gated_gain_part = jnp.sum(heads_grad * gated_normed, axis=0)
    scaled_heads = heads_grad * gated_local
    cross_sum = lax.psum(jnp.sum(scaled_heads * gated_normed, axis=-1), "tensor")
    pre_grad = inv_gated * (
        scaled_heads - gated_normed * (cross_sum / (local_width * tensor_count))[:, None]
    )
    (
        gate_mix_grad,
        value_mix_grad,
        shared_grad,
        step_grad,
        filter_grad,
        bias_grad,
        decay_grad,
        skip_grad,
    ) = mamba_back(pre_grad)
    query_grad, keyval_grad = attend_back(attn_grad)
    mixed_low = jnp.stack([gate_mix_grad, value_mix_grad], axis=1).astype(jnp.bfloat16)
    shared_low = shared_grad.astype(jnp.bfloat16)
    step_low = step_grad.astype(jnp.bfloat16)
    query_low = query_grad.astype(jnp.bfloat16)
    keyval_low = keyval_grad.astype(jnp.bfloat16)
    mixer_in_grad = jnp.einsum(
        "rd,rkc->dkc", normed_in, mixed_low, preferred_element_type=jnp.float32
    )
    step_in_grad = jnp.einsum("rd,rc->dc", normed_in, step_low, preferred_element_type=jnp.float32)
    shared_part = jnp.einsum("rd,rc->dc", normed_in, shared_low, preferred_element_type=jnp.float32)
    query_in_grad = jnp.einsum(
        "rd,rc->dc", normed_in, query_low, preferred_element_type=jnp.float32
    )
    keyval_local = jnp.einsum(
        "rd,rc->dc", normed_in, keyval_low, preferred_element_type=jnp.float32
    )
    keyval_part = lax.dynamic_update_slice_in_dim(
        jnp.zeros((normed_in.shape[1], keyval_full.shape[1]), jnp.float32),
        keyval_local,
        kv_head * 2 * HD,
        1,
    )
    normed_grad = jnp.einsum(
        "rkc,dkc->rd", mixed_low, mixer_full, preferred_element_type=jnp.float32
    )
    normed_grad = normed_grad + jnp.einsum(
        "rc,dc->rd", shared_low, shared_full, preferred_element_type=jnp.float32
    )
    normed_grad = normed_grad + jnp.einsum(
        "rc,dc->rd", step_low, step_full, preferred_element_type=jnp.float32
    )
    normed_grad = normed_grad + jnp.einsum(
        "rc,dc->rd", query_low, query_full, preferred_element_type=jnp.float32
    )
    normed_grad = normed_grad + jnp.einsum(
        "rc,dc->rd", keyval_low, keyval_cols, preferred_element_type=jnp.float32
    )
    first_grad, shared_in_grad, keyval_in_grad = (
        lax.psum_scatter(
            normed_grad.astype(jnp.bfloat16), "tensor", scatter_dimension=0, tiled=True
        ).astype(jnp.float32),
        lax.psum_scatter(
            shared_part.astype(jnp.bfloat16), "tensor", scatter_dimension=1, tiled=True
        ).astype(jnp.float32),
        lax.psum_scatter(
            keyval_part.astype(jnp.bfloat16), "tensor", scatter_dimension=1, tiled=True
        ).astype(jnp.float32),
    )
    normed_share = rows_of(normed_first, tensor_idx * share_rows, share_rows)
    inv_share = rows_of(inv_first, tensor_idx * share_rows, share_rows)
    norm_gain_part = jnp.sum(first_grad * normed_share, axis=0)
    scaled_first = first_grad * norm_gain
    residual_grad = middle_grad + inv_share * (
        scaled_first - normed_share * jnp.mean(scaled_first * normed_share, axis=-1, keepdims=True)
    )
    summed = (
        lax.psum_scatter(mixer_in_grad, "dp", scatter_dimension=0, tiled=True),
        lax.psum_scatter(step_in_grad, "dp", scatter_dimension=0, tiled=True),
        lax.psum_scatter(shared_in_grad, "dp", scatter_dimension=0, tiled=True),
        lax.psum_scatter(query_in_grad, "dp", scatter_dimension=0, tiled=True),
        lax.psum_scatter(keyval_in_grad, "dp", scatter_dimension=0, tiled=True),
        lax.psum_scatter(mixer_proj_grad, "dp", scatter_dimension=1, tiled=True),
        lax.psum_scatter(attn_proj_grad, "dp", scatter_dimension=1, tiled=True),
        lax.psum_scatter(gate_up_grad, "dp", scatter_dimension=0, tiled=True),
        lax.psum_scatter(down_grad, "dp", scatter_dimension=1, tiled=True),
    )
    (
        mixer_in_sum,
        step_in_sum,
        shared_in_sum,
        query_in_sum,
        keyval_in_sum,
        mixer_proj_sum,
        attn_proj_sum,
        gate_up_sum,
        down_sum,
    ) = summed
    filter_value_part = lax.dynamic_update_slice_in_dim(
        jnp.zeros((KC, ssm_width), jnp.float32),
        filter_grad[:, :local_width],
        tensor_idx * local_width,
        1,
    )
    filter_part = jnp.concatenate([filter_value_part, filter_grad[:, local_width:]], axis=1)
    head_total = ssm_width // PH
    decay_part = lax.dynamic_update_slice_in_dim(
        jnp.zeros((head_total,), jnp.float32), decay_grad, tensor_idx * local_heads, 0
    )
    skip_part = lax.dynamic_update_slice_in_dim(
        jnp.zeros((head_total,), jnp.float32), skip_grad, tensor_idx * local_heads, 0
    )
    bias_part = lax.dynamic_update_slice_in_dim(
        jnp.zeros((head_total,), jnp.float32), bias_grad, tensor_idx * local_heads, 0
    )
    gated_part = lax.dynamic_update_slice_in_dim(
        jnp.zeros((ssm_width,), jnp.float32), gated_gain_part, tensor_idx * local_width, 0
    )
    small_sums = lax.psum(
        (norm_gain_part, mlp_gain_part, filter_part, decay_part, skip_part, bias_part, gated_part),
        ("dp", "tensor"),
    )
    norm_gain_sum, mlp_gain_sum, filter_sum, decay_sum, skip_sum, bias_sum, gated_sum = small_sums
    return (
        output,
        residual_grad,
        mixer_in_sum,
        step_in_sum,
        shared_in_sum,
        query_in_sum,
        keyval_in_sum,
        mixer_proj_sum,
        attn_proj_sum,
        gate_up_sum,
        down_sum,
        norm_gain_sum,
        mlp_gain_sum,
        filter_sum,
        decay_sum,
        skip_sum,
        bias_sum,
        gated_sum,
    )


def solution(mesh):
    return jax.shard_map(
        shards,
        mesh=mesh,
        in_specs=(
            P(("dp", "tensor"), None),
            P("dp", None, "tensor"),
            P("dp", "tensor"),
            P("dp", "tensor"),
            P("dp", "tensor"),
            P("dp", "tensor"),
            P("tensor", "dp"),
            P("tensor", "dp"),
            P("dp", None, "tensor"),
            P("tensor", "dp"),
            P(),
            P(),
            P(),
            P(),
            P(),
            P(),
            P(),
            P(("dp", "tensor"), None),
        ),
        out_specs=(
            P(("dp", "tensor"), None),
            P(("dp", "tensor"), None),
            P("dp", None, "tensor"),
            P("dp", "tensor"),
            P("dp", "tensor"),
            P("dp", "tensor"),
            P("dp", "tensor"),
            P("tensor", "dp"),
            P("tensor", "dp"),
            P("dp", None, "tensor"),
            P("tensor", "dp"),
            P(),
            P(),
            P(),
            P(),
            P(),
            P(),
            P(),
        ),
        check_vma=False,
    )
```

profile of v0, /device:TPU:0, one launch (start us, length us, event | category | flops | bytes accessed | tf_op | source)
XLA Modules:
  0.0 2023.3 jit_solution(11648989060384646102)
XLA Ops:
  20.5 22.8 %all_gather.55 = bf16[1024,256]{0,1:T(8,128)(2,1)S(1)} all-gather(bf16[1024,64]{0,1:T(8,128)(2,1)S(1)} %all_gather.54), channel_id=1, replica_groups=mesh['dp'=8,'tensor'=4] {'tensor'}, dimensions={1}, use_global_device_ids=true | all-gather | bytes 655360 | tf_op jit(solution)/shard_map/all_gather | solution.py:187
  63.2 23.0 %all_gather.60 = bf16[1024,256]{0,1:T(8,128)(2,1)} all-gather(bf16[1024,64]{0,1:T(8,128)(2,1)S(1)} %all_gather.59), channel_id=1, replica_groups=mesh['dp'=8,'tensor'=4] {'tensor'}, dimensions={1}, use_global_device_ids=true | all-gather | bytes 655360 | tf_op jit(solution)/shard_map/all_gather | solution.py:188
  181.4 93.0 %while.234 = (s32[]{:T(128)}, f32[2,1024,6,64]{1,3,2,0:T(8,128)}, f32[2,1024,6,64]{1,3,2,0:T(8,128)}, f32[2,1024,6]{1,2,0:T(8,128)S(1)}, f32[2,1024,128]{2,1,0:T...) while((s32[]{:T(128)}, f32[2,1024,6,64]{1,3,2,0:T(8,128)}, ...), condition=%wide.region_6.7_spmd.clone, body=%wide.region_1.6_spmd.clone.sunk | while | flops 2825852928 | bytes 51622372 | solution.py:85
  298.7 11.8 psum.63
  333.9 56.2 %while.229 = (s32[]{:T(128)}, bf16[2,1024,2,64]{3,2,1,0:T(2,128)(2,1)}, f32[2,1024,2,64]{1,3,2,0:T(8,128)}, f32[2,1024,2,64]{1,3,2,0:T(8,128)}, f32[2,1024,2,64]...) while((s32[]{:T(128)}, ...), condition=%wide.region_16.17_spmd, body=%wide.region_11.16_spmd.sunk | while | flops 1617950720 | bytes 21779260 | solution.py:137
  337.3 23.3 %while.238 = (s32[]{:T(128)}, bf16[2,512,2,64]{1,3,2,0:T(8,128)(2,1)S(1)}, pred[2,2,512,1024]{3,2,1,0:T(32,128)(4,1)S(1)}, s32[2]{0:T(128)S(1)}, f32[1024,2,64]{...) while((s32[]{:T(128)}, bf16[2,512,2,64]{1,3,2,0:T(8,128)(2,1)S(1)}, ...), condition=%wide.region_15.15_spmd, body=%wide.region_12.14_spmd.sunk | while | flops 1617950720 | bytes 17322120 | solution.py:135
  365.3 23.3 %while.238 = (s32[]{:T(128)}, bf16[2,512,2,64]{1,3,2,0:T(8,128)(2,1)S(1)}, pred[2,2,512,1024]{3,2,1,0:T(32,128)(4,1)S(1)}, s32[2]{0:T(128)S(1)}, f32[1024,2,64]{...) while((s32[]{:T(128)}, bf16[2,512,2,64]{1,3,2,0:T(8,128)(2,1)S(1)}, ...), condition=%wide.region_15.15_spmd, body=%wide.region_12.14_spmd.sunk | while | flops 1617950720 | bytes 17322120 | solution.py:135
  404.1 72.4 %reduce-scatter.16.cloned.1.call-done = bf16[512,1024]{1,0:T(8,128)(2,1)} async-done(((bf16[2048,1024]{1,0:T(8,128)(2,1)}), bf16[512,1024]{1,0:T(8,128)(2,1)}) %reduce-scatter.16.cloned.1.call-update) | async-done | bytes 1048592 | tf_op jit(solution)/shard_map/reduce_scatter | solution.py:239
  482.4 25.1 %all-gather.14.cloned.1.call-done = bf16[1024,2,512]{2,0,1:T(8,128)(2,1)} async-done(((bf16[128,2,512]{2,0,1:T(8,128)(2,1)}), bf16[1024,2,512]{2,0,1:T(8,128)(2,1)}) %all-gather.14.cloned.1.call-update) | async-done | bytes 2097168 | tf_op jit(solution)/shard_map/all_gather | solution.py:171
  507.4 82.9 %all-gather.12.cloned.1.call-done = bf16[2048,1024]{1,0:T(8,128)(2,1)} async-done(((bf16[512,1024]{1,0:T(8,128)(2,1)}), bf16[2048,1024]{1,0:T(8,128)(2,1)}) %all-gather.12.cloned.1.call-update) | async-done | bytes 4194320 | tf_op jit(solution)/shard_map/all_gather | solution.py:256
  601.1 13.2 all-gather.16.cloned.1.call-done
  614.3 82.4 %all-gather.18.cloned.1.call-done = bf16[2048,1024]{1,0:T(8,128)(2,1)} async-done(((bf16[512,1024]{1,0:T(8,128)(2,1)}), bf16[2048,1024]{1,0:T(8,128)(2,1)}) %all-gather.18.cloned.1.call-update) | async-done | bytes 4194320 | tf_op jit(solution)/shard_map/all_gather | solution.py:273
  715.8 75.4 %reduce-scatter.20.cloned.1.call-done = bf16[512,1024]{1,0:T(8,128)(2,1)} async-done(((bf16[2048,1024]{1,0:T(8,128)(2,1)}), bf16[512,1024]{1,0:T(8,128)(2,1)}) %reduce-scatter.20.cloned.1.call-update) | async-done | bytes 1048592 | tf_op jit(solution)/shard_map/reduce_scatter | solution.py:292
  800.7 78.5 %all-gather.20.cloned.1.call-done = bf16[2048,1024]{1,0:T(8,128)(2,1)} async-done(((bf16[512,1024]{1,0:T(8,128)(2,1)}), bf16[2048,1024]{1,0:T(8,128)(2,1)}) %all-gather.20.cloned.1.call-update) | async-done | bytes 4194320 | tf_op jit(solution)/shard_map/all_gather | solution.py:309
  925.0 282.3 %while.232 = (s32[]{:T(128)}, f32[2,1024,6,64]{1,3,2,0:T(8,128)}, f32[2,1024,6]{1,2,0:T(8,128)}, f32[2,1024,6]{1,2,0:T(8,128)}, f32[2,1024,128]{1,2,0:T(8,128)},...) while((s32[]{:T(128)}, f32[2,1024,6,64]{1,3,2,0:T(8,128)}, ...), condition=%wide.region_40.41_spmd, body=%wide.region_24.40_spmd.sunk | while | flops 7273916416 | bytes 164118672 | solution.py:85
  1027.2 30.2 %reduce-window.76 = f32[4,6,2,128]{3,2,1,0:T(2,128)S(1)} reduce-window(f32[4,6,2,128]{3,2,1,0:T(2,128)S(1)} %reshape.632, f32[]{:T(128)} %constant.431.clone.1..sunk), window={size=1x1x1x128 pad=0_0x0_0x0_0x0_127}, to_apply=%region_37.37 | reduce-window | flops 780288 | bytes 49156 | tf_op jit(solution)/shard_map/reduce-window.36
  1153.9 30.2 %reduce-window.76 = f32[4,6,2,128]{3,2,1,0:T(2,128)S(1)} reduce-window(f32[4,6,2,128]{3,2,1,0:T(2,128)S(1)} %reshape.632, f32[]{:T(128)} %constant.431.clone.1..sunk), window={size=1x1x1x128 pad=0_0x0_0x0_0x0_127}, to_apply=%region_37.37 | reduce-window | flops 780288 | bytes 49156 | tf_op jit(solution)/shard_map/reduce-window.36
  1246.9 206.4 %while.237 = (s32[]{:T(128)}, f32[2,1024,2,64]{1,0,3,2:T(2,128)}, f32[2,1024,2,64]{1,3,2,0:T(8,128)}, f32[2,1024,2,64]{1,3,2,0:T(8,128)}, f32[2,1024,2,64]{1,0,3...) while((s32[]{:T(128)}, f32[2,1024,2,64]{1,0,3,2:T(2,128)}, ...), condition=%wide.region_49.50_spmd.clone, body=%wide.region_41.49_spmd.clone.sunk | while | flops 4064346624 | bytes 110195312 | solution.py:137
  1271.3 71.7 %while.242 = (s32[]{:T(128)}, f32[1024,2,64]{0,2,1:T(8,128)S(1)}, f32[1024,2,64]{0,2,1:T(8,128)S(1)}, f32[1024,2,64]{0,2,1:T(8,128)}, s32[2]{0:T(128)S(1)}, /*in...) while((s32[]{:T(128)}, f32[1024,2,64]{0,2,1:T(8,128)S(1)}, ...), condition=%wide.region_48.48_spmd.clone, body=%wide.region_42.47_spmd.clone.sunk | while | flops 4064346624 | bytes 91844904 | solution.py:135
  1361.8 71.7 %while.242 = (s32[]{:T(128)}, f32[1024,2,64]{0,2,1:T(8,128)S(1)}, f32[1024,2,64]{0,2,1:T(8,128)S(1)}, f32[1024,2,64]{0,2,1:T(8,128)}, s32[2]{0:T(128)S(1)}, /*in...) while((s32[]{:T(128)}, f32[1024,2,64]{0,2,1:T(8,128)S(1)}, ...), condition=%wide.region_48.48_spmd.clone, body=%wide.region_42.47_spmd.clone.sunk | while | flops 4064346624 | bytes 91844904 | solution.py:135
  1500.3 12.4 fusion.125
  1553.4 30.2 %reduce-scatter.24.cloned.1.call-done = f32[128,2,384]{2,0,1:T(8,128)} async-done(((f32[1024,2,384]{2,0,1:T(8,128)}), f32[128,2,384]{2,0,1:T(8,128)}) %reduce-scatter.24.cloned.1.call-update) | async-done | bytes 393232 | tf_op jit(solution)/shard_map/reduce_scatter | solution.py:393
  1585.6 76.9 %reduce-scatter.22.cloned.1.call-done = bf16[512,1024]{1,0:T(8,128)(2,1)} async-done(((bf16[2048,1024]{1,0:T(8,128)(2,1)}), bf16[512,1024]{1,0:T(8,128)(2,1)}) %reduce-scatter.22.cloned.1.call-update) | async-done | bytes 1048592 | tf_op jit(solution)/shard_map/reduce_scatter | solution.py:375
  1665.0 46.6 %all-reduce.20 = (f32[1024]{0:T(1024)}, f32[1024]{0:T(1024)}, f32[4,1792]{1,0:T(4,128)}, f32[24]{0:T(128)}, f32[24]{0:T(128)}, /*index=5*/f32[24]{0:T(128)}, f32[1536]{0:T(1024)}) all-reduce(f32[1024]{0:T(1024)S(1)} %get-tuple-element.1685, f32[1024]{0:T(1024)S(1)} %copy-done.104, ...), channel_id=1, replica_groups=mesh['dp'=8,'tensor'=4] {'dp','tensor'}, use_global_device_ids=true, to_apply=%region_66.67 | all-reduce | flops 10824 | bytes 86592 | tf_op jit(solution)/shard_map/psum | solution.py:434
  1711.6 31.5 %reduce-scatter.18.cloned.1.call-done = bf16[512,1024]{1,0:T(8,128)(2,1)} async-done(((bf16[2048,1024]{1,0:T(8,128)(2,1)}), bf16[512,1024]{1,0:T(8,128)(2,1)}) %reduce-scatter.18.cloned.1.call-update) | async-done | bytes 1048592 | tf_op jit(solution)/shard_map/reduce_scatter | solution.py:265
  1747.6 41.0 %reduce-scatter.44.cloned.1.call-done = f32[512,128]{1,0:T(8,128)} async-done(((f32[512,1024]{1,0:T(8,128)}), f32[512,128]{1,0:T(8,128)}) %reduce-scatter.44.cloned.1.call-update) | async-done | bytes 262160 | tf_op jit(solution)/shard_map/reduce_scatter | solution.py:401
  1788.5 35.0 %reduce-scatter.26.cloned.1.call-done = f32[128,6]{0,1:T(8,128)} async-done(((f32[1024,6]{0,1:T(8,128)}), f32[128,6]{0,1:T(8,128)}) %reduce-scatter.26.cloned.1.call-update) | async-done | bytes 3088 | tf_op jit(solution)/shard_map/reduce_scatter | solution.py:394
  1823.5 37.7 %reduce-scatter.40.cloned.1.call-done = f32[128,128]{1,0:T(8,128)} async-done(((f32[128,1024]{1,0:T(8,128)}), f32[128,128]{1,0:T(8,128)}) %reduce-scatter.40.cloned.1.call-update) | async-done | bytes 65552 | tf_op jit(solution)/shard_map/reduce_scatter | solution.py:399
  1861.2 38.1 %reduce-scatter.32.cloned.1.call-done = f32[128,128]{1,0:T(8,128)} async-done(((f32[1024,128]{1,0:T(8,128)}), f32[128,128]{1,0:T(8,128)}) %reduce-scatter.32.cloned.1.call-update) | async-done | bytes 65552 | tf_op jit(solution)/shard_map/reduce_scatter | solution.py:396
  1899.3 37.1 %reduce-scatter.30.cloned.1.call-done = f32[128,64]{0,1:T(8,128)} async-done(((f32[1024,64]{0,1:T(8,128)}), f32[128,64]{0,1:T(8,128)}) %reduce-scatter.30.cloned.1.call-update) | async-done | bytes 32784 | tf_op jit(solution)/shard_map/reduce_scatter | solution.py:395
  1936.3 37.5 %reduce-scatter.36.cloned.1.call-done = f32[128,64]{0,1:T(8,128)} async-done(((f32[1024,64]{0,1:T(8,128)}), f32[128,64]{0,1:T(8,128)}) %reduce-scatter.36.cloned.1.call-update) | async-done | bytes 32784 | tf_op jit(solution)/shard_map/reduce_scatter | solution.py:397
  1973.9 42.4 %reduce-scatter.38.cloned.1.call-done = f32[384,128]{1,0:T(8,128)} async-done(((f32[384,1024]{1,0:T(8,128)}), f32[384,128]{1,0:T(8,128)}) %reduce-scatter.38.cloned.1.call-update) | async-done | bytes 196624 | tf_op jit(solution)/shard_map/reduce_scatter | solution.py:398
  (959 shorter events, 969.7 us)
Async XLA Ops:
  7.2 120.3 %all-gather.8.cloned.1.call-start = ((), (), s32[]{:S(2)}) async-start(), calls=%async_computation.15 | async-start | bytes 5242880 | tf_op jit(solution)/shard_map/all_gather | solution.py:186
  8.0 128.6 %all-gather.10.cloned.1.call-start = ((), (), s32[]{:S(2)}) async-start(), calls=%async_computation.16 | async-start | bytes 1769472 | tf_op jit(solution)/shard_map/all_gather | solution.py:164
  9.7 466.8 %reduce-scatter.16.cloned.1.call-start = ((), (), s32[]{:S(2)}) async-start(), calls=%async_computation.17 | async-start | bytes 5242880 | tf_op jit(solution)/shard_map/reduce_scatter | solution.py:239
  54.9 229.3 %copy-start.114 = (f32[6]{0:T(128)}, f32[6]{0:T(128)S(1)}, u32[]{:S(2)}) copy-start(f32[6]{0:T(128)S(1)} %dynamic_slice.249) | copy-start | bytes 76
  86.8 241.4 %copy-start.47 = (f32[1024,32]{0,1:T(8,128)}, f32[1024,32]{0,1:T(8,128)S(1)}, u32[]{:S(2)}) copy-start(f32[1024,32]{0,1:T(8,128)S(1)} %get-tuple-element.1919) | copy-start | bytes 393220
  86.8 241.4 %copy-start.49 = (f32[1024,32]{0,1:T(8,128)}, f32[1024,32]{0,1:T(8,128)S(1)}, u32[]{:S(2)}) copy-start(f32[1024,32]{0,1:T(8,128)S(1)} %get-tuple-element.1920) | copy-start | bytes 393220
  402.3 105.1 %all-gather.14.cloned.1.call-start = ((), (), s32[]{:S(2)}) async-start(), calls=%async_computation.19 | async-start | bytes 2359296 | tf_op jit(solution)/shard_map/all_gather | solution.py:171
  404.0 186.3 %all-gather.12.cloned.1.call-start = ((), (), s32[]{:S(2)}) async-start(), calls=%async_computation.18 | async-start | bytes 5242880 | tf_op jit(solution)/shard_map/all_gather | solution.py:256
  478.1 315.8 %copy-start.85 = (f32[512]{0:T(512)}, f32[512]{0:T(512)S(1)}, u32[]{:S(2)}) copy-start(f32[512]{0:T(512)S(1)} %add_rsqrt_fusion.2) | copy-start | bytes 6148
  480.8 133.6 %all-gather.16.cloned.1.call-start = ((), (), s32[]{:S(2)}) async-start(), calls=%async_computation.20 | async-start | bytes 1179648 | tf_op jit(solution)/shard_map/all_gather | solution.py:172
  481.3 215.4 %all-gather.18.cloned.1.call-start = ((), (), s32[]{:S(2)}) async-start(), calls=%async_computation.22 | async-start | bytes 5242880 | tf_op jit(solution)/shard_map/all_gather | solution.py:273
  482.1 309.1 %reduce-scatter.20.cloned.1.call-start = ((), (), s32[]{:S(2)}) async-start(), calls=%async_computation.23 | async-start | bytes 5242880 | tf_op jit(solution)/shard_map/reduce_scatter | solution.py:292
  715.7 163.5 %all-gather.20.cloned.1.call-start = ((), (), s32[]{:S(2)}) async-start(), calls=%async_computation.24 | async-start | bytes 5242880 | tf_op jit(solution)/shard_map/all_gather | solution.py:309
  797.8 741.9 %reduce-scatter.28.cloned.1.call-start = ((), (), s32[]{:S(2)}) async-start(), calls=%async_computation.28 | async-start | bytes 655360 | tf_op jit(solution)/shard_map/reduce_scatter | solution.py:378
  925.0 282.3 %copy-start.115 = (f32[6]{0:T(128)S(1)}, f32[6]{0:T(128)}, u32[]{:S(2)}) copy-start(f32[6]{0:T(128)} %copy-done.114) | copy-start | bytes 76
  1243.4 298.1 %reduce-scatter.34.cloned.1.call-start = ((), (), s32[]{:S(2)}) async-start(), calls=%async_computation.31 | async-start | bytes 655360 | tf_op jit(solution)/shard_map/reduce_scatter | solution.py:381
  1459.9 89.8 %reduce-scatter.42.cloned.1.call-start = ((), (), s32[]{:S(2)}) async-start(), calls=%async_computation.35 | async-start | bytes 4718592 | tf_op jit(solution)/shard_map/reduce_scatter | solution.py:400
  1469.4 114.1 %reduce-scatter.24.cloned.1.call-start = ((), (), s32[]{:S(2)}) async-start(), calls=%async_computation.26 | async-start | bytes 3538944 | tf_op jit(solution)/shard_map/reduce_scatter | solution.py:393
  1480.6 181.8 %reduce-scatter.22.cloned.1.call-start = ((), (), s32[]{:S(2)}) async-start(), calls=%async_computation.25 | async-start | bytes 5242880 | tf_op jit(solution)/shard_map/reduce_scatter | solution.py:375
  1512.7 230.4 %reduce-scatter.18.cloned.1.call-start = ((), (), s32[]{:S(2)}) async-start(), calls=%async_computation.21 | async-start | bytes 5242880 | tf_op jit(solution)/shard_map/reduce_scatter | solution.py:265
  1519.9 268.6 %reduce-scatter.44.cloned.1.call-start = ((), (), s32[]{:S(2)}) async-start(), calls=%async_computation.36 | async-start | bytes 2359296 | tf_op jit(solution)/shard_map/reduce_scatter | solution.py:401
  1527.3 296.2 %reduce-scatter.26.cloned.1.call-start = ((), (), s32[]{:S(2)}) async-start(), calls=%async_computation.27 | async-start | bytes 36864 | tf_op jit(solution)/shard_map/reduce_scatter | solution.py:394
  1530.9 330.3 %reduce-scatter.40.cloned.1.call-start = ((), (), s32[]{:S(2)}) async-start(), calls=%async_computation.34 | async-start | bytes 589824 | tf_op jit(solution)/shard_map/reduce_scatter | solution.py:399
  1535.0 364.2 %reduce-scatter.32.cloned.1.call-start = ((), (), s32[]{:S(2)}) async-start(), calls=%async_computation.30 | async-start | bytes 589824 | tf_op jit(solution)/shard_map/reduce_scatter | solution.py:396
  1539.7 396.7 %reduce-scatter.30.cloned.1.call-start = ((), (), s32[]{:S(2)}) async-start(), calls=%async_computation.29 | async-start | bytes 294912 | tf_op jit(solution)/shard_map/reduce_scatter | solution.py:395
  1541.4 432.5 %reduce-scatter.36.cloned.1.call-start = ((), (), s32[]{:S(2)}) async-start(), calls=%async_computation.32 | async-start | bytes 294912 | tf_op jit(solution)/shard_map/reduce_scatter | solution.py:397
  1543.2 473.0 %reduce-scatter.38.cloned.1.call-start = ((), (), s32[]{:S(2)}) async-start(), calls=%async_computation.33 | async-start | bytes 1769472 | tf_op jit(solution)/shard_map/reduce_scatter | solution.py:398
  1548.8 194.3 %copy-start.26 = (bf16[512,1024]{1,0:T(8,128)(2,1)S(1)}, bf16[512,1024]{1,0:T(8,128)(2,1)}, u32[]{:S(2)}) copy-start(bf16[512,1024]{1,0:T(8,128)(2,1)} %param.38) | copy-start | bytes 3145732
  1548.8 194.3 %copy-start.30 = (bf16[512,1024]{1,0:T(8,128)(2,1)S(1)}, bf16[512,1024]{1,0:T(8,128)(2,1)}, u32[]{:S(2)}) copy-start(bf16[512,1024]{1,0:T(8,128)(2,1)} %reduce-scatter.16.cloned.1.call-done) | copy-start | bytes 3145732
  1548.8 194.3 %copy-start.40 = (bf16[512,1024]{1,0:T(8,128)(2,1)S(1)}, bf16[512,1024]{1,0:T(8,128)(2,1)}, u32[]{:S(2)}) copy-start(bf16[512,1024]{1,0:T(8,128)(2,1)} %param.55) | copy-start | bytes 3145732
  1548.8 194.3 %copy-start.84 = (f32[1024]{0:T(1024)S(1)}, f32[1024]{0:T(1024)}, u32[]{:S(2)}) copy-start(f32[1024]{0:T(1024)} %param.49) | copy-start | bytes 12292
  1548.8 194.3 %copy-start.86 = (f32[512]{0:T(512)S(1)}, f32[512]{0:T(512)}, u32[]{:S(2)}) copy-start(f32[512]{0:T(512)} %copy-done.85) | copy-start | bytes 6148
  (159 other events, 2644.6 us)
Sparse Core Ops, SparseCore 0:
  9.6 100.1 all-gather.7
  112.3 24.2 all-gather.9
  402.5 73.9 reduce-scatter.15
  479.0 28.4 all-gather.13
  509.5 80.7 all-gather.11
  592.2 22.0 all-gather.15
  616.0 80.7 all-gather.17
  715.8 75.2 reduce-scatter.19
  797.9 81.2 all-gather.19
  1243.5 20.6 reduce-scatter.27
  1460.1 20.6 reduce-scatter.33
  1484.0 49.4 reduce-scatter.41
  1537.3 46.2 reduce-scatter.23
  1585.7 76.7 reduce-scatter.21
  1664.7 78.3 reduce-scatter.17
  1746.8 41.6 reduce-scatter.43
  1792.2 31.2 reduce-scatter.25
  1827.0 34.1 reduce-scatter.39
  1865.1 34.0 reduce-scatter.31
  1902.7 33.5 reduce-scatter.29
  1940.2 33.5 reduce-scatter.35
  1977.7 38.4 reduce-scatter.37
where the time goes:
time: 2030 us; the launch traced here: 2020 us
  waiting for transfers between devices  840 us (41%)
  matrix products  407 us (20%)
  other arithmetic  264 us (13%)
  local copies, waits for them, and re-layouts  254 us (13%)
  blocking collectives  172 us (8%)
  loops' own time  68.6 us (3%)
    another operation x29, other arithmetic  94.4 us
    all_gather x1, waiting for transfers between devices, shards(): mlp_rows = lax.all_gather(mlp_share, 'tensor', axis=0, tiled=True)  82.9 us
    all_gather x1, waiting for transfers between devices, shards(): grad_rows = lax.all_gather(cotangent, 'tensor', axis=0, tiled=True)  82.4 us
    all_gather x1, waiting for transfers between devices, shards(): lax.all_gather(middle_grad.astype(jnp.bfloat16), 'tensor', axis=0, tiled=...  78.5 us
    reduce_scatter x1, waiting for transfers between devices, shards(): lax.psum_scatter(normed_grad.astype(jnp.bfloat16), 'tensor', scatter_dime...  76.9 us
    reduce_scatter x1, waiting for transfers between devices, shards(): lax.psum_scatter(jnp.einsum('rkf,dkf->rd', rows_of(both_grad, jnp.int32(0...  75.4 us
    dot_general x16, matrix products, one_block(): jnp.einsum('qhd,khd->hqk', block_queries, seq_keys, precision=highest)  74.3 us
    reduce_scatter x1, waiting for transfers between devices, shards(): lax.psum_scatter((matmul(rows_of(mixer_heads, first_row, share_rows * lax...  72.4 us
  transfers between devices with their start and end apart: 22, of which 18 were waited for; matrix products, arithmetic and copies ran while one was open for 15% of the time, Pallas kernels for 0%

commit v1 on v0

v1 whole, which is shorter than its diff:
```python
import functools

import jax
import jax.numpy as jnp
from jax import lax
from jax.experimental import pallas as pl
from jax.experimental.pallas import tpu as pltpu
from jax.sharding import PartitionSpec as P

PH = 64
NS = 128
KC = 4
AH = 8
KVH = 2
HD = 64
LEN = 1024
CHUNK = 128
HALO = 16
GROUP = 4
GW = GROUP * PH

epsilon = 1e-05
rope_base = 100000000000.0
masked_fill = -1e30
highest = lax.Precision.HIGHEST
f32 = jnp.float32
bf16 = jnp.bfloat16
VMEM_BYTES = 52 * 1024 * 1024


def call(kernel, grid, in_specs, out_specs, out_shape, scratch=(), flops=0, moved=0):
    return pl.pallas_call(
        kernel,
        grid=grid,
        in_specs=in_specs,
        out_specs=out_specs,
        out_shape=out_shape,
        scratch_shapes=list(scratch),
        compiler_params=pltpu.CompilerParams(
            vmem_limit_bytes=VMEM_BYTES, dimension_semantics=("arbitrary",) * len(grid)
        ),
        cost_estimate=pl.CostEstimate(flops=flops, bytes_accessed=moved, transcendentals=0),
    )


def spec(block, index):
    return pl.BlockSpec(block, index)


def shape(dims, kind):
    return jax.ShapeDtypeStruct(dims, kind)


def dot(left, right, dims):
    return lax.dot_general(left, right, ((dims[:1], dims[1:]), ((), ())), preferred_element_type=f32)


NN = (1, 0)
NT = (1, 1)
TN = (0, 0)


def sigmoid(value):
    return 1.0 / (1.0 + jnp.exp(-value))


def pair_lanes(left, right, rows):
    lane = lax.broadcasted_iota(jnp.int32, (rows, 2 * PH), 1)
    return jnp.where(lane < PH, left, right)


def spread_heads(columns, first, count, rows):
    parts = [
        pair_lanes(
            columns[:, first + 2 * p : first + 2 * p + 1],
            columns[:, first + 2 * p + 1 : first + 2 * p + 2],
            rows,
        )
        for p in range(count // 2)
    ]
    return jnp.concatenate(parts, axis=1) if len(parts) > 1 else parts[0]


def conv_of(ref, taps, rows):
    total = ref[pl.ds(HALO - KC + 1, rows), :] * taps[0:1, :]
    for offset in range(1, KC):
        total = total + ref[pl.ds(HALO - KC + 1 + offset, rows), :] * taps[offset : offset + 1, :]
    return total


def causal_mask(transposed):
    row = lax.broadcasted_iota(jnp.int32, (CHUNK, CHUNK), 0)
    col = lax.broadcasted_iota(jnp.int32, (CHUNK, CHUNK), 1)
    return col >= row if transposed else row >= col


def mixer_kernel(
    val_ref, shr_ref, tapv_ref, taps_ref, cumc_ref, cumr_ref, dt_ref, skip_ref,
    y_ref, state_ref, bc_ref, aff_ref,
):
    rows = y_ref.shape[0]
    chunks = rows // CHUNK

    @pl.when(pl.program_id(0) == 0)
    def _():
        pre = conv_of(shr_ref, taps_ref[...], rows)
        bc_ref[...] = (pre * sigmoid(pre)).astype(bf16)
        for c in range(chunks):
            sl = pl.ds(c * CHUNK, CHUNK)
            aff_ref[c] = dot(bc_ref[sl, NS:], bc_ref[sl, :NS], NT)

    pre = conv_of(val_ref, tapv_ref[...], rows)
    head_in = pre * sigmoid(pre)
    mask = causal_mask(False)
    skip = skip_ref[...]
    state = jnp.zeros((NS, GW), f32)
    for c in range(chunks):
        sl = pl.ds(c * CHUNK, CHUNK)
        x = head_in[c * CHUNK : (c + 1) * CHUNK]
        cumc = cumc_ref[0, sl, :]
        cumr = cumr_ref[0, :, sl]
        dt = dt_ref[0, sl, :]
        w = x * spread_heads(dt, 0, GROUP, CHUNK)
        w_low = w.astype(bf16)
        inner = []
        for p in range(GROUP // 2):
            both = []
            for h in (2 * p, 2 * p + 1):
                gap = cumc[:, h : h + 1] - cumr[h : h + 1, :]
                decay = jnp.exp(jnp.where(mask, gap, masked_fill))
                weight = (aff_ref[c] * decay).astype(bf16)
                both.append(dot(weight, w_low[:, p * 2 * PH : (p + 1) * 2 * PH], NN))
            inner.append(pair_lanes(both[0], both[1], CHUNK))
        out = jnp.concatenate(inner, axis=1) + skip * x
        b_now = bc_ref[sl, :NS]
        c_now = bc_ref[sl, NS:]
        last = cumc[CHUNK - 1 : CHUNK, :]
        if c > 0:
            grown = spread_heads(jnp.exp(cumc), 0, GROUP, CHUNK)
            out = out + dot(c_now, state.astype(bf16), NN) * grown
        y_ref[sl, :] = out
        to_end = spread_heads(jnp.exp(last - cumc), 0, GROUP, CHUNK)
        added = dot(b_now, (w * to_end).astype(bf16), TN)
        fall = spread_heads(jnp.exp(last), 0, GROUP, 1)
        state = state * fall + added
    state_ref[...] = state


def finish_kernel(y_ref, gate_ref, bc_ref, grow_ref, state_ref, gain_ref, scan_ref, heads_ref):
    rows, width = y_ref.shape
    grown = spread_heads(grow_ref[...], 0, width // PH, rows)
    scan = y_ref[...] + dot(bc_ref[:, NS:], state_ref[...].astype(bf16), NN) * grown
    scan_ref[...] = scan
    gate = gate_ref[...]
    pre = scan * gate * sigmoid(gate)
    inv = lax.rsqrt(jnp.mean(pre * pre, axis=1, keepdims=True) + epsilon)
    heads_ref[...] = (pre * inv * gain_ref[...]).astype(bf16)


def ungate_kernel(
    ga_ref, gb_ref, scan_ref, gate_ref, bc_ref, grow_ref, gain_ref,
    dgate_ref, dscan_ref, dgain_ref, dstate_ref,
):
    rows, width = scan_ref.shape
    scan = scan_ref[...]
    gate = gate_ref[...]
    sig = sigmoid(gate)
    silu = gate * sig
    pre = scan * silu
    inv = lax.rsqrt(jnp.mean(pre * pre, axis=1, keepdims=True) + epsilon)
    normed = pre * inv
    grad = jnp.concatenate([ga_ref[...], gb_ref[...]], axis=1)
    u = grad * gain_ref[...]
    cross = jnp.mean(u * normed, axis=1, keepdims=True)
    dpre = inv * (u - normed * cross)
    dscan = dpre * silu
    dgate_ref[...] = (dpre * scan * sig * (1.0 + gate * (1.0 - sig))).astype(bf16)
    dscan_ref[...] = dscan
    grown = spread_heads(grow_ref[...], 0, width // PH, rows)
    dstate = dot(bc_ref[:, NS:], (dscan * grown).astype(bf16), TN)
    dgain = jnp.sum(grad * normed, axis=0, keepdims=True)
    first = pl.program_id(0) == 0

    @pl.when(first)
    def _():
        dgain_ref[...] = dgain
        dstate_ref[...] = dstate

    @pl.when(jnp.logical_not(first))
    def _():
        dgain_ref[...] += dgain
        dstate_ref[...] += dstate


def split_sum(value, ones_at):
    high = value.astype(bf16)
    low = (value - high.astype(f32)).astype(bf16)
    return dot(high, ones_at, NN) + dot(low, ones_at, NN)


def unconv(ref, taps, dact, pad_ref, out_ref, dtaps_ref, rows):
    pre = conv_of(ref, taps, rows)
    sig = sigmoid(pre)
    dpre = dact * sig * (1.0 + pre * (1.0 - sig))
    lead = HALO + 8
    width = dact.shape[1]
    pad_ref[pl.ds(0, lead), :] = jnp.zeros((lead, width), f32)
    pad_ref[pl.ds(lead + rows, 8), :] = jnp.zeros((8, width), f32)
    pad_ref[pl.ds(lead, rows), :] = dpre
    total = None
    dtaps = []
    for offset in range(KC):
        part = pad_ref[pl.ds(8 + KC - 1 - offset, rows + HALO), :] * taps[offset : offset + 1, :]
        total = part if total is None else total + part
        moved = ref[pl.ds(HALO - KC + 1 + offset, rows), :]
        dtaps.append(jnp.sum(dpre * moved, axis=0, keepdims=True))
    out_ref[...] = total.astype(bf16)
    dtaps_ref[...] = jnp.concatenate(dtaps, axis=0)


def unmix_kernel(
    val_ref, shr_ref, tapv_ref, taps_ref, cumc_ref, cumr_ref, dt_ref, skip_ref, bc_ref,
    dscan_ref, enter_ref, dleave_ref,
    dval_ref, dshr_ref, cols_ref, rows_ref, dlast_ref, dtapv_ref, dtaps_ref, dskip_ref,
    aff_ref, daff_ref, dbc_ref, dx_ref, states_ref, pad_ref,
):
    rows = dscan_ref.shape[0]
    chunks = rows // CHUNK
    step = pl.program_id(0)

    @pl.when(step == 0)
    def _():
        for c in range(chunks):
            sl = pl.ds(c * CHUNK, CHUNK)
            aff_ref[c] = dot(bc_ref[sl, :NS], bc_ref[sl, NS:], NT)
        daff_ref[...] = jnp.zeros(daff_ref.shape, f32)
        dbc_ref[...] = jnp.zeros(dbc_ref.shape, f32)

    pre = conv_of(val_ref, tapv_ref[...], rows)
    dx_ref[...] = pre * sigmoid(pre)
    mask = causal_mask(True)
    skip = skip_ref[...]
    lane = lax.broadcasted_iota(jnp.int32, (GW, 2 * GROUP), 0) // PH
    slot = lax.broadcasted_iota(jnp.int32, (GW, 2 * GROUP), 1)
    ones_dt = jnp.where(lane == slot, 1.0, 0.0).astype(bf16)
    ones_cum = jnp.where(lane + GROUP == slot, 1.0, 0.0).astype(bf16)
    half_lane = lax.broadcasted_iota(jnp.int32, (CHUNK, 2 * PH), 1) // PH
    slot_lane = lax.broadcasted_iota(jnp.int32, (CHUNK, 2 * GROUP), 1)

    state = enter_ref[...]
    states_ref[0] = state
    for c in range(chunks - 1):
        sl = pl.ds(c * CHUNK, CHUNK)
        cumc = cumc_ref[0, sl, :]
        last = cumc[CHUNK - 1 : CHUNK, :]
        scale = spread_heads(dt_ref[0, sl, :] * jnp.exp(last - cumc), 0, GROUP, CHUNK)
        added = dot(bc_ref[sl, :NS], (dx_ref[sl, :] * scale).astype(bf16), TN)
        state = state * spread_heads(jnp.exp(last), 0, GROUP, 1) + added
        states_ref[c + 1] = state

    dstate = dleave_ref[...]
    dskip = jnp.zeros((1, GW), f32)
    for c in reversed(range(chunks)):
        sl = pl.ds(c * CHUNK, CHUNK)
        x = dx_ref[sl, :]
        dy = dscan_ref[sl, :]
        dy_low = dy.astype(bf16)
        cumc = cumc_ref[0, sl, :]
        cumr = cumr_ref[0, :, sl]
        last = cumc[CHUNK - 1 : CHUNK, :]
        dt = spread_heads(dt_ref[0, sl, :], 0, GROUP, CHUNK)
        w = x * dt
        w_low = w.astype(bf16)
        b_now = bc_ref[sl, :NS]
        c_now = bc_ref[sl, NS:]
        affinity = aff_ref[c]
        dcum = jnp.zeros((CHUNK, 2 * GROUP), f32)
        daff = daff_ref[c]
        dw_parts = []
        for p in range(GROUP // 2):
            pair = slice(p * 2 * PH, (p + 1) * 2 * PH)
            both = []
            for h in (2 * p, 2 * p + 1):
                gap = cumr[h : h + 1, :] - cumc[:, h : h + 1]
                decay = jnp.exp(jnp.where(mask, gap, masked_fill))
                weight = affinity * decay
                w_own = jnp.where(half_lane == h - 2 * p, w[:, pair], 0.0).astype(bf16)
                dweight = dot(w_own, dy_low[:, pair], NT)
                daff = daff + dweight * decay
                moved = dweight * weight
                rows_ref[0, h : h + 1, sl] = jnp.sum(moved, axis=0, keepdims=True)
                dcum = dcum - jnp.where(
                    slot_lane == GROUP + h, jnp.sum(moved, axis=1, keepdims=True), 0.0
                )
                both.append(dot(weight.astype(bf16), dy_low[:, pair], NN))
            dw_parts.append(pair_lanes(both[0], both[1], CHUNK))
        daff_ref[c] = daff
        state = states_ref[c]
        state_low = state.astype(bf16)
        dstate_low = dstate.astype(bf16)
        grown = spread_heads(jnp.exp(cumc), 0, GROUP, CHUNK)
        to_end = spread_heads(jnp.exp(last - cumc), 0, GROUP, CHUNK)
        fall = spread_heads(jnp.exp(last), 0, GROUP, 1)
        dy_grown = (dy * grown).astype(bf16)
        carried = dot(c_now, state_low, NN) * grown
        from_end = dot(b_now, dstate_low, NN) * to_end
        dbc_ref[sl, NS:] += dot(dy_grown, state_low, NT)
        dbc_ref[sl, :NS] += dot((w * to_end).astype(bf16), dstate_low, NT)
        dw = jnp.concatenate(dw_parts, axis=1) + from_end
        ended = w * from_end
        cols_ref[0, sl, :] = (
            dcum + split_sum(dw * x, ones_dt) + split_sum(dy * carried - ended, ones_cum)
        )
        dlast_ref[c : c + 1, :] = jnp.sum(ended, axis=0, keepdims=True) + fall * jnp.sum(
            state * dstate, axis=0, keepdims=True
        )
        dstate = fall * dstate + dot(c_now, dy_grown, TN)
        dskip = dskip + jnp.sum(dy * x, axis=0, keepdims=True)
        dx_ref[sl, :] = dw * dt + skip * dy
    dskip_ref[...] = dskip
    unconv(val_ref, tapv_ref[...], dx_ref[...], pad_ref, dval_ref, dtapv_ref, rows)

    @pl.when(step == pl.num_programs(0) - 1)
    def _():
        for c in range(chunks):
            sl = pl.ds(c * CHUNK, CHUNK)
            daff_low = daff_ref[c].astype(bf16)
            dbc_ref[sl, :NS] += dot(daff_low, bc_ref[sl, NS:], NN)
            dbc_ref[sl, NS:] += dot(daff_low, bc_ref[sl, :NS], TN)
        unconv(shr_ref, taps_ref[...], dbc_ref[...], pad_ref, dshr_ref, dtaps_ref, rows)


def swap_halves(value):
    half = HD // 2
    width = value.shape[1]
    lane = lax.broadcasted_iota(jnp.int32, value.shape, 1) % HD
    return jnp.where(
        lane < half, pltpu.roll(value, width - half, 1), pltpu.roll(value, half, 1)
    )


def rotate_kernel(value_ref, cos_ref, sin_ref, out_ref):
    value = value_ref[...]
    out_ref[...] = (value * cos_ref[...] + swap_halves(value) * sin_ref[...]).astype(bf16)


def unrotate_kernel(own_ref, late_ref, cos_ref, sin_ref, out_ref):
    value = own_ref[...] + late_ref[...].astype(f32)
    out_ref[...] = (value * cos_ref[...] + swap_halves(value * sin_ref[...])).astype(bf16)


def head_queries(query, which):
    lane = lax.broadcasted_iota(jnp.int32, query.shape, 1)
    moved = pltpu.roll(query, HD, 1) if which else query
    return jnp.where(lane < HD, moved, 0.0)


def score_weights(query, before, own, allowed):
    early = jnp.where(allowed, dot(query, before, NT), masked_fill)
    late = dot(query, own, NT)
    row = lax.broadcasted_iota(jnp.int32, late.shape, 0)
    col = lax.broadcasted_iota(jnp.int32, late.shape, 1)
    late = jnp.where(row >= col, late, masked_fill)
    top = jnp.maximum(
        jnp.max(early, axis=1, keepdims=True), jnp.max(late, axis=1, keepdims=True)
    )
    early = jnp.exp(early - top)
    late = jnp.exp(late - top)
    total = jnp.sum(early, axis=1, keepdims=True) + jnp.sum(late, axis=1, keepdims=True)
    return early, late, 1.0 / total


def rotated_queries(q_ref, cos_ref, sin_ref):
    query = q_ref[...]
    return (query * cos_ref[...] + swap_halves(query) * sin_ref[...]) * (HD**-0.5)


def attend_kernel(part_ref, q_ref, cos_ref, sin_ref, before_ref, own_ref, out_ref):
    allowed = part_ref[0] > 0
    query = rotated_queries(q_ref, cos_ref, sin_ref)
    before = before_ref[...]
    own = own_ref[...]
    results = []
    for which in range(2):
        q_low = head_queries(query, which).astype(bf16)
        early, late, scale = score_weights(q_low, before, own, allowed)
        result = dot(early.astype(bf16), before, NN) + dot(late.astype(bf16), own, NN)
        results.append(result * scale)
    out_ref[...] = pair_lanes(pltpu.roll(results[0], HD, 1), results[1], query.shape[0]).astype(
        bf16
    )


def unattend_kernel(
    part_ref, q_ref, cos_ref, sin_ref, before_ref, own_ref, dout_ref,
    dq_ref, dbefore_ref, down_ref,
):
    allowed = part_ref[0] > 0
    query = rotated_queries(q_ref, cos_ref, sin_ref)
    before = before_ref[...]
    own = own_ref[...]
    dout = dout_ref[...]
    lane = lax.broadcasted_iota(jnp.int32, dout.shape, 1)
    dqs = []
    dbefore = None
    down = None
    for which in range(2):
        q_low = head_queries(query, which).astype(bf16)
        early, late, scale = score_weights(q_low, before, own, allowed)
        early = early * scale
        late = late * scale
        dout_own = dout if which else pltpu.roll(dout, HD, 1)
        dout_low = jnp.where(lane >= HD, dout_own, 0.0).astype(bf16)
        dearly = dot(dout_low, before, NT)
        dlate = dot(dout_low, own, NT)
        cross = jnp.sum(early * dearly, axis=1, keepdims=True) + jnp.sum(
            late * dlate, axis=1, keepdims=True
        )
        dearly = (early * (dearly - cross)).astype(bf16)
        dlate = (late * (dlate - cross)).astype(bf16)
        dqs.append(dot(dearly, before, NN) + dot(dlate, own, NN))
        part_before = dot(dearly, q_low, TN) + dot(early.astype(bf16), dout_low, TN)
        part_own = dot(dlate, q_low, TN) + dot(late.astype(bf16), dout_low, TN)
        dbefore = part_before if dbefore is None else dbefore + part_before
        down = part_own if down is None else down + part_own
    dq = pair_lanes(dqs[0], pltpu.roll(dqs[1], HD, 1), dout.shape[0]) * (HD**-0.5)
    dq_ref[...] = (dq * cos_ref[...] + swap_halves(dq * sin_ref[...])).astype(bf16)
    first = lax.rem(pl.program_id(0), AH // KVH // 2) == 0

    @pl.when(first)
    def _():
        dbefore_ref[...] = dbefore
        down_ref[...] = down

    @pl.when(jnp.logical_not(first))
    def _():
        dbefore_ref[...] += dbefore
        down_ref[...] += down


def matmul(left, right, dims=NN):
    return dot(left, right, dims)


def partner(value, bit):
    count = lax.axis_size("dp")
    return lax.ppermute(value, "dp", [(i, i ^ (1 << bit)) for i in range(count)])


def bit_axes():
    bits = lax.axis_size("dp").bit_length() - 1
    return [0] + list(range(bits - 1, 0, -1))


def stages(flip):
    bits = lax.axis_size("dp").bit_length() - 1
    high = list(range(1, bits))
    return (high[::-1] if flip else high) + [0]


def spread(piece, flip):
    axes = bit_axes()
    held = piece.reshape((1,) * len(axes) + piece.shape)
    for bit in stages(flip):
        held = jnp.concatenate([held, partner(held, bit)], axis=axes.index(bit))
    return held.reshape((-1,) + piece.shape[1:])


def collect(keep, send, flip):
    axes = bit_axes()[1:]
    got = partner(send.astype(bf16), 0)
    held = (keep + got.astype(f32)).astype(bf16)
    held = held.reshape((2,) * len(axes) + (-1,) + held.shape[1:])
    for bit in stages(flip)[:-1][::-1]:
        axis = axes.index(bit)
        mine = lax.slice_in_dim(held, 0, 1, axis=axis)
        theirs = lax.slice_in_dim(held, 1, 2, axis=axis)
        held = (mine.astype(f32) + partner(theirs, bit).astype(f32)).astype(bf16)
    return held.reshape(held.shape[-2:])


def block_sources():
    count = lax.axis_size("dp")
    half = count // 2
    me = lax.axis_index("dp")
    return [me ^ (((p % half) << 1) | (p // half)) for p in range(count)]


def block_places():
    count = lax.axis_size("dp")
    me = lax.axis_index("dp")
    return [((me ^ b) >> 1) | (((me ^ b) & 1) * (count // 2)) for b in range(count)]


def take_blocks(value, sources):
    width = value.shape[-1] // len(sources)
    axis = value.ndim - 1
    return jnp.concatenate(
        [lax.dynamic_slice_in_dim(value, s * width, width, axis) for s in sources], axis=axis
    )


def permute_features(value):
    return take_blocks(value, block_sources())


def restore_features(value):
    return take_blocks(value, block_places())


def norm_of(rows):
    inv = lax.rsqrt(jnp.mean(rows * rows, axis=-1, keepdims=True) + epsilon)
    return rows * inv, inv


def norm_back(grad, gain, normed, inv):
    scaled = grad * gain
    return inv * (scaled - normed * jnp.mean(scaled * normed, axis=-1, keepdims=True))


def over_tensor(piece):
    return lax.all_gather(piece, "tensor", axis=0)


def columns_of(gathered, start, stop):
    part = gathered[:, :, start:stop]
    count, rows, width = part.shape
    return part.transpose(1, 0, 2).reshape(rows, count * width)


def split_columns(value, count):
    rows, width = value.shape
    return value.reshape(rows, count, width // count).transpose(1, 0, 2)


def shards(
    residual,
    mixer_in,
    step_in,
    shared_in,
    query_in,
    keyval_in,
    mixer_proj,
    attn_proj,
    gate_up,
    down_proj,
    norm_gain,
    mlp_gain,
    conv_filter,
    decay_log,
    skip_gain,
    step_bias,
    gated_gain,
    cotangent,
):
    tensor_count = lax.axis_size("tensor")
    rows, model = residual.shape
    depth = mixer_in.shape[0]
    ssm = conv_filter.shape[1] - 2 * NS
    heads = ssm // PH
    groups = heads // GROUP
    chunks = rows // CHUNK
    span = LEN // rows
    part = lax.axis_index("tensor") % span
    onward = [(i, i + 1) for i in range(tensor_count) if i % span != span - 1]
    backward = [(j, i) for i, j in onward]
    gate_w = mixer_in.shape[2]
    hidden_w = gate_up.shape[2]
    query_w = query_in.shape[1]
    shared_w = shared_in.shape[1]
    keyval_w = keyval_in.shape[1]
    step_w = step_in.shape[1]
    attn_w = AH * HD
    out_w = ssm + attn_w
    ff = hidden_w * tensor_count

    in_piece = over_tensor(
        jnp.concatenate(
            [mixer_in[:, 0], query_in, mixer_in[:, 1], shared_in, keyval_in, step_in], axis=1
        )
    )
    cuts = [0, gate_w, query_w, gate_w, shared_w, keyval_w, step_w]
    ends = [sum(cuts[: i + 1]) for i in range(len(cuts))]
    in_parts = [columns_of(in_piece, ends[i], ends[i + 1]) for i in range(6)]
    step_total = step_w * tensor_count
    step_pad = -step_total % 128
    in_a = spread(
        jnp.concatenate([in_parts[0], in_parts[1], jnp.pad(in_parts[5], ((0, 0), (0, step_pad)))], 1),
        False,
    )
    in_b = spread(jnp.concatenate(in_parts[2:5], axis=1), True)
    out_piece = over_tensor(jnp.concatenate([mixer_proj, attn_proj], axis=0).T)
    out_cut = mixer_proj.shape[0]
    out_all = jnp.concatenate(
        [columns_of(out_piece, 0, out_cut), columns_of(out_piece, out_cut, out_piece.shape[2])], 1
    )
    out_a = spread(out_all[:, : out_w // 2], False)
    out_b = spread(out_all[:, out_w // 2 :], True)
    ff_piece = over_tensor(gate_up.reshape(depth, 2 * hidden_w))
    gate_full = spread(columns_of(ff_piece, 0, hidden_w), False)
    up_full = spread(columns_of(ff_piece, hidden_w, 2 * hidden_w), True)
    down_all = columns_of(over_tensor(down_proj.T), 0, hidden_w)
    down_a = spread(down_all[:, : ff // 2], False)
    down_b = spread(down_all[:, ff // 2 :], True)

    before_rows = lax.ppermute(residual[rows - HALO :], "tensor", onward)
    ext_low = permute_features(jnp.concatenate([before_rows, residual], axis=0))
    cot = permute_features(cotangent)
    gain_first = permute_features(norm_gain)
    gain_second = permute_features(mlp_gain)
    ext_normed, ext_inv = norm_of(ext_low.astype(f32))
    ext_in = (ext_normed * gain_first).astype(bf16)
    normed_first = ext_normed[HALO:]
    inv_first = ext_inv[HALO:]
    normed_in = ext_in[HALO:]
    group_rows = ext_low[HALO:].astype(f32)
    proj_a = matmul(normed_in, in_a)
    proj_b = matmul(ext_in, in_b)

    step_proj = proj_a[:, ssm + attn_w : ssm + attn_w + heads]
    step_size = jax.nn.softplus(step_proj + step_bias)
    rate = jnp.exp(decay_log)
    log_decay = -rate * step_size
    lower = jnp.tril(jnp.ones((CHUNK, CHUNK), f32))
    cum = jnp.einsum(
        "ij,cjh->cih", lower, log_decay.reshape(chunks, CHUNK, heads), precision=highest
    )
    ends_of = cum[:, -1, :]
    prefix = jnp.concatenate([jnp.zeros((1, heads), f32), jnp.cumsum(ends_of, axis=0)[:-1]], 0)
    grow = jnp.exp(cum + prefix[:, None, :]).reshape(rows, heads)
    cum = cum.reshape(rows, heads)
    cum_cols = cum.reshape(rows, groups, GROUP).transpose(1, 0, 2)
    cum_rows = cum.T.reshape(groups, GROUP, rows)
    dt_cols = step_size.reshape(rows, groups, GROUP).transpose(1, 0, 2)
    skip_lanes = jnp.repeat(skip_gain, PH)[None, :]

    ext = rows + HALO
    val_spec = spec((ext, GW), lambda g: (0, g))
    shr_spec = spec((ext, 2 * NS), lambda g: (0, ssm // (2 * NS)))
    tapv_spec = spec((KC, GW), lambda g: (0, g))
    taps_spec = spec((KC, 2 * NS), lambda g: (0, ssm // (2 * NS)))
    col_spec = spec((1, rows, GROUP), lambda g: (g, 0, 0))
    row_spec = spec((1, GROUP, rows), lambda g: (g, 0, 0))
    lane_spec = spec((1, GW), lambda g: (0, g))
    bc_spec = spec((rows, 2 * NS), lambda g: (0, 0))
    grp_spec = spec((rows, GW), lambda g: (0, g))
    state_spec = spec((NS, GW), lambda g: (0, g))
    y_local, state_local, bc_act = call(
        mixer_kernel,
        (groups,),
        [val_spec, shr_spec, tapv_spec, taps_spec, col_spec, row_spec, col_spec, lane_spec],
        [grp_spec, state_spec, bc_spec],
        [shape((rows, ssm), f32), shape((NS, ssm), f32), shape((rows, 2 * NS), bf16)],
        [pltpu.VMEM((chunks, CHUNK, CHUNK), f32)],
        flops=2 * rows * ssm * 512,
        moved=rows * ssm * 8,
    )(proj_b, proj_b, conv_filter, conv_filter, cum_cols, cum_rows, dt_cols, skip_lanes)
    entering = lax.ppermute(state_local, "tensor", onward)

    half = HD // 2
    frequency = rope_base ** (-2.0 * jnp.arange(half, dtype=f32) / HD)
    place = (part * rows + jnp.arange(rows, dtype=jnp.int32)).astype(f32)
    angles = place[:, None] * frequency[None, :]
    cosine = jnp.cos(angles)
    sine = jnp.sin(angles)
    cos_q = jnp.concatenate([cosine] * 4, axis=1)
    sin_q = jnp.concatenate([-sine, sine] * 2, axis=1)
    ones = jnp.ones((rows, HD), f32)
    cos_kv = jnp.concatenate([cosine, cosine, ones] * KVH, axis=1)
    sin_kv = jnp.concatenate([-sine, sine, 0.0 * ones] * KVH, axis=1)
    kv_w = 2 * KVH * HD
    whole = lambda width: spec((rows, width), lambda i: (0, 0))
    own_kv = call(
        rotate_kernel,
        (1,),
        [whole(kv_w)] * 3,
        whole(kv_w),
        shape((rows, kv_w), bf16),
        moved=rows * kv_w * 12,
    )(proj_b[HALO:, ssm + 2 * NS :], cos_kv, sin_kv)
    before_kv = lax.ppermute(own_kv, "tensor", onward)
    part_arg = part.astype(jnp.int32).reshape(1)
    pairs = AH // 2
    per_kv = AH // KVH // 2
    smem = pl.BlockSpec(memory_space=pltpu.SMEM)
    q_spec = spec((rows, 2 * HD), lambda i: (0, ssm // (2 * HD) + i))
    table_spec = spec((rows, 2 * HD), lambda i: (0, 0))
    kv_spec = spec((rows, 2 * HD), lambda i: (0, i // per_kv))
    pair_spec = spec((rows, 2 * HD), lambda i: (0, i))
    attn_heads = call(
        attend_kernel,
        (pairs,),
        [smem, q_spec, table_spec, table_spec, kv_spec, kv_spec],
        pair_spec,
        shape((rows, attn_w), bf16),
        flops=2 * AH * rows * LEN * 256,
        moved=rows * attn_w * 8,
    )(part_arg, proj_a, cos_q, sin_q, before_kv, own_kv)

    block_rows = CHUNK
    wide = spec((block_rows, ssm), lambda i: (i, 0))
    bc_block = spec((block_rows, 2 * NS), lambda i: (i, 0))
    grow_block = spec((block_rows, heads), lambda i: (i, 0))
    state_whole = spec((NS, ssm), lambda i: (0, 0))
    gain_whole = spec((1, ssm), lambda i: (0, 0))
    gated_row = gated_gain[None, :]
    scanned, mixer_heads = call(
        finish_kernel,
        (rows // block_rows,),
        [wide, wide, bc_block, grow_block, state_whole, gain_whole],
        [wide, wide],
        [shape((rows, ssm), f32), shape((rows, ssm), bf16)],
        flops=2 * rows * ssm * NS,
        moved=rows * ssm * 14,
    )(y_local, proj_a, bc_act, grow, entering, gated_row)

    out_half = out_w // 2
    heads_a = mixer_heads[:, :out_half]
    heads_b = jnp.concatenate([mixer_heads[:, out_half:], attn_heads], axis=1)
    middle = group_rows + (matmul(heads_a, out_a, NT) + matmul(heads_b, out_b, NT))
    second_normed, inv_second = norm_of(middle)
    mlp_rows = (second_normed * gain_second).astype(bf16)
    gate_val = matmul(mlp_rows, gate_full)
    up_val = matmul(mlp_rows, up_full)
    sig_gate = jax.nn.sigmoid(gate_val)
    silu_gate = gate_val * sig_gate
    hidden = (silu_gate * up_val).astype(bf16)
    ff_half = ff // 2
    output = middle + (
        matmul(hidden[:, :ff_half], down_a, NT) + matmul(hidden[:, ff_half:], down_b, NT)
    )

    near = model // 2

    def weight_grad(left, right, flip):
        keep = matmul(left[:, :near], right, TN)
        send = matmul(left[:, near:], right, TN)
        return collect(keep, send, flip)

    down_sum_a = weight_grad(cot, hidden[:, :ff_half], False)
    down_sum_b = weight_grad(cot, hidden[:, ff_half:], True)
    hidden_grad = jnp.concatenate([matmul(cot, down_a), matmul(cot, down_b)], axis=1)
    gate_grad = (hidden_grad * up_val * sig_gate * (1.0 + gate_val * (1.0 - sig_gate))).astype(bf16)
    up_grad = (hidden_grad * silu_gate).astype(bf16)
    gate_sum = weight_grad(mlp_rows, gate_grad, False)
    up_sum = weight_grad(mlp_rows, up_grad, True)
    mlp_in_grad = matmul(gate_grad, gate_full, NT) + matmul(up_grad, up_full, NT)
    mlp_gain_part = jnp.sum(mlp_in_grad * second_normed, axis=0)
    middle_grad = cot.astype(f32) + norm_back(mlp_in_grad, gain_second, second_normed, inv_second)

    branch_grad = middle_grad.astype(bf16)
    heads_grad_a = matmul(branch_grad, out_a)
    heads_grad_b = matmul(branch_grad, out_b)
    out_sum_a = weight_grad(branch_grad, heads_a, False)
    out_sum_b = weight_grad(branch_grad, heads_b, True)
    gate_grad_mix, dscan, gated_gain_part, dstate_local = call(
        ungate_kernel,
        (rows // block_rows,),
        [
            spec((block_rows, out_half), lambda i: (i, 0)),
            spec((block_rows, ssm - out_half), lambda i: (i, 0)),
            wide, wide, bc_block, grow_block, gain_whole,
        ],
        [wide, wide, gain_whole, state_whole],
        [
            shape((rows, ssm), bf16),
            shape((rows, ssm), f32),
            shape((1, ssm), f32),
            shape((NS, ssm), f32),
        ],
        flops=2 * rows * ssm * NS,
        moved=rows * ssm * 18,
    )(heads_grad_a, heads_grad_b, scanned, proj_a, bc_act, grow, gated_row)
    leaving_grad = lax.ppermute(dstate_local, "tensor", backward)

    dout_spec = spec((rows, 2 * HD), lambda i: (0, (ssm - out_half) // (2 * HD) + i))
    query_low, before_grad, own_grad = call(
        unattend_kernel,
        (pairs,),
        [smem, q_spec, table_spec, table_spec, kv_spec, kv_spec, dout_spec],
        [pair_spec, kv_spec, kv_spec],
        [shape((rows, attn_w), bf16), shape((rows, kv_w), f32), shape((rows, kv_w), f32)],
        flops=2 * AH * rows * LEN * 640,
        moved=rows * attn_w * 16,
    )(part_arg, proj_a, cos_q, sin_q, before_kv, own_kv, heads_grad_b)
    late_grad = lax.ppermute(before_grad.astype(bf16), "tensor", backward)

    dval, dshr, dcols, drows, dlast, dtapv, dtaps, dskip = call(
        unmix_kernel,
        (groups,),
        [
            val_spec, shr_spec, tapv_spec, taps_spec, col_spec, row_spec, col_spec, lane_spec,
            bc_spec, grp_spec, state_spec, state_spec,
        ],
        [
            val_spec,
            spec((ext, 2 * NS), lambda g: (0, 0)),
            spec((1, rows, 2 * GROUP), lambda g: (g, 0, 0)),
            row_spec,
            spec((chunks, GW), lambda g: (0, g)),
            tapv_spec,
            spec((KC, 2 * NS), lambda g: (0, 0)),
            lane_spec,
        ],
        [
            shape((ext, ssm), bf16),
            shape((ext, 2 * NS), bf16),
            shape((groups, rows, 2 * GROUP), f32),
            shape((groups, GROUP, rows), f32),
            shape((chunks, ssm), f32),
            shape((KC, ssm), f32),
            shape((KC, 2 * NS), f32),
            shape((1, ssm), f32),
        ],
        [
            pltpu.VMEM((chunks, CHUNK, CHUNK), f32),
            pltpu.VMEM((chunks, CHUNK, CHUNK), f32),
            pltpu.VMEM((rows, 2 * NS), f32),
            pltpu.VMEM((rows, GW), f32),
            pltpu.VMEM((chunks, NS, GW), f32),
            pltpu.VMEM((rows + HALO + 16, GW), f32),
        ],
        flops=2 * rows * ssm * 1280,
        moved=rows * ssm * 12,
    )(
        proj_b, proj_b, conv_filter, conv_filter, cum_cols, cum_rows, dt_cols, skip_lanes,
        bc_act, dscan, entering, leaving_grad,
    )
    kv_low = call(
        unrotate_kernel,
        (1,),
        [whole(kv_w)] * 4,
        whole(kv_w),
        shape((rows, kv_w), bf16),
        moved=rows * kv_w * 16,
    )(own_grad, late_grad, cos_kv, sin_kv)

    by_head = dcols.transpose(1, 0, 2)
    dstep_direct = by_head[:, :, :GROUP].reshape(rows, heads)
    dcum = by_head[:, :, GROUP:].reshape(rows, heads) + drows.reshape(heads, rows).T
    dcum = dcum.reshape(chunks, CHUNK, heads)
    at_end = dlast.reshape(chunks, heads, PH).sum(axis=-1)
    dlog = jnp.einsum("ij,cih->cjh", lower, dcum, precision=highest) + at_end[:, None, :]
    dlog = dlog.reshape(rows, heads)
    decay_part = jnp.sum(dlog * log_decay, axis=0)
    dstep = (dstep_direct - rate * dlog) * jax.nn.sigmoid(step_proj + step_bias)
    bias_part = jnp.sum(dstep, axis=0)
    skip_part = dskip.reshape(heads, PH).sum(axis=-1)

    step_low = jnp.pad(dstep.astype(bf16), ((0, 0), (0, step_pad)))
    low_a = jnp.concatenate([gate_grad_mix, query_low, step_low], axis=1)
    low_b = jnp.concatenate([dval, dshr, jnp.pad(kv_low, ((HALO, 0), (0, 0)))], axis=1)
    in_sum_a = weight_grad(normed_in, low_a, False)
    in_sum_b = weight_grad(ext_in, low_b, True)
    grad_b = matmul(low_b, in_b, NT)
    late_rows = lax.ppermute(grad_b[:HALO], "tensor", backward)
    first_grad = grad_b[HALO:] + matmul(low_a, in_a, NT)
    first_grad = jnp.concatenate([first_grad[: rows - HALO], first_grad[rows - HALO :] + late_rows], 0)
    norm_gain_part = jnp.sum(first_grad * normed_first, axis=0)
    residual_grad = middle_grad + norm_back(first_grad, gain_first, normed_first, inv_first)

    def sum_tensor(parts):
        joined = jnp.concatenate([split_columns(p, tensor_count) for p in parts], axis=2)
        total = lax.psum_scatter(joined, "tensor", scatter_dimension=0, tiled=False)
        total = total.astype(f32)
        ends = [0]
        for p in parts:
            ends.append(ends[-1] + p.shape[1] // tensor_count)
        return [total[:, ends[i] : ends[i + 1]] for i in range(len(parts))]

    down_sum = jnp.concatenate([down_sum_a, down_sum_b], axis=1)
    (down_t,) = sum_tensor([down_sum])
    gate_up_sum = jnp.stack(sum_tensor([gate_sum, up_sum]), axis=1)
    mixer_t, attn_t = sum_tensor(
        [
            jnp.concatenate([out_sum_a, out_sum_b[:, : ssm - out_half]], axis=1),
            out_sum_b[:, ssm - out_half :],
        ]
    )
    in_sums = sum_tensor(
        [
            in_sum_a[:, :ssm],
            in_sum_b[:, :ssm],
            in_sum_a[:, ssm : ssm + attn_w],
            in_sum_b[:, ssm : ssm + 2 * NS],
            in_sum_b[:, ssm + 2 * NS :],
            in_sum_a[:, ssm + attn_w : ssm + attn_w + heads],
        ]
    )

    small = [
        restore_features(norm_gain_part),
        restore_features(mlp_gain_part),
        jnp.concatenate([dtapv, dtaps], axis=1).reshape(-1),
        decay_part,
        skip_part,
        bias_part,
        gated_gain_part.reshape(-1),
    ]
    sizes = [item.shape[0] for item in small]
    total = lax.psum(jnp.concatenate(small), ("dp", "tensor"))
    marks = [sum(sizes[:i]) for i in range(len(sizes) + 1)]
    sums = [total[marks[i] : marks[i + 1]] for i in range(len(sizes))]
    return (
        restore_features(output),
        restore_features(residual_grad),
        jnp.stack(in_sums[:2], axis=1),
        in_sums[5],
        in_sums[3],
        in_sums[2],
        in_sums[4],
        mixer_t.T,
        attn_t.T,
        gate_up_sum,
        down_t.T,
        sums[0],
        sums[1],
        sums[2].reshape(conv_filter.shape),
        sums[3],
        sums[4],
        sums[5],
        sums[6],
    )


def solution(mesh):
    rows_spec = P(("dp", "tensor"), None)
    into = P("dp", "tensor")
    out_of = P("tensor", "dp")
    double = P("dp", None, "tensor")
    weights = (double, into, into, into, into, out_of, out_of, double, out_of)
    return jax.shard_map(
        shards,
        mesh=mesh,
        in_specs=(rows_spec,) + weights + (P(),) * 7 + (rows_spec,),
        out_specs=(rows_spec, rows_spec) + weights + (P(),) * 7,
        check_vma=False,
    )
```

time: 2030 us -> 748 us (0.37)
  waiting for transfers between devices: 840 us -> 161 us
  matrix products: 407 us -> 102 us
  other arithmetic: 264 us -> 88.2 us
  local copies, waits for them, and re-layouts: 254 us -> 146 us
  Pallas kernels: 0 us -> 98.1 us
  blocking collectives: 172 us -> 77.8 us
  loops' own time: 68.6 us -> 0 us
  starting transfers between devices: 1.96 us -> 53 us
    reduce_scatter x15 -> x3, waiting for transfers between devices: 555 us -> 0.01 us  [sum_tensor(): total = lax.psum_scatter(joined, 'tensor', scatter_dimension=0, tiled=False)]
    dot_general x85 -> x34, matrix products: 407 us -> 102 us  [the longest x32 101 us: dot(): lax.dot_general(left, right, ((dims[:1], dims[1:]), ((), ())), preferred_...]
    all_gather x7 -> x2, waiting for transfers between devices: 282 us -> 0.01 us  [over_tensor(): return lax.all_gather(piece, 'tensor', axis=0)]
    ppermute x0 -> x54, waiting for transfers between devices: none -> 141 us  [the longest x48 128 us: partner(): return lax.ppermute(value, 'dp', [(i, i ^ 1 << bit) for i in range(count)])]
    pallas_call x0 -> x8, Pallas kernels: none -> 98.1 us  [the longest x1 38.8 us: shards(): call(unmix_kernel, (groups,), [val_spec, shr_spec, tapv_spec, taps_spec,...]
    another operation x29 -> x3, other arithmetic: 94.4 us -> 0.1 us  [the longest x1 0.04 us: shards(): jnp.cumsum(ends_of, axis=0)[:-1]]
    another operation x15 -> x0, loops' own time: 68.6 us -> none  [the longest x2 30 us: mamba_inner(): lax.map(jax.checkpoint(state_scan), (head_in, step_size, log_decay, matri...]
    all_gather x8 -> x2, blocking collectives: 105 us -> 37.8 us  [over_tensor(): return lax.all_gather(piece, 'tensor', axis=0)]
  transfers between devices with their start and end apart: 22 -> 60, of which waited for: 18 -> 24; matrix products, arithmetic and copies ran while one was open for 15% -> 37% of each run, Pallas kernels for 0% -> 10%
where the time goes in v1:
time: 748 us; the launch traced here: 743 us
  waiting for transfers between devices  161 us (22%)
  local copies, waits for them, and re-layouts  146 us (20%)
  matrix products  102 us (14%)
  Pallas kernels  98.1 us (13%)
  other arithmetic  88.2 us (12%)
  blocking collectives  77.8 us (10%)
  starting transfers between devices  53 us (7%)
  between operations  16.8 us (2%)
    ppermute x48, waiting for transfers between devices, partner(): return lax.ppermute(value, 'dp', [(i, i ^ 1 << bit) for i in range(count)])  128 us
    dot_general x32, matrix products, dot(): lax.dot_general(left, right, ((dims[:1], dims[1:]), ((), ())), preferred_...  101 us
    concatenate x24, other arithmetic, spread(): held = jnp.concatenate([held, partner(held, bit)], axis=axes.index(bit))  54.1 us
    unnamed x310, local copies, waits for them, and re-layouts  50.5 us
    concatenate x8, local copies, waits for them, and re-layouts, spread(): held = jnp.concatenate([held, partner(held, bit)], axis=axes.index(bit))  42 us
    psum x1, blocking collectives, shards(): total = lax.psum(jnp.concatenate(small), ('dp', 'tensor'))  40 us
    ppermute x48, starting transfers between devices, partner(): return lax.ppermute(value, 'dp', [(i, i ^ 1 << bit) for i in range(count)])  39.4 us
    pallas_call x1, Pallas kernels, shards(): call(unmix_kernel, (groups,), [val_spec, shr_spec, tapv_spec, taps_spec,...  38.8 us
  transfers between devices with their start and end apart: 60, of which 24 were waited for; matrix products, arithmetic and copies ran while one was open for 37% of the time, Pallas kernels for 10%

profile of v1, /device:TPU:0, one launch (start us, length us, event | category | flops | bytes accessed | tf_op | source)
XLA Modules:
  0.0 742.6 jit_solution(17926286990779603066)
XLA Ops:
  8.0 4.9 collective-permute-start
  15.9 19.3 %all-gather.2 = bf16[512,512]{1,0:T(8,128)(2,1)S(1)} all-gather(bf16[128,512]{1,0:T(8,128)(2,1)S(1)} %bitcast.304), channel_id=4, replica_groups=mesh['dp'=8,'tensor'=4] {'tensor'}, dimensions={0}, use_global_device_ids=true | all-gather | bytes 655360 | tf_op jit(solution)/shard_map/all_gather | solution.py:522
  39.0 18.5 %all-gather.1 = bf16[512,512]{1,0:T(8,128)(2,1)S(1)} all-gather(bf16[128,512]{1,0:T(8,128)(2,1)S(1)} %maximum_bitcast_fusion.2), channel_id=3, replica_groups=mesh['dp'=8,'tensor'=4] {'tensor'}, dimensions={0}, use_global_device_ids=true | all-gather | bytes 655360 | tf_op jit(solution)/shard_map/all_gather | solution.py:522
  129.5 9.9 %collective-permute-done.1 = bf16[1,1,1,128,2048]{3,4,2,1,0:T(8,128)(2,1)S(1)} collective-permute-done((bf16[1,1,1,128,2048]{3,4,2,1,0:T(8,128)(2,1)}, bf16[1,1,1,128,2048]{3,4,2,1,0:T(8,128)(2,1)S(1)}, u32[]{:S(2)}, u32[]{:S(2)}) %collective-permute-start.1) | collective-permute-done | bytes 524320 | tf_op jit(solution)/shard_map/ppermute | solution.py:447
  154.4 11.1 %collective-permute-done.19 = bf16[1,2,1,128,2048]{3,4,2,1,0:T(8,128)(2,1)S(1)} collective-permute-done((bf16[1,2,1,128,2048]{3,4,2,1,0:T(8,128)(2,1)S(1)}, bf16[1,2,1,128,2048]{3,4,2,1,0:T(8,128)(2,1)S(1)}, u32[]{:S(2)}, u32[]{:S(2)}) %collective-permute-start.19) | collective-permute-done | bytes 1048608 | tf_op jit(solution)/shard_map/ppermute | solution.py:447
  168.4 19.6 %collective-permute-done.2 = bf16[1,2,1,128,2048]{3,4,2,1,0:T(8,128)(2,1)S(1)} collective-permute-done((bf16[1,2,1,128,2048]{3,4,2,1,0:T(8,128)(2,1)S(1)}, bf16[1,2,1,128,2048]{3,4,2,1,0:T(8,128)(2,1)S(1)}, u32[]{:S(2)}, u32[]{:S(2)}) %collective-permute-start.2) | collective-permute-done | bytes 1048608 | tf_op jit(solution)/shard_map/ppermute | solution.py:447
  220.5 16.2 %collective-permute-done.16 = bf16[1,1,2,128,2048]{3,4,2,1,0:T(8,128)(2,1)S(1)} collective-permute-done((bf16[1,1,2,128,2048]{3,4,2,1,0:T(8,128)(2,1)S(1)}, bf16[1,1,2,128,2048]{3,4,2,1,0:T(8,128)(2,1)S(1)}, u32[]{:S(2)}, u32[]{:S(2)}) %collective-permute-start.16) | collective-permute-done | bytes 1048608 | tf_op jit(solution)/shard_map/ppermute | solution.py:447
  243.1 6.3 copy.241
  253.0 6.3 copy.219
  259.3 7.1 fusion.116.val_ref.shr_ref
  270.1 6.7 copy.223
  276.7 4.9 fusion.7.gate_ref.q_ref
  287.9 13.1 %shard_map.313 = (f32[512,1536]{1,0:T(8,128)}, f32[128,1536]{1,0:T(8,128)}, bf16[512,256]{1,0:T(8,128)(2,1)S(1)}) custom-call(f32[528,2048]{1,0:T(8,128)} %fusion.116.val_ref.shr_ref, f32[528,2048]{1,0:T(8,128)} %fusion.116.val_ref.shr_ref, f32[4,1792]{1,0:T(4,128)S(1)} %copy-done.2, f32[4,1792]{1,0:T(4,128)S(1)} %copy-done.2, f32[6,512,4]{2,1,0:T(8,128)} %bitcast.239, ...), custom_call_target="tpu_custom_call" | custom-call | flops 805306368 | bytes 6291456 | tf_op jit(solution)/shard_map/pallas_call | solution.py:648
  307.5 6.3 copy.239
  317.1 10.1 %collective-permute-done.11.before_ref = bf16[512,256]{1,0:T(8,128)(2,1)S(1)} collective-permute-done((bf16[512,256]{1,0:T(8,128)(2,1)S(1)}, bf16[512,256]{1,0:T(8,128)(2,1)S(1)}, u32[]{:S(2)}, u32[]{:S(2)}) %collective-permute-start.11) | collective-permute-done | bytes 262176 | tf_op jit(solution)/shard_map/ppermute | solution.py:681
  327.2 9.4 %shard_map.316 = bf16[512,512]{1,0:T(8,128)(2,1)S(1)} custom-call(s32[1]{0:T(128)} %bitcast.31.part_ref, f32[512,2176]{1,0:T(8,128)} %copy-done.7, f32[512,128]{1,0:T(8,128)S(1)} %get-tuple-element.245.cos_ref, f32[512,128]{1,0:T(8,128)S(1)} %get-tuple-element.246.sin_ref, bf16[512,256]{1,0:T(8,128)(2,1)S(1)} %collective-permute-done.11.before_ref, ...), custom_call_target="tpu_custom_call" | custom-call | flops 2147483648 | bytes 2097152 | tf_op jit(solution)/shard_map/pallas_call | solution.py:690
  336.6 6.7 shard_map.314
  353.5 6.8 multiply_convert_fusion.1
  383.8 19.1 %shard_map.319 = (bf16[512,512]{1,0:T(8,128)(2,1)S(1)}, f32[512,256]{1,0:T(8,128)}, f32[512,256]{1,0:T(8,128)}) custom-call(s32[1]{0:T(128)} %bitcast.31.part_ref, f32[512,2176]{1,0:T(8,128)} %copy-done.7, f32[512,128]{1,0:T(8,128)S(1)} %get-tuple-element.245.cos_ref, f32[512,128]{1,0:T(8,128)S(1)} %get-tuple-element.246.sin_ref, ...), custom_call_target="tpu_custom_call" | custom-call | flops 5368709120 | bytes 4194304 | tf_op jit(solution)/shard_map/pallas_call | solution.py:777
  405.5 9.2 %shard_map.317 = (bf16[512,1536]{1,0:T(8,128)(2,1)}, f32[512,1536]{1,0:T(8,128)}, f32[1,1536]{1,0:T(1,128)S(1)}, f32[128,1536]{1,0:T(8,128)}) custom-call(f32[512,1024]{1,0:T(8,128)} %fusion.121.ga_ref, f32[512,1024]{1,0:T(8,128)} %fusion.122.gb_ref.dout_ref, f32[512,1536]{1,0:T(8,128)} %get-tuple-element.42.scan_ref, f32[512,2176]{1,0:T(8,128)} %copy-done.7, ...), custom_call_target="tpu_custom_call" | custom-call | flops 201326592 | bytes 14155776 | tf_op jit(solution)/shard_map/pallas_call | solution.py:756
  436.2 38.8 %shard_map.318 = (bf16[528,1536]{1,0:T(8,128)(2,1)}, bf16[528,256]{1,0:T(8,128)(2,1)S(1)}, f32[6,512,8]{2,1,0:T(8,128)}, f32[6,4,512]{2,1,0:T(4,128)S(1)}, f32[4...) custom-call(f32[528,2048]{1,0:T(8,128)} %fusion.116.val_ref.shr_ref, ...), custom_call_target="tpu_custom_call" | custom-call | flops 2013265920 | bytes 9437184 | tf_op jit(solution)/shard_map/pallas_call | solution.py:788
  475.0 5.3 fusion.91
  491.0 7.5 %slice_add_fusion = f32[512,1024]{1,0:T(8,128)} fusion(f32[528,1024]{1,0:T(8,128)} %fusion.91, bf16[1024,2176]{1,0:T(8,128)(2,1)} %bitcast.255, bf16[512,24]{1,0:T(8,128)(2,1)S(1)} %get-tuple-element.153, bf16[512,512]{1,0:T(8,128)(2,1)S(1)} %copy-done.4, bf16[512,1536]{1,0:T(8,128)(2,1)} %get-tuple-element.49), kind=kOutput, calls=%fused_computation.30 | convolution fusion | flops 2291138560 | bytes 10772480 | tf_op jit(solution)/shard_map/dot_general | solution.py:55
  526.5 7.8 %collective-permute-done.37 = bf16[1,2,128,1024]{3,2,1,0:T(8,128)(2,1)S(1)} collective-permute-done((bf16[1,2,128,1024]{3,2,1,0:T(8,128)(2,1)S(1)}, bf16[1,2,128,1024]{3,2,1,0:T(8,128)(2,1)S(1)}, u32[]{:S(2)}, u32[]{:S(2)}) %collective-permute-start.37) | collective-permute-done | bytes 524320 | tf_op jit(solution)/shard_map/ppermute | solution.py:447
  547.9 8.9 %collective-permute-done.52 = bf16[2,1,128,1024]{3,2,1,0:T(8,128)(2,1)} collective-permute-done((bf16[2,1,128,1024]{3,2,1,0:T(8,128)(2,1)}, bf16[2,1,128,1024]{3,2,1,0:T(8,128)(2,1)}, u32[]{:S(2)}, u32[]{:S(2)}) %collective-permute-start.52) | collective-permute-done | bytes 524320 | tf_op jit(solution)/shard_map/ppermute | solution.py:447
  562.1 40.0 %psum.7 = f32[10824]{0:T(1024)S(1)} all-reduce(f32[10824]{0:T(1024)S(1)} %concatenate.226), channel_id=1, replica_groups=mesh['dp'=8,'tensor'=4] {'dp','tensor'}, use_global_device_ids=true, to_apply=%region_15.16 | all-reduce | flops 10824 | bytes 86592 | tf_op jit(solution)/shard_map/psum | solution.py:901
  635.7 5.0 collective-permute-done.46
  655.7 5.7 collective-permute-done.47
  662.7 11.4 %collective-permute-done.44 = bf16[1,1,128,2048]{2,3,1,0:T(8,128)(2,1)} collective-permute-done((bf16[1,1,128,2048]{2,3,1,0:T(8,128)(2,1)}, bf16[1,1,128,2048]{2,3,1,0:T(8,128)(2,1)}, u32[]{:S(2)}, u32[]{:S(2)}) %collective-permute-start.44) | collective-permute-done | bytes 524320 | tf_op jit(solution)/shard_map/ppermute | solution.py:447
  680.5 4.7 collective-permute-done.31
  687.6 8.1 %collective-permute-done.35 = bf16[1,1,128,2048]{3,2,1,0:T(8,128)(2,1)S(1)} collective-permute-done((bf16[1,1,128,2048]{3,2,1,0:T(8,128)(2,1)S(1)}, bf16[1,1,128,2048]{3,2,1,0:T(8,128)(2,1)S(1)}, u32[]{:S(2)}, u32[]{:S(2)}) %collective-permute-start.35) | collective-permute-done | bytes 524320 | tf_op jit(solution)/shard_map/ppermute | solution.py:447
  711.3 20.3 %reduce-scatter.13.cloned.1.call-done = bf16[1,128,1030]{1,2,0:T(8,128)(2,1)} async-done(((bf16[4,128,1030]{1,2,0:T(8,128)(2,1)}), bf16[1,128,1030]{1,2,0:T(8,128)(2,1)}) %reduce-scatter.13.cloned.1.call-update) | async-done | bytes 263696
  (647 shorter events, 351.0 us)
Async XLA Ops:
  7.2 99.6 %all-gather.6.cloned.1.call-start = ((), (), s32[]{:S(2)}) async-start(), calls=%async_computation.4 | async-start | bytes 1310720 | tf_op jit(solution)/shard_map/all_gather | solution.py:522
  8.0 72.1 %collective-permute-start = (bf16[16,1024]{1,0:T(8,128)(2,1)S(1)}, bf16[16,1024]{1,0:T(8,128)(2,1)S(1)}, u32[]{:S(2)}, u32[]{:S(2)}) collective-permute-start(bf16[16,1024]{1,0:T(8,128)(2,1)S(1)} %slice.331), channel_id=1, source_target_pairs={{0,1},{2,3},{4,5},{6,7},{8,9},{10,11},{12,13},{14,15},{16,17},{18,... | collective-permute-start | bytes 98312 | tf_op jit(solution)/shard_map/ppermute | solution.py:606
  14.8 95.3 %all-gather.8.cloned.1.call-start = ((), (), s32[]{:S(2)}) async-start(), calls=%async_computation.8 | async-start | bytes 1474560 | tf_op jit(solution)/shard_map/all_gather | solution.py:522
  35.5 46.8 %collective-permute-start.21 = (bf16[1,1,1,128,1024]{3,4,2,1,0:T(8,128)(2,1)S(1)}, bf16[1,1,1,128,1024]{3,4,2,1,0:T(8,128)(2,1)}, u32[]{:S(2)}, u32[]{:S(2)}) collective-permute-start(bf16[1,1,1,128,1024]{3,4,2,1,0:T(8,128)(2,1)S(1)} %get-tuple-element.203), channel_id=1, source_target_pairs={{0,8},{4,12},{8,0},{12,4},{16,24},{20,28},{24,16},{28,20},{1,9},{5... | collective-permute-start | bytes 786440 | tf_op jit(solution)/shard_map/ppermute | solution.py:447
  37.1 46.9 %collective-permute-start.24 = (bf16[1,1,1,128,1024]{3,4,2,1,0:T(8,128)(2,1)S(1)}, bf16[1,1,1,128,1024]{3,4,2,1,0:T(8,128)(2,1)}, u32[]{:S(2)}, u32[]{:S(2)}) collective-permute-start(bf16[1,1,1,128,1024]{3,4,2,1,0:T(8,128)(2,1)S(1)} %get-tuple-element.204), channel_id=1, source_target_pairs={{0,16},{4,20},{8,24},{12,28},{16,0},{20,4},{24,8},{28,12},{1,17},{... | collective-permute-start | bytes 786440 | tf_op jit(solution)/shard_map/ppermute | solution.py:447
  62.6 642.7 %reduce-scatter.7.cloned.1.call-start = ((), (), s32[]{:S(2)}) async-start(), calls=%async_computation.5 | async-start | bytes 655360 | tf_op jit(solution)/shard_map/reduce_scatter | solution.py:864
  98.2 43.2 %collective-permute-start.23 = (bf16[1,2,2,128,1024]{3,4,2,1,0:T(8,128)(2,1)}, bf16[1,2,2,128,1024]{3,4,2,1,0:T(8,128)(2,1)}, u32[]{:S(2)}, u32[]{:S(2)}) collective-permute-start(bf16[1,2,2,128,1024]{3,4,2,1,0:T(8,128)(2,1)} %pad_maximum_fusion.21), channel_id=1, source_target_pairs={{0,4},{4,0},{8,12},{12,8},{16,20},{20,16},{24,28},{28,24},{1,5},{5... | collective-permute-start | bytes 3145736 | tf_op jit(solution)/shard_map/ppermute | solution.py:447
  100.6 44.9 %collective-permute-start.26 = (bf16[1,2,2,128,1024]{3,4,2,1,0:T(8,128)(2,1)}, bf16[1,2,2,128,1024]{3,4,2,1,0:T(8,128)(2,1)}, u32[]{:S(2)}, u32[]{:S(2)}) collective-permute-start(bf16[1,2,2,128,1024]{3,4,2,1,0:T(8,128)(2,1)} %pad_maximum_fusion.22), channel_id=1, source_target_pairs={{0,4},{4,0},{8,12},{12,8},{16,20},{20,16},{24,28},{28,24},{1,5},{5... | collective-permute-start | bytes 3145736 | tf_op jit(solution)/shard_map/ppermute | solution.py:447
  103.8 46.6 %collective-permute-start.10 = (bf16[1,2,2,128,1024]{3,4,2,1,0:T(8,128)(2,1)}, bf16[1,2,2,128,1024]{3,4,2,1,0:T(8,128)(2,1)}, u32[]{:S(2)}, u32[]{:S(2)}) collective-permute-start(bf16[1,2,2,128,1024]{3,4,2,1,0:T(8,128)(2,1)} %pad_maximum_fusion.16), channel_id=1, source_target_pairs={{0,4},{4,0},{8,12},{12,8},{16,20},{20,16},{24,28},{28,24},{1,5},{5... | collective-permute-start | bytes 3145736 | tf_op jit(solution)/shard_map/ppermute | solution.py:447
  141.4 46.6 %collective-permute-start.2 = (bf16[1,2,1,128,2048]{3,4,2,1,0:T(8,128)(2,1)S(1)}, bf16[1,2,1,128,2048]{3,4,2,1,0:T(8,128)(2,1)S(1)}, u32[]{:S(2)}, u32[]{:S(2)}) collective-permute-start(bf16[1,2,1,128,2048]{3,4,2,1,0:T(8,128)(2,1)S(1)} %pad_maximum_fusion.15), channel_id=1, source_target_pairs={{0,8},{4,12},{8,0},{12,4},{16,24},{20,28},{24,16},{28,20},{1,9},{5... | collective-permute-start | bytes 3145736 | tf_op jit(solution)/shard_map/ppermute | solution.py:447
  145.5 45.4 %collective-permute-start.14 = (bf16[1,2,2,128,1024]{3,4,2,1,0:T(8,128)(2,1)S(1)}, bf16[1,2,2,128,1024]{3,4,2,1,0:T(8,128)(2,1)S(1)}, u32[]{:S(2)}, u32[]{:S(2)}) collective-permute-start(bf16[1,2,2,128,1024]{3,4,2,1,0:T(8,128)(2,1)S(1)} %copy-done.67), channel_id=1, source_target_pairs={{0,4},{4,0},{8,12},{12,8},{16,20},{20,16},{24,28},{28,24},{1,5},{5... | collective-permute-start | bytes 3145736 | tf_op jit(solution)/shard_map/ppermute | solution.py:447
  148.4 61.4 %collective-permute-start.15 = (bf16[1,1,1,128,2048]{3,4,2,1,0:T(8,128)(2,1)S(1)}, bf16[1,1,1,128,2048]{3,4,2,1,0:T(8,128)(2,1)}, u32[]{:S(2)}, u32[]{:S(2)}) collective-permute-start(bf16[1,1,1,128,2048]{3,4,2,1,0:T(8,128)(2,1)S(1)} %bitcast.245), channel_id=1, source_target_pairs={{0,8},{4,12},{8,0},{12,4},{16,24},{20,28},{24,16},{28,20},{1,9},{5... | collective-permute-start | bytes 1572872 | tf_op jit(solution)/shard_map/ppermute | solution.py:447
  150.4 61.6 %collective-permute-start.5 = (bf16[1,1,2,128,2176]{3,4,2,1,0:T(8,128)(2,1)}, bf16[1,1,2,128,2176]{3,4,2,1,0:T(8,128)(2,1)}, u32[]{:S(2)}, u32[]{:S(2)}) collective-permute-start(bf16[1,1,2,128,2176]{3,4,2,1,0:T(8,128)(2,1)} %pad_maximum_fusion.14), channel_id=1, source_target_pairs={{0,16},{4,20},{8,24},{12,28},{16,0},{20,4},{24,8},{28,12},{1,17},{... | collective-permute-start | bytes 3342344 | tf_op jit(solution)/shard_map/ppermute | solution.py:447
  168.4 71.3 %collective-permute-start.20 = (bf16[1,2,2,128,2048]{3,4,2,1,0:T(8,128)(2,1)}, bf16[1,2,2,128,2048]{3,4,2,1,0:T(8,128)(2,1)}, u32[]{:S(2)}, u32[]{:S(2)}) collective-permute-start(bf16[1,2,2,128,2048]{3,4,2,1,0:T(8,128)(2,1)} %pad_maximum_fusion.10), channel_id=1, source_target_pairs={{0,4},{4,0},{8,12},{12,8},{16,20},{20,16},{24,28},{28,24},{1,5},{5... | collective-permute-start | bytes 6291464 | tf_op jit(solution)/shard_map/ppermute | solution.py:447
  190.9 58.5 %collective-permute-start.3 = (bf16[1,2,2,128,2048]{3,4,2,1,0:T(8,128)(2,1)}, bf16[1,2,2,128,2048]{3,4,2,1,0:T(8,128)(2,1)}, u32[]{:S(2)}, u32[]{:S(2)}) collective-permute-start(bf16[1,2,2,128,2048]{3,4,2,1,0:T(8,128)(2,1)} %pad_maximum_fusion.6), channel_id=1, source_target_pairs={{0,4},{4,0},{8,12},{12,8},{16,20},{20,16},{24,28},{28,24},{1,5},{5... | collective-permute-start | bytes 6291464 | tf_op jit(solution)/shard_map/ppermute | solution.py:447
  214.8 51.6 %collective-permute-start.6 = (bf16[1,2,2,128,2176]{3,4,2,1,0:T(8,128)(2,1)}, bf16[1,2,2,128,2176]{3,4,2,1,0:T(8,128)(2,1)}, u32[]{:S(2)}, u32[]{:S(2)}) collective-permute-start(bf16[1,2,2,128,2176]{3,4,2,1,0:T(8,128)(2,1)} %pad_maximum_fusion.5), channel_id=1, source_target_pairs={{0,4},{4,0},{8,12},{12,8},{16,20},{20,16},{24,28},{28,24},{1,5},{5... | collective-permute-start | bytes 6684680 | tf_op jit(solution)/shard_map/ppermute | solution.py:447
  239.6 64.4 %collective-permute-start.17 = (bf16[1,2,2,128,2048]{3,4,2,1,0:T(8,128)(2,1)}, bf16[1,2,2,128,2048]{3,4,2,1,0:T(8,128)(2,1)}, u32[]{:S(2)}, u32[]{:S(2)}) collective-permute-start(bf16[1,2,2,128,2048]{3,4,2,1,0:T(8,128)(2,1)} %pad_maximum_fusion.9), channel_id=1, source_target_pairs={{0,4},{4,0},{8,12},{12,8},{16,20},{20,16},{24,28},{28,24},{1,5},{5... | collective-permute-start | bytes 6291464 | tf_op jit(solution)/shard_map/ppermute | solution.py:447
  301.0 35.6 %collective-permute-start.7 = (f32[128,1536]{1,0:T(8,128)}, f32[128,1536]{1,0:T(8,128)S(1)}, u32[]{:S(2)}, u32[]{:S(2)}) collective-permute-start(f32[128,1536]{1,0:T(8,128)} %get-tuple-element.40), channel_id=1, source_target_pairs={{0,1},{2,3},{4,5},{6,7},{8,9},{10,11},{12,13},{14,15},{16,17},{18,... | collective-permute-start | bytes 2359304 | tf_op jit(solution)/shard_map/ppermute | solution.py:658
  416.0 104.3 %collective-permute-start.51 = (bf16[512,1024]{1,0:T(8,128)(2,1)}, bf16[512,1024]{1,0:T(8,128)(2,1)}, u32[]{:S(2)}, u32[]{:S(2)}) collective-permute-start(bf16[512,1024]{1,0:T(8,128)(2,1)} %convolution_convert_fusion.4), channel_id=1, source_target_pairs={{0,4},{4,0},{8,12},{12,8},{16,20},{20,16},{24,28},{28,24},{1,5},{5... | collective-permute-start | bytes 3145736 | tf_op jit(solution)/shard_map/ppermute | solution.py:447
  416.1 107.7 %collective-permute-start.48 = (bf16[512,1024]{1,0:T(8,128)(2,1)}, bf16[512,1024]{1,0:T(8,128)(2,1)}, u32[]{:S(2)}, u32[]{:S(2)}) collective-permute-start(bf16[512,1024]{1,0:T(8,128)(2,1)} %convolution_convert_fusion.5), channel_id=1, source_target_pairs={{0,4},{4,0},{8,12},{12,8},{16,20},{20,16},{24,28},{28,24},{1,5},{5... | collective-permute-start | bytes 3145736 | tf_op jit(solution)/shard_map/ppermute | solution.py:447
  416.6 101.1 %collective-permute-start.36 = (bf16[512,1024]{1,0:T(8,128)(2,1)}, bf16[512,1024]{1,0:T(8,128)(2,1)}, u32[]{:S(2)}, u32[]{:S(2)}) collective-permute-start(bf16[512,1024]{1,0:T(8,128)(2,1)} %convolution_convert_fusion.7), channel_id=1, source_target_pairs={{0,4},{4,0},{8,12},{12,8},{16,20},{20,16},{24,28},{28,24},{1,5},{5... | collective-permute-start | bytes 3145736 | tf_op jit(solution)/shard_map/ppermute | solution.py:447
  433.2 80.3 %collective-permute-start.39 = (bf16[512,1024]{1,0:T(8,128)(2,1)}, bf16[512,1024]{1,0:T(8,128)(2,1)}, u32[]{:S(2)}, u32[]{:S(2)}) collective-permute-start(bf16[512,1024]{1,0:T(8,128)(2,1)} %convolution_convert_fusion.6), channel_id=1, source_target_pairs={{0,4},{4,0},{8,12},{12,8},{16,20},{20,16},{24,28},{28,24},{1,5},{5... | collective-permute-start | bytes 3145736 | tf_op jit(solution)/shard_map/ppermute | solution.py:447
  508.4 99.0 %collective-permute-start.45 = (bf16[512,2048]{1,0:T(8,128)(2,1)}, bf16[512,2048]{1,0:T(8,128)(2,1)}, u32[]{:S(2)}, u32[]{:S(2)}) collective-permute-start(bf16[512,2048]{1,0:T(8,128)(2,1)} %convolution_convert_fusion.1), channel_id=1, source_target_pairs={{0,4},{4,0},{8,12},{12,8},{16,20},{20,16},{24,28},{28,24},{1,5},{5... | collective-permute-start | bytes 6291464 | tf_op jit(solution)/shard_map/ppermute | solution.py:447
  514.8 101.5 %collective-permute-start.42 = (bf16[512,2048]{1,0:T(8,128)(2,1)}, bf16[512,2048]{1,0:T(8,128)(2,1)}, u32[]{:S(2)}, u32[]{:S(2)}) collective-permute-start(bf16[512,2048]{1,0:T(8,128)(2,1)} %convolution_convert_fusion.2), channel_id=1, source_target_pairs={{0,4},{4,0},{8,12},{12,8},{16,20},{20,16},{24,28},{28,24},{1,5},{5... | collective-permute-start | bytes 6291464 | tf_op jit(solution)/shard_map/ppermute | solution.py:447
  517.7 107.1 %collective-permute-start.33 = (bf16[512,2048]{1,0:T(8,128)(2,1)}, bf16[512,2048]{1,0:T(8,128)(2,1)}, u32[]{:S(2)}, u32[]{:S(2)}) collective-permute-start(bf16[512,2048]{1,0:T(8,128)(2,1)} %convolution_convert_fusion.3), channel_id=1, source_target_pairs={{0,4},{4,0},{8,12},{12,8},{16,20},{20,16},{24,28},{28,24},{1,5},{5... | collective-permute-start | bytes 6291464 | tf_op jit(solution)/shard_map/ppermute | solution.py:447
  547.8 159.7 %reduce-scatter.11.cloned.1.call-start = ((), (), s32[]{:S(2)}) async-start(), calls=%async_computation.7 | async-start | bytes 655360 | tf_op jit(solution)/shard_map/reduce_scatter | solution.py:864
  558.9 44.5 %collective-permute-start.53 = (bf16[1,1,128,1024]{3,2,1,0:T(8,128)(2,1)}, bf16[1,1,128,1024]{3,2,1,0:T(8,128)(2,1)S(1)}, u32[]{:S(2)}, u32[]{:S(2)}) collective-permute-start(bf16[1,1,128,1024]{3,2,1,0:T(8,128)(2,1)} %slice.519), channel_id=1, source_target_pairs={{0,16},{4,20},{8,24},{12,28},{16,0},{20,4},{24,8},{28,12},{1,17},{... | collective-permute-start | bytes 786440 | tf_op jit(solution)/shard_map/ppermute | solution.py:447
  560.7 44.5 %collective-permute-start.50 = (bf16[1,1,128,1024]{3,2,1,0:T(8,128)(2,1)}, bf16[1,1,128,1024]{3,2,1,0:T(8,128)(2,1)}, u32[]{:S(2)}, u32[]{:S(2)}) collective-permute-start(bf16[1,1,128,1024]{3,2,1,0:T(8,128)(2,1)} %slice.515), channel_id=1, source_target_pairs={{0,8},{4,12},{8,0},{12,4},{16,24},{20,28},{24,16},{28,20},{1,9},{5... | collective-permute-start | bytes 786440 | tf_op jit(solution)/shard_map/ppermute | solution.py:447
  607.4 101.7 %reduce-scatter.9.cloned.1.call-start = ((), (), s32[]{:S(2)}) async-start(), calls=%async_computation.6 | async-start | bytes 1310720 | tf_op jit(solution)/shard_map/reduce_scatter | solution.py:864
  631.3 45.4 %collective-permute-start.34 = (bf16[2,1,128,2048]{3,2,1,0:T(8,128)(2,1)}, bf16[2,1,128,2048]{3,2,1,0:T(8,128)(2,1)}, u32[]{:S(2)}, u32[]{:S(2)}) collective-permute-start(bf16[2,1,128,2048]{3,2,1,0:T(8,128)(2,1)} %slice.472), channel_id=1, source_target_pairs={{0,8},{4,12},{8,0},{12,4},{16,24},{20,28},{24,16},{28,20},{1,9},{5... | collective-permute-start | bytes 3145736 | tf_op jit(solution)/shard_map/ppermute | solution.py:447
  653.6 31.7 %collective-permute-start.31 = (bf16[1,2,128,2176]{2,3,1,0:T(8,128)(2,1)}, bf16[1,2,128,2176]{2,3,1,0:T(8,128)(2,1)}, u32[]{:S(2)}, u32[]{:S(2)}) collective-permute-start(bf16[1,2,128,2176]{2,3,1,0:T(8,128)(2,1)} %copy.251), channel_id=1, source_target_pairs={{0,16},{4,20},{8,24},{12,28},{16,0},{20,4},{24,8},{28,12},{1,17},{... | collective-permute-start | bytes 3342344 | tf_op jit(solution)/shard_map/ppermute | solution.py:447
  676.6 54.9 %reduce-scatter.13.cloned.1.call-start = ((), (), s32[]{:S(2)}) async-start(), calls=%async_computation.9 | async-start | bytes 1320960
  (150 other events, 1846.2 us)
Sparse Core Ops, SparseCore 0:
  14.9 37.4 all-gather.5
  62.8 29.0 all-gather.7
  547.8 20.9 reduce-scatter.6
  607.6 21.8 reduce-scatter.10
  676.7 26.7 reduce-scatter.8
  705.7 25.7 reduce-scatter.12

commit v2 on v1

v2 whole, which is shorter than its diff:
```python
import functools

import jax
import jax.numpy as jnp
from jax import lax
from jax.experimental import pallas as pl
from jax.experimental.pallas import tpu as pltpu
from jax.sharding import PartitionSpec as P

PH = 64
NS = 128
KC = 4
AH = 8
KVH = 2
HD = 64
LEN = 1024
CHUNK = 128
HALO = 16
GROUP = 6
SLOT = 8
GW = GROUP * PH

epsilon = 1e-05
rope_base = 100000000000.0
masked_fill = -1e30
highest = lax.Precision.HIGHEST
f32 = jnp.float32
bf16 = jnp.bfloat16
VMEM_BYTES = 52 * 1024 * 1024


def call(
    kernel, grid, in_specs, out_specs, out_shape, scratch=(), flops=0, moved=0, aliases=None, deps=()
):
    late = jax.tree.leaves(deps)
    count = len(in_specs)

    def body(*refs):
        kernel(*refs[:count], *refs[count + len(late) :])

    run = pl.pallas_call(
        body,
        grid=grid,
        in_specs=list(in_specs) + [pl.BlockSpec(memory_space=pl.ANY)] * len(late),
        out_specs=out_specs,
        out_shape=out_shape,
        scratch_shapes=list(scratch),
        input_output_aliases=aliases or {},
        compiler_params=pltpu.CompilerParams(
            vmem_limit_bytes=VMEM_BYTES, dimension_semantics=("arbitrary",) * len(grid)
        ),
        cost_estimate=pl.CostEstimate(flops=1, bytes_accessed=1, transcendentals=0),
    )
    return lambda *args: run(*args, *late)


def spec(block, index):
    return pl.BlockSpec(block, index)


def shape(dims, kind):
    return jax.ShapeDtypeStruct(dims, kind)


def dot(left, right, dims):
    return lax.dot_general(left, right, ((dims[:1], dims[1:]), ((), ())), preferred_element_type=f32)


NN = (1, 0)
NT = (1, 1)
TN = (0, 0)


def sigmoid(value):
    return 1.0 / (1.0 + jnp.exp(-value))


def pair_lanes(left, right, rows):
    lane = lax.broadcasted_iota(jnp.int32, (rows, 2 * PH), 1)
    return jnp.where(lane < PH, left, right)


def spread_heads(columns, first, count, rows):
    parts = [
        pair_lanes(
            columns[:, first + 2 * p : first + 2 * p + 1],
            columns[:, first + 2 * p + 1 : first + 2 * p + 2],
            rows,
        )
        for p in range(count // 2)
    ]
    return jnp.concatenate(parts, axis=1) if len(parts) > 1 else parts[0]


def conv_of(ref, taps, rows):
    width = taps.shape[1]
    total = ref[pl.ds(HALO - KC + 1, rows), :width] * taps[0:1, :]
    for offset in range(1, KC):
        moved = ref[pl.ds(HALO - KC + 1 + offset, rows), :width]
        total = total + moved * taps[offset : offset + 1, :]
    return total


def causal_mask(transposed):
    row = lax.broadcasted_iota(jnp.int32, (CHUNK, CHUNK), 0)
    col = lax.broadcasted_iota(jnp.int32, (CHUNK, CHUNK), 1)
    return col >= row if transposed else row >= col


def exact(left, right, dims):
    return lax.dot_general(
        left,
        right,
        ((dims[:1], dims[1:]), ((), ())),
        precision=highest,
        preferred_element_type=f32,
    )


def lower_ones():
    return jnp.where(causal_mask(False), 1.0, 0.0)


def softplus(value):
    return jnp.maximum(value, 0.0) + jnp.log1p(jnp.exp(-jnp.abs(value)))


def prepare_kernel(
    t0_ref, t1_ref, t2_ref, t3_ref, bias_ref, rate_ref,
    shr_ref, step_ref, cols_ref, rows_ref, grow_ref,
):
    tails = [t0_ref[...], t1_ref[...], t2_ref[...], t3_ref[...]]
    ext = tails[0].shape[0]
    shr_ref[:, :NS] = pair_lanes(tails[0], pltpu.roll(tails[1], PH, 1), ext)
    shr_ref[:, NS:] = pair_lanes(tails[2], pltpu.roll(tails[3], PH, 1), ext)
    rows = ext - HALO
    lane = lax.broadcasted_iota(jnp.int32, (rows, 128), 1)
    steps = jnp.zeros((rows, 128), f32)
    for t in range(4):
        moved = pltpu.roll(tails[t][HALO:], (GROUP * t - PH) % 128, 1)
        steps = jnp.where(lane // GROUP == t, moved, steps)
    steps = steps + bias_ref[...]
    step_ref[...] = steps
    dt = softplus(steps)
    decay = -rate_ref[...] * dt
    lower = lower_ones()
    prefix = jnp.zeros((1, 128), f32)
    parts = []
    for c in range(rows // CHUNK):
        sl = slice(c * CHUNK, (c + 1) * CHUNK)
        cum = exact(lower, decay[sl], NN)
        parts.append(cum)
        grow_ref[sl, :] = jnp.exp(cum + prefix)
        prefix = prefix + cum[CHUNK - 1 : CHUNK]
    cum = jnp.concatenate(parts, axis=0)
    for t in range(4):
        shift = (-GROUP * t) % 128
        dt_own = pltpu.roll(dt, shift, 1) if t else dt
        cum_own = pltpu.roll(cum, shift, 1) if t else cum
        both = jnp.where(lane < SLOT, dt_own, pltpu.roll(cum_own, SLOT, 1))
        cols_ref[t] = both[:, : 2 * SLOT]
        rows_ref[t] = jnp.transpose(cum_own)[:SLOT]


def mixer_kernel(
    val_ref, shr_ref, tapv_ref, taps_ref, cols_ref, cumr_ref, skip_ref,
    y_ref, state_ref, bc_ref, aff_ref,
):
    rows = y_ref.shape[0]
    chunks = rows // CHUNK

    @pl.when(pl.program_id(0) == 0)
    def _():
        pre = conv_of(shr_ref, taps_ref[...], rows)
        bc_ref[...] = (pre * sigmoid(pre)).astype(bf16)
        for c in range(chunks):
            sl = pl.ds(c * CHUNK, CHUNK)
            aff_ref[c] = dot(bc_ref[sl, NS:], bc_ref[sl, :NS], NT)

    pre = conv_of(val_ref, tapv_ref[...], rows)
    head_in = pre * sigmoid(pre)
    mask = causal_mask(False)
    skip = skip_ref[...]
    state = jnp.zeros((NS, GW), f32)
    for c in range(chunks):
        sl = pl.ds(c * CHUNK, CHUNK)
        x = head_in[c * CHUNK : (c + 1) * CHUNK]
        cols = cols_ref[0, sl, :]
        cumc = cols[:, SLOT:]
        cumr = cumr_ref[0, :, sl]
        w = x * spread_heads(cols, 0, GROUP, CHUNK)
        w_low = w.astype(bf16)
        inner = []
        for p in range(GROUP // 2):
            both = []
            for h in (2 * p, 2 * p + 1):
                gap = cumc[:, h : h + 1] - cumr[h : h + 1, :]
                decay = jnp.exp(jnp.where(mask, gap, masked_fill))
                weight = (aff_ref[c] * decay).astype(bf16)
                both.append(dot(weight, w_low[:, p * 2 * PH : (p + 1) * 2 * PH], NN))
            inner.append(pair_lanes(both[0], both[1], CHUNK))
        out = jnp.concatenate(inner, axis=1) + skip * x
        b_now = bc_ref[sl, :NS]
        c_now = bc_ref[sl, NS:]
        last = cumc[CHUNK - 1 : CHUNK, :]
        if c > 0:
            grown = spread_heads(jnp.exp(cumc), 0, GROUP, CHUNK)
            out = out + dot(c_now, state.astype(bf16), NN) * grown
        y_ref[sl, :] = out
        to_end = spread_heads(jnp.exp(last - cumc), 0, GROUP, CHUNK)
        added = dot(b_now, (w * to_end).astype(bf16), TN)
        fall = spread_heads(jnp.exp(last), 0, GROUP, 1)
        state = state * fall + added
    state_ref[...] = state.astype(bf16)


def gate_lanes(ref, width):
    count = ref.shape[1] // (width + 2 * PH * 2)
    step = ref.shape[1] // count
    return jnp.concatenate([ref[:, t * step : t * step + width] for t in range(count)], axis=1)


def finish_kernel(
    y_ref, gate_ref, bc_ref, grow_ref, state_ref, gain_ref, attn_ref, scan_ref, heads_ref
):
    rows, width = y_ref.shape
    grown = spread_heads(grow_ref[...], 0, width // PH, rows)
    scan = y_ref[...] + dot(bc_ref[:, NS:], state_ref[...], NN) * grown
    scan_ref[...] = scan
    gate = gate_lanes(gate_ref, GW)
    pre = scan * gate * sigmoid(gate)
    inv = lax.rsqrt(jnp.mean(pre * pre, axis=1, keepdims=True) + epsilon)
    low = (pre * inv * gain_ref[...]).astype(bf16)
    step = GW + 2 * HD
    for t in range(width // GW):
        heads_ref[:, t * step : t * step + GW] = low[:, t * GW : (t + 1) * GW]
        heads_ref[:, t * step + GW : (t + 1) * step] = attn_ref[:, t * 2 * HD : (t + 1) * 2 * HD]


def ungate_kernel(
    grad_ref, scan_ref, gate_ref, bc_ref, grow_ref, gain_ref,
    dgate_ref, dscan_ref, dgain_ref, dstate_ref,
):
    rows, width = scan_ref.shape
    scan = scan_ref[...]
    gate = gate_lanes(gate_ref, GW)
    sig = sigmoid(gate)
    silu = gate * sig
    pre = scan * silu
    inv = lax.rsqrt(jnp.mean(pre * pre, axis=1, keepdims=True) + epsilon)
    normed = pre * inv
    step = GW + 2 * HD
    grad = jnp.concatenate(
        [grad_ref[:, t * step : t * step + GW] for t in range(width // GW)], axis=1
    )
    u = grad * gain_ref[...]
    cross = jnp.mean(u * normed, axis=1, keepdims=True)
    dpre = inv * (u - normed * cross)
    dscan = dpre * silu
    dgate_ref[...] = (dpre * scan * sig * (1.0 + gate * (1.0 - sig))).astype(bf16)
    dscan_ref[...] = dscan
    grown = spread_heads(grow_ref[...], 0, width // PH, rows)
    dstate = dot(bc_ref[:, NS:], (dscan * grown).astype(bf16), TN)
    dgain = jnp.sum(grad * normed, axis=0, keepdims=True)
    first = pl.program_id(0) == 0

    @pl.when(first)
    def _():
        dgain_ref[...] = dgain
        dstate_ref[...] = dstate

    @pl.when(jnp.logical_not(first))
    def _():
        dgain_ref[...] += dgain
        dstate_ref[...] += dstate


def split_sum(value, ones_at):
    high = value.astype(bf16)
    low = (value - high.astype(f32)).astype(bf16)
    return dot(high, ones_at, NN) + dot(low, ones_at, NN)


def unconv(ref, taps, dact, pad_ref, out_ref, dtaps_ref, rows):
    pre = conv_of(ref, taps, rows)
    sig = sigmoid(pre)
    dpre = dact * sig * (1.0 + pre * (1.0 - sig))
    lead = HALO + 8
    width = dact.shape[1]
    pad_ref[pl.ds(0, lead), :width] = jnp.zeros((lead, width), f32)
    pad_ref[pl.ds(lead + rows, 8), :width] = jnp.zeros((8, width), f32)
    pad_ref[pl.ds(lead, rows), :width] = dpre
    total = None
    dtaps = []
    for offset in range(KC):
        part = pad_ref[pl.ds(8 + KC - 1 - offset, rows + HALO), :width]
        part = part * taps[offset : offset + 1, :]
        total = part if total is None else total + part
        moved = ref[pl.ds(HALO - KC + 1 + offset, rows), :width]
        dtaps.append(jnp.sum(dpre * moved, axis=0, keepdims=True))
    out_ref[:, :width] = total.astype(out_ref.dtype)
    dtaps_ref[...] = jnp.concatenate(dtaps, axis=0)


def unmix_kernel(
    val_ref, shr_ref, tapv_ref, taps_ref, in_ref, cumr_ref, skip_ref, bc_ref,
    dscan_ref, enter_ref, dleave_ref,
    dval_ref, dshr_ref, cols_ref, rows_ref, dlast_ref, dtapv_ref, dtaps_ref, dskip_ref,
    daff_ref, dbc_ref, aff_ref, dx_ref, states_ref, pad_ref,
):
    rows = dscan_ref.shape[0]
    chunks = rows // CHUNK
    step = pl.program_id(0)

    @pl.when(step == 0)
    def _():
        for c in range(chunks):
            sl = pl.ds(c * CHUNK, CHUNK)
            aff_ref[c] = dot(bc_ref[sl, :NS], bc_ref[sl, NS:], NT)
        daff_ref[...] = jnp.zeros(daff_ref.shape, f32)
        dbc_ref[...] = jnp.zeros(dbc_ref.shape, f32)

    pre = conv_of(val_ref, tapv_ref[...], rows)
    dx_ref[...] = pre * sigmoid(pre)
    mask = causal_mask(True)
    skip = skip_ref[...]
    lane = lax.broadcasted_iota(jnp.int32, (GW, 128), 0) // PH
    slot = lax.broadcasted_iota(jnp.int32, (GW, 128), 1)
    ones_dt = jnp.where(lane == slot, 1.0, 0.0).astype(bf16)
    ones_cum = jnp.where(lane + SLOT == slot, 1.0, 0.0).astype(bf16)
    half_lane = lax.broadcasted_iota(jnp.int32, (CHUNK, 2 * PH), 1) // PH
    slot_lane = lax.broadcasted_iota(jnp.int32, (CHUNK, 128), 1)

    state = enter_ref[...].astype(f32)
    states_ref[0] = state
    for c in range(chunks - 1):
        sl = pl.ds(c * CHUNK, CHUNK)
        cumc = in_ref[0, sl, SLOT:]
        last = cumc[CHUNK - 1 : CHUNK, :]
        scale = spread_heads(in_ref[0, sl, :SLOT] * jnp.exp(last - cumc), 0, GROUP, CHUNK)
        added = dot(bc_ref[sl, :NS], (dx_ref[sl, :] * scale).astype(bf16), TN)
        state = state * spread_heads(jnp.exp(last), 0, GROUP, 1) + added
        states_ref[c + 1] = state

    dstate = dleave_ref[...].astype(f32)
    dskip = jnp.zeros((1, GW), f32)
    for c in reversed(range(chunks)):
        sl = pl.ds(c * CHUNK, CHUNK)
        x = dx_ref[sl, :]
        dy = dscan_ref[sl, :]
        dy_low = dy.astype(bf16)
        cumc = in_ref[0, sl, SLOT:]
        cumr = cumr_ref[0, :, sl]
        last = cumc[CHUNK - 1 : CHUNK, :]
        dt = spread_heads(in_ref[0, sl, :SLOT], 0, GROUP, CHUNK)
        w = x * dt
        w_low = w.astype(bf16)
        b_now = bc_ref[sl, :NS]
        c_now = bc_ref[sl, NS:]
        affinity = aff_ref[c]
        dcum = jnp.zeros((CHUNK, 128), f32)
        daff = daff_ref[c]
        dw_parts = []
        for p in range(GROUP // 2):
            pair = slice(p * 2 * PH, (p + 1) * 2 * PH)
            both = []
            for h in (2 * p, 2 * p + 1):
                gap = cumr[h : h + 1, :] - cumc[:, h : h + 1]
                decay = jnp.exp(jnp.where(mask, gap, masked_fill))
                weight = affinity * decay
                w_own = jnp.where(half_lane == h - 2 * p, w[:, pair], 0.0).astype(bf16)
                dweight = dot(w_own, dy_low[:, pair], NT)
                daff = daff + dweight * decay
                moved = dweight * weight
                rows_ref[0, h : h + 1, sl] = jnp.sum(moved, axis=0, keepdims=True)
                dcum = dcum - jnp.where(
                    slot_lane == SLOT + h, jnp.sum(moved, axis=1, keepdims=True), 0.0
                )
                both.append(dot(weight.astype(bf16), dy_low[:, pair], NN))
            dw_parts.append(pair_lanes(both[0], both[1], CHUNK))
        daff_ref[c] = daff
        state = states_ref[c]
        state_low = state.astype(bf16)
        dstate_low = dstate.astype(bf16)
        grown = spread_heads(jnp.exp(cumc), 0, GROUP, CHUNK)
        to_end = spread_heads(jnp.exp(last - cumc), 0, GROUP, CHUNK)
        fall = spread_heads(jnp.exp(last), 0, GROUP, 1)
        dy_grown = (dy * grown).astype(bf16)
        carried = dot(c_now, state_low, NN) * grown
        from_end = dot(b_now, dstate_low, NN) * to_end
        dbc_ref[sl, NS:] += dot(dy_grown, state_low, NT)
        dbc_ref[sl, :NS] += dot((w * to_end).astype(bf16), dstate_low, NT)
        dw = jnp.concatenate(dw_parts, axis=1) + from_end
        ended = w * from_end
        cols_ref[0, sl, :] = (
            dcum + split_sum(dw * x, ones_dt) + split_sum(dy * carried - ended, ones_cum)
        )
        dlast_ref[c : c + 1, :] = jnp.sum(ended, axis=0, keepdims=True) + fall * jnp.sum(
            state * dstate, axis=0, keepdims=True
        )
        dstate = fall * dstate + dot(c_now, dy_grown, TN)
        dskip = dskip + jnp.sum(dy * x, axis=0, keepdims=True)
        dx_ref[sl, :] = dw * dt + skip * dy
    dskip_ref[...] = dskip
    unconv(val_ref, tapv_ref[...], dx_ref[...], pad_ref, dval_ref, dtapv_ref, rows)

    @pl.when(step == pl.num_programs(0) - 1)
    def _():
        for c in range(chunks):
            sl = pl.ds(c * CHUNK, CHUNK)
            daff_low = daff_ref[c].astype(bf16)
            dbc_ref[sl, :NS] += dot(daff_low, bc_ref[sl, NS:], NN)
            dbc_ref[sl, NS:] += dot(daff_low, bc_ref[sl, :NS], TN)
        unconv(shr_ref, taps_ref[...], dbc_ref[...], pad_ref, dshr_ref, dtaps_ref, rows)


def settle_kernel(
    low_in_ref, dshr_ref, cols_ref, rows_ref, dlast_ref, step_ref, rate_ref,
    low_ref, ddecay_ref, dbias_ref, dstep_ref,
):
    rows = step_ref.shape[0]
    t = pl.program_id(0)
    lane = lax.broadcasted_iota(jnp.int32, (rows, 128), 1)

    @pl.when(t == 0)
    def _():
        ddt = jnp.zeros((rows, 128), f32)
        dcum = jnp.zeros((rows, 128), f32)
        for i in range(4):
            own = lane // GROUP == i
            cols = cols_ref[i]
            ddt = jnp.where(own, pltpu.roll(cols, GROUP * i, 1) if i else cols, ddt)
            dcum = jnp.where(own, pltpu.roll(cols, (GROUP * i - SLOT) % 128, 1), dcum)
        filled = jnp.concatenate(
            [rows_ref[i] for i in range(4)] + [jnp.zeros((128 - 4 * SLOT, rows), f32)], axis=0
        )
        turned = jnp.transpose(filled)
        for i in range(4):
            moved = pltpu.roll(turned, ((GROUP - SLOT) * i) % 128, 1) if i else turned
            dcum = dcum + jnp.where(lane // GROUP == i, moved, 0.0)
        width = dlast_ref.shape[1]
        head = lax.broadcasted_iota(jnp.int32, (width, 128), 0) // PH
        place = lax.broadcasted_iota(jnp.int32, (width, 128), 1)
        at_end = exact(dlast_ref[...], jnp.where(head == place, 1.0, 0.0), NN)
        lower = lower_ones()
        steps = step_ref[...]
        rate = rate_ref[...]
        decay = -rate * softplus(steps)
        ddecay = jnp.zeros((1, 128), f32)
        dbias = jnp.zeros((1, 128), f32)
        for c in range(rows // CHUNK):
            sl = slice(c * CHUNK, (c + 1) * CHUNK)
            dlog = exact(lower, dcum[sl], TN) + at_end[c : c + 1]
            ddecay = ddecay + jnp.sum(dlog * decay[sl], axis=0, keepdims=True)
            dstep = (ddt[sl] - rate * dlog) * sigmoid(steps[sl])
            dbias = dbias + jnp.sum(dstep, axis=0, keepdims=True)
            dstep_ref[sl, :] = dstep
        ddecay_ref[...] = ddecay
        dbias_ref[...] = dbias

    for i in range(4):

        @pl.when(t == i)
        def _(i=i):
            shared = dshr_ref[:, (i // 2) * 2 * PH : (i // 2 + 1) * 2 * PH]
            if i % 2:
                shared = pltpu.roll(shared, PH, 1)
            steps = pltpu.roll(dstep_ref[...], (PH - GROUP * i) % 128, 1)
            steps = jnp.where((lane >= PH) & (lane < PH + GROUP), steps, 0.0)
            low_ref[pl.ds(0, HALO), :] = jnp.where(lane < PH, 1.0, 0.0)[:HALO].astype(bf16) * (
                shared[:HALO].astype(bf16)
            )
            low_ref[pl.ds(HALO, rows), :] = jnp.where(lane < PH, shared[HALO:], steps).astype(bf16)


def first_back_kernel(
    a_ref, b_ref, late_ref, rows_ref, middle_ref, gain_ref, more_ref, out_ref, gains_ref
):
    rows = a_ref.shape[0]
    out_ref[...] = a_ref[...] + b_ref[pl.ds(HALO, rows), :]
    out_ref[pl.ds(rows - HALO, HALO), :] += late_ref[...]
    grad = out_ref[...]
    values = rows_ref[...].astype(f32)
    inv = lax.rsqrt(jnp.mean(values * values, axis=1, keepdims=True) + epsilon)
    normed = values * inv
    gains_ref[...] = jnp.zeros(gains_ref.shape, f32)
    gains_ref[0:1, :] = jnp.sum(grad * normed, axis=0, keepdims=True)
    gains_ref[1:2, :] = more_ref[...]
    scaled = grad * gain_ref[...]
    cross = jnp.mean(scaled * normed, axis=1, keepdims=True)
    out_ref[...] = middle_ref[...] + inv * (scaled - normed * cross)


def swap_halves(value):
    half = HD // 2
    width = value.shape[1]
    lane = lax.broadcasted_iota(jnp.int32, value.shape, 1) % HD
    return jnp.where(
        lane < half, pltpu.roll(value, width - half, 1), pltpu.roll(value, half, 1)
    )


def rotate_kernel(t0_ref, t1_ref, t2_ref, t3_ref, cos_ref, sin_ref, out_ref):
    rows = cos_ref.shape[0]
    for head, (key, value) in enumerate(((t0_ref, t1_ref), (t2_ref, t3_ref))):
        both = pair_lanes(key[...], pltpu.roll(value[...], HD, 1), rows)
        out = both * cos_ref[...] + swap_halves(both) * sin_ref[...]
        out_ref[:, head * 2 * HD : (head + 1) * 2 * HD] = out.astype(bf16)


def unrotate_kernel(low_in_ref, own_ref, late_ref, cos_ref, sin_ref, out_ref):
    value = own_ref[...] + late_ref[...].astype(f32)
    value = value * cos_ref[...] + swap_halves(value * sin_ref[...])
    odd = lax.rem(pl.program_id(0), 2) == 1
    value = jnp.where(odd, pltpu.roll(value, HD, 1), value)
    lane = lax.broadcasted_iota(jnp.int32, value.shape, 1)
    out_ref[...] = jnp.where(lane < HD, value, 0.0).astype(bf16)


def head_queries(query, which):
    lane = lax.broadcasted_iota(jnp.int32, query.shape, 1)
    moved = pltpu.roll(query, HD, 1) if which else query
    return jnp.where(lane < HD, moved, 0.0)


def score_weights(query, before, own, allowed):
    early = jnp.where(allowed, dot(query, before, NT), masked_fill)
    late = dot(query, own, NT)
    row = lax.broadcasted_iota(jnp.int32, late.shape, 0)
    col = lax.broadcasted_iota(jnp.int32, late.shape, 1)
    late = jnp.where(row >= col, late, masked_fill)
    top = jnp.maximum(
        jnp.max(early, axis=1, keepdims=True), jnp.max(late, axis=1, keepdims=True)
    )
    early = jnp.exp(early - top)
    late = jnp.exp(late - top)
    total = jnp.sum(early, axis=1, keepdims=True) + jnp.sum(late, axis=1, keepdims=True)
    return early, late, 1.0 / total


def rotated_queries(q_ref, cos_ref, sin_ref):
    query = q_ref[...]
    return (query * cos_ref[...] + swap_halves(query) * sin_ref[...]) * (HD**-0.5)


def attend_kernel(part_ref, q_ref, cos_ref, sin_ref, before_ref, own_ref, out_ref):
    allowed = part_ref[0] > 0
    query = rotated_queries(q_ref, cos_ref, sin_ref)
    before = before_ref[...]
    own = own_ref[...]
    results = []
    for which in range(2):
        q_low = head_queries(query, which).astype(bf16)
        early, late, scale = score_weights(q_low, before, own, allowed)
        result = dot(early.astype(bf16), before, NN) + dot(late.astype(bf16), own, NN)
        results.append(result * scale)
    out_ref[...] = pair_lanes(pltpu.roll(results[0], HD, 1), results[1], query.shape[0]).astype(
        bf16
    )


def unattend_kernel(
    part_ref, q_ref, cos_ref, sin_ref, before_ref, own_ref, dout_ref,
    dq_ref, dbefore_ref, down_ref,
):
    allowed = part_ref[0] > 0
    query = rotated_queries(q_ref, cos_ref, sin_ref)
    before = before_ref[...]
    own = own_ref[...]
    dout = dout_ref[...]
    lane = lax.broadcasted_iota(jnp.int32, dout.shape, 1)
    dqs = []
    dbefore = None
    down = None
    for which in range(2):
        q_low = head_queries(query, which).astype(bf16)
        early, late, scale = score_weights(q_low, before, own, allowed)
        early = early * scale
        late = late * scale
        dout_own = dout if which else pltpu.roll(dout, HD, 1)
        dout_low = jnp.where(lane >= HD, dout_own, 0.0).astype(bf16)
        dearly = dot(dout_low, before, NT)
        dlate = dot(dout_low, own, NT)
        cross = jnp.sum(early * dearly, axis=1, keepdims=True) + jnp.sum(
            late * dlate, axis=1, keepdims=True
        )
        dearly = (early * (dearly - cross)).astype(bf16)
        dlate = (late * (dlate - cross)).astype(bf16)
        dqs.append(dot(dearly, before, NN) + dot(dlate, own, NN))
        part_before = dot(dearly, q_low, TN) + dot(early.astype(bf16), dout_low, TN)
        part_own = dot(dlate, q_low, TN) + dot(late.astype(bf16), dout_low, TN)
        dbefore = part_before if dbefore is None else dbefore + part_before
        down = part_own if down is None else down + part_own
    dq = pair_lanes(dqs[0], pltpu.roll(dqs[1], HD, 1), dout.shape[0]) * (HD**-0.5)
    dq_ref[...] = (dq * cos_ref[...] + swap_halves(dq * sin_ref[...])).astype(bf16)
    first = lax.rem(pl.program_id(0), AH // KVH // 2) == 0

    @pl.when(first)
    def _():
        dbefore_ref[...] = dbefore
        down_ref[...] = down

    @pl.when(jnp.logical_not(first))
    def _():
        dbefore_ref[...] += dbefore
        down_ref[...] += down


def times(rows_in, blocks, outs, finish, extras=(), specs=(), out_specs=None, deps=()):
    rows, depth = rows_in.shape
    groups, _, width = blocks[0].shape
    tile = width
    count = len(blocks)
    tile_spec = spec((rows, tile), lambda i: (0, i))

    def kernel(rows_ref, *refs):
        weight = jnp.concatenate([ref[0] for ref in refs[:count]], axis=0)
        finish(dot(rows_ref[...], weight, NN), *refs[count:])

    return call(
        kernel,
        (groups,),
        [spec((rows, depth), lambda i: (0, 0))]
        + [spec((1, b.shape[1], tile), lambda i: (i, 0, 0)) for b in blocks]
        + list(specs),
        out_specs or [tile_spec] * len(outs),
        outs,
        flops=2 * rows * depth * width * groups,
        moved=depth * width * groups * 2 + rows * width * groups * 4,
        deps=deps,
    )(rows_in, *blocks, *extras)


def times_transposed(lefts, blocks, outs, finish, extras=(), deps=()):
    rows = lefts[0].shape[0]
    groups, _, width = blocks[0].shape
    count = len(blocks)
    depth = sum(b.shape[1] for b in blocks)
    whole = lambda item: spec(item.shape, lambda i: (0, 0))

    def kernel(*refs):
        left = [ref[...] for ref in refs[: len(lefts)]]
        left = jnp.concatenate(left, axis=1) if len(left) > 1 else left[0]
        refs = refs[len(lefts) :]
        weight = jnp.concatenate([ref[0] for ref in refs[:count]], axis=0)
        part = dot(left, weight, NT)
        total = refs[-1]
        step = pl.program_id(0)

        @pl.when(step == 0)
        def _():
            total[...] = part

        @pl.when(step > 0)
        def _():
            total[...] += part

        @pl.when(step == pl.num_programs(0) - 1)
        def _():
            finish(total[...], *refs[count:-1])

    return call(
        kernel,
        (groups,),
        [spec((rows, item.shape[1] // groups), lambda i: (0, i)) for item in lefts]
        + [spec((1, b.shape[1], width), lambda i: (i, 0, 0)) for b in blocks]
        + [whole(e) for e in extras],
        [whole(o) for o in outs],
        outs,
        [pltpu.VMEM((rows, depth), f32)],
        flops=2 * rows * depth * width * groups,
        moved=depth * width * groups * 2 + rows * depth * 8,
        deps=deps,
    )(*lefts, *blocks, *extras)


def store(value, out_ref):
    out_ref[...] = value.astype(out_ref.dtype)


def add_store(value, other_ref, out_ref):
    out_ref[...] = value + other_ref[...]


def middle_finish(value, rows_ref, gain_ref, middle_ref, low_ref):
    middle = rows_ref[...] + value
    middle_ref[...] = middle
    inv = lax.rsqrt(jnp.mean(middle * middle, axis=1, keepdims=True) + epsilon)
    low_ref[...] = (middle * inv * gain_ref[...]).astype(bf16)


def unit_finish(value, hidden_ref, by_gate_ref, by_up_ref):
    half = value.shape[1] // 2
    gate = value[:, :half]
    up = value[:, half:]
    sig = sigmoid(gate)
    silu = gate * sig
    hidden_ref[...] = (silu * up).astype(bf16)
    by_gate_ref[...] = (up * sig * (1.0 + gate * (1.0 - sig))).astype(bf16)
    by_up_ref[...] = silu.astype(bf16)


def unit_back_finish(value, by_gate_ref, by_up_ref, out_ref):
    half = value.shape[1]
    out_ref[:, :half] = (value * by_gate_ref[...].astype(f32)).astype(bf16)
    out_ref[:, half:] = (value * by_up_ref[...].astype(f32)).astype(bf16)


def middle_back_finish(value, middle_ref, cot_ref, gain_ref, grad_ref, low_ref, dgain_ref):
    middle = middle_ref[...]
    inv = lax.rsqrt(jnp.mean(middle * middle, axis=1, keepdims=True) + epsilon)
    normed = middle * inv
    dgain_ref[...] = jnp.sum(value * normed, axis=0, keepdims=True)
    scaled = value * gain_ref[...]
    cross = jnp.mean(scaled * normed, axis=1, keepdims=True)
    grad = cot_ref[...].astype(f32) + inv * (scaled - normed * cross)
    grad_ref[...] = grad
    low_ref[...] = grad.astype(bf16)


def partner(value, bit):
    count = lax.axis_size("dp")
    return lax.ppermute(value, "dp", [(i, i ^ (1 << bit)) for i in range(count)])


def high_bits():
    return list(range(1, lax.axis_size("dp").bit_length() - 1))


def put_rows(out_ref, parts):
    if parts[0].shape[0] % 16:
        parts = [jnp.concatenate([p.astype(f32) for p in parts], axis=0).astype(bf16)]
    at = 0
    for p in parts:
        out_ref[0, at : at + p.shape[0], :] = p
        at += p.shape[0]


def cut_pieces(gathered, ranges, deps=()):
    groups, rows, width = gathered.shape
    half = rows // 2

    def kernel(in_ref, *out_refs):
        for i, (start, stop) in enumerate(ranges):
            part = in_ref[0, :, start:stop]
            if half % 16:
                part = part.astype(f32)
            out_refs[2 * i][0] = part[:half].astype(bf16)
            out_refs[2 * i + 1][0] = part[half:].astype(bf16)

    sizes = [stop - start for start, stop in ranges for _ in range(2)]
    outs = call(
        kernel,
        (groups,),
        [spec((1, rows, width), lambda t: (t, 0, 0))],
        [spec((1, half, w), lambda t: (t, 0, 0)) for w in sizes],
        [shape((groups, half, w), bf16) for w in sizes],
        moved=groups * rows * width * 4,
        deps=deps,
    )(gathered)
    return [(outs[2 * i], outs[2 * i + 1]) for i in range(len(ranges))]


def spread_send(held, step):
    bits = high_bits()
    return partner(held[0], bits[step]), partner(held[1], bits[-1 - step])


def join_all(items, deps=()):
    groups = items[0][0][0].shape[0]
    args, in_specs, out_specs, outs, moved = [], [], [], [], 0
    for held, got, last in items:
        _, rows, width = held[0].shape
        args += [held[0], got[0], held[1], got[1]]
        in_specs += [spec((1, rows, width), lambda t: (t, 0, 0))] * 4
        size = 4 if last else 2
        number = 1 if last else 2
        out_specs += [spec((1, size * rows, width), lambda t: (t, 0, 0))] * number
        outs += [shape((groups, size * rows, width), bf16)] * number
        moved += groups * rows * width * 16

    def kernel(*refs):
        out_refs = list(refs[len(args) :])
        for i, (_, _, last) in enumerate(items):
            a_ref, b_ref, c_ref, d_ref = refs[4 * i : 4 * i + 4]
            upper = [a_ref[0], b_ref[0]]
            lower = [c_ref[0], d_ref[0]]
            if last:
                put_rows(out_refs.pop(0), upper + lower)
            else:
                put_rows(out_refs.pop(0), upper)
                put_rows(out_refs.pop(0), lower)

    out = list(
        call(kernel, (groups,), in_specs, out_specs, outs, moved=moved, deps=deps)(*args)
    )
    return [[out.pop(0)] if last else [out.pop(0), out.pop(0)] for _, _, last in items]


def join(held, got, deps=(), last=False):
    return join_all([(held, got, last)], deps)[0]


def spread_rest(held, got, first, deps=()):
    steps = len(high_bits())
    for i in range(first, steps):
        held = join(held, got, deps, i + 1 == steps)
        if i + 1 < steps:
            got = spread_send(held, i + 1)
    return held


def spread_end(held):
    return held[0], partner(held[0], 0)


def route_bits(route):
    return high_bits()[::-1] if route else high_bits()


def send_one(held, route, step):
    return partner(held, route_bits(route)[step])


def join_one(held, got, route, step, deps=()):
    groups, rows, width = held.shape
    bits = route_bits(route)
    masks = [(0, 0), (0, 1)]
    for bit in bits[: step + 1]:
        masks = masks + [(m | (1 << bit), p) for m, p in masks]
    places = list(range(len(masks)))
    if step + 1 == len(bits):
        goal = block_masks()[: len(masks)]
        places = [masks.index(m) for m in goal]
    size = 2 * rows // len(masks)

    def kernel(a_ref, b_ref, out_ref):
        if step + 1 < len(bits):
            put_rows(out_ref, [a_ref[0], b_ref[0]])
            return
        parts = []
        for place in places:
            ref, at = (a_ref, place * size) if place * size < rows else (b_ref, place * size - rows)
            parts.append(ref[0, at : at + size, :])
        put_rows(out_ref, parts)

    one = spec((1, rows, width), lambda t: (t, 0, 0))
    return call(
        kernel,
        (groups,),
        [one] * 2,
        spec((1, 2 * rows, width), lambda t: (t, 0, 0)),
        shape((groups, 2 * rows, width), bf16),
        moved=groups * rows * width * 8,
        deps=deps,
    )(held, got)


def rest_one(held, got, route, first, deps=()):
    steps = len(high_bits())
    for i in range(first, steps):
        held = join_one(held, got, route, i, deps)
        if i + 1 < steps:
            got = send_one(held, route, i + 1)
    return held


def slice_one(gathered, start, stop, deps=()):
    groups, rows, width = gathered.shape

    def kernel(in_ref, out_ref):
        out_ref[0] = in_ref[0, :, start:stop]

    return call(
        kernel,
        (groups,),
        [spec((1, rows, width), lambda t: (t, 0, 0))],
        spec((1, rows, stop - start), lambda t: (t, 0, 0)),
        shape((groups, rows, stop - start), bf16),
        moved=groups * rows * width * 4,
        deps=deps,
    )(gathered)


def tile_of(width):
    return next(t for t in (1024, 768, 512, 256, 128) if width % t == 0)


def collect_send(left, right, deps=()):
    rows, depth = left.shape
    near = depth // 2
    width = right.shape[1]
    tile = tile_of(width)

    def kernel(left_ref, right_ref, out_ref):
        out_ref[...] = dot(left_ref[...], right_ref[...], TN).astype(bf16)

    send = call(
        kernel,
        (width // tile,),
        [spec((rows, near), lambda i: (0, 1)), spec((rows, tile), lambda i: (0, i))],
        spec((near, tile), lambda i: (0, i)),
        shape((near, width), bf16),
        flops=2 * rows * near * width,
        moved=(rows + near) * width * 2,
        deps=deps,
    )(left, right)
    return send, partner(send, 0)


def collect_keep(left, right, got, deps=(), route=None):
    rows, depth = left.shape
    near = depth // 2
    quarter = near // 4
    if route is not None:
        masks, bit = route_masks(route, 0)
        lists = split_masks(masks, bit)
    else:
        lists = [[2 * i, 2 * i + 1] for i in range(4)]
    size = near // sum(len(x) for x in lists) if route is not None else quarter // 2
    width = right.shape[1]
    tile = tile_of(width)

    def kernel(left_ref, right_ref, got_ref, *out_refs):
        total = dot(left_ref[...], right_ref[...], TN) + got_ref[...].astype(f32)
        for places, out_ref in zip(lists, out_refs):
            out_ref[...] = pick_rows(total, places, size).astype(bf16)

    high = near // len(lists)
    out = spec((high, tile), lambda i: (0, i))
    return call(
        kernel,
        (width // tile,),
        [
            spec((rows, near), lambda i: (0, 0)),
            spec((rows, tile), lambda i: (0, i)),
            spec((near, tile), lambda i: (0, i)),
        ],
        [out] * len(lists),
        [shape((high, width), bf16)] * len(lists),
        flops=2 * rows * near * width,
        moved=(rows + 2 * near) * width * 2,
        deps=deps,
    )(left, right, got)


def pick_rows(value, places, size):
    parts, at = [], 0
    while at < len(places):
        end = at + 1
        while end < len(places) and places[end] == places[end - 1] + 1:
            end += 1
        parts.append(value[places[at] * size : (places[end - 1] + 1) * size])
        at = end
    return jnp.concatenate(parts, axis=0) if len(parts) > 1 else parts[0]


def route_masks(route, step):
    bits = route_bits(route)[::-1]
    masks = block_masks()[: 2 << len(bits)]
    for bit in bits[:step]:
        masks = [m for m in masks if not m[0] >> bit & 1]
    return masks, bits[step] if step < len(bits) else None


def split_masks(masks, bit):
    return [
        [i for i, m in enumerate(masks) if (m[0] >> bit & 1) == side] for side in range(2)
    ]


def move_one(parts, route, step):
    return partner(parts[1], route_bits(route)[::-1][step])


def add_one(parts, got, route, step, deps=()):
    rows, width = parts[0].shape
    half = rows // 2
    tile = tile_of(width)
    masks, bit = route_masks(route, step + 1)
    lists = split_masks(masks, bit)
    size = rows // len(masks)

    def kernel(a_ref, b_ref, *out_refs):
        total = a_ref[...].astype(f32) + b_ref[...].astype(f32)
        for places, out_ref in zip(lists, out_refs):
            out_ref[...] = pick_rows(total, places, size).astype(bf16)

    block = spec((rows, tile), lambda i: (0, i))
    return call(
        kernel,
        (width // tile,),
        [block] * 2,
        [spec((half, tile), lambda i: (0, i))] * 2,
        [shape((half, width), bf16)] * 2,
        moved=rows * width * 6,
        deps=deps,
    )(parts[0], got)


def collect_move(parts, step):
    bits = high_bits()
    return partner(parts[1], bits[-1 - step]), partner(parts[3], bits[step])


def collect_add(parts, got, deps=()):
    rows, width = parts[0].shape
    half = rows // 2
    tile = tile_of(width)

    def kernel(a_ref, b_ref, c_ref, d_ref, *out_refs):
        for i, (own, other) in enumerate(((a_ref, b_ref), (c_ref, d_ref))):
            total = own[...].astype(f32) + other[...].astype(f32)
            out_refs[2 * i][...] = total[:half].astype(bf16)
            out_refs[2 * i + 1][...] = total[half:].astype(bf16)

    block = spec((rows, tile), lambda i: (0, i))
    return call(
        kernel,
        (width // tile,),
        [block] * 4,
        [spec((half, tile), lambda i: (0, i))] * 4,
        [shape((half, width), bf16)] * 4,
        moved=rows * width * 12,
        deps=deps,
    )(parts[0], got[0], parts[2], got[1])


def collect_end(pairs, deps=()):
    groups = lax.axis_size("tensor")
    args, in_specs, widths, counts = [], [], [], []
    for parts, got in pairs:
        width = parts[0].shape[1] // groups
        widths.append(width)
        both = len(parts) == 4
        add = [parts[0], got[0], parts[2], got[1]] if both else [parts[0], got]
        counts.append(len(add))
        args += add
        in_specs += [spec((parts[0].shape[0], width), lambda t: (0, t))] * len(add)
        rows = parts[0].shape[0] // (1 if both else 2)

    def kernel(*refs):
        at = first = 0
        for width, count in zip(widths, counts):
            values = [ref[...].astype(f32) for ref in refs[first : first + count]]
            sums = [values[i] + values[i + 1] for i in range(0, count, 2)]
            out = jnp.concatenate(sums, axis=0) if len(sums) > 1 else sums[0]
            refs[-1][0, :, at : at + width] = out.astype(bf16)
            at += width
            first += count

    total = sum(widths)
    return call(
        kernel,
        (groups,),
        in_specs,
        spec((1, 2 * rows, total), lambda t: (t, 0, 0)),
        shape((groups, 2 * rows, total), bf16),
        moved=groups * rows * total * 12,
        deps=deps,
    )(*args)


def block_masks():
    bits = high_bits()
    count = 1 << len(bits)
    masks = []
    for core in range(2):
        for part in range(2):
            for j in range(count):
                order = bits[::-1] if part else bits
                mask = sum(((j >> i) & 1) << bit for i, bit in enumerate(order))
                masks.append((mask | core, part))
    return masks


def take_blocks(value, sources):
    width = value.shape[-1] // len(sources)
    axis = value.ndim - 1
    return jnp.concatenate(
        [lax.dynamic_slice_in_dim(value, s * width, width, axis) for s in sources], axis=axis
    )


def permute_features(value):
    me = lax.axis_index("dp")
    return take_blocks(value, [(me ^ mask) * 2 + part for mask, part in block_masks()])


def restore_features(value):
    me = lax.axis_index("dp")
    masks = block_masks()
    count = lax.axis_size("dp")
    table = jnp.array(
        [[masks.index((m, part)) for part in range(2)] for m in range(count)], jnp.int32
    )
    return take_blocks(
        value, [table[me ^ block, part] for block in range(count) for part in range(2)]
    )


def restore_all(values, deps=()):
    count = lax.axis_size("dp")
    if values[0].shape[1] // count != 128:
        return [restore_features(v) for v in values]
    masks = block_masks()
    places = [[masks.index((m, part)) for part in range(2)] for m in range(count)]
    rows = jnp.array([[p[0] // 2, p[0] % 2, p[1] // 2, p[1] % 2] for p in places], jnp.int32)
    table = rows[lax.axis_index("dp") ^ jnp.arange(count, dtype=jnp.int32)].reshape(-1)
    late = jax.tree.leaves(deps)
    number = len(values)

    def kernel(table_ref, *refs):
        i = pl.program_id(0)
        out_refs = refs[2 * number + len(late) :]
        for n in range(number):
            front, back = refs[2 * n][...], refs[2 * n + 1][...]
            front = jnp.where(table_ref[4 * i + 1] > 0, pltpu.roll(front, 64, 1), front)
            back = jnp.where(table_ref[4 * i + 3] > 0, back, pltpu.roll(back, 64, 1))
            lane = lax.broadcasted_iota(jnp.int32, front.shape, 1)
            out_refs[n][...] = jnp.where(lane < 64, front, back)

    in_specs = []
    for v in values:
        for at in (0, 2):
            in_specs.append(spec((v.shape[0], 128), lambda i, t, at=at: (0, t[4 * i + at])))
    in_specs += [pl.BlockSpec(memory_space=pl.ANY)] * len(late)
    return pl.pallas_call(
        kernel,
        grid_spec=pltpu.PrefetchScalarGridSpec(
            num_scalar_prefetch=1,
            grid=(count,),
            in_specs=in_specs,
            out_specs=[spec((v.shape[0], 128), lambda i, t: (0, i)) for v in values],
        ),
        out_shape=[shape(v.shape, v.dtype) for v in values],
        compiler_params=pltpu.CompilerParams(vmem_limit_bytes=VMEM_BYTES),
        cost_estimate=pl.CostEstimate(flops=1, bytes_accessed=1, transcendentals=0),
    )(table, *[v for v in values for _ in range(2)], *late)


def sum_all(value):
    for axis in ("dp", "tensor"):
        count = lax.axis_size(axis)
        for bit in range(count.bit_length() - 1):
            value = value + lax.ppermute(value, axis, [(i, i ^ (1 << bit)) for i in range(count)])
    return value


def norm_of(rows):
    inv = lax.rsqrt(jnp.mean(rows * rows, axis=-1, keepdims=True) + epsilon)
    return rows * inv, inv


def norm_back(grad, gain, normed, inv):
    scaled = grad * gain
    return inv * (scaled - normed * jnp.mean(scaled * normed, axis=-1, keepdims=True))


def over_tensor(piece):
    return lax.all_gather(piece, "tensor", axis=0)


def shards(
    residual,
    mixer_in,
    step_in,
    shared_in,
    query_in,
    keyval_in,
    mixer_proj,
    attn_proj,
    gate_up,
    down_proj,
    norm_gain,
    mlp_gain,
    conv_filter,
    decay_log,
    skip_gain,
    step_bias,
    gated_gain,
    cotangent,
):
    tensor_count = lax.axis_size("tensor")
    rows, model = residual.shape
    depth = mixer_in.shape[0]
    ssm = conv_filter.shape[1] - 2 * NS
    heads = ssm // PH
    groups = heads // GROUP
    chunks = rows // CHUNK
    span = LEN // rows
    part = lax.axis_index("tensor") % span
    onward = [(i, i + 1) for i in range(tensor_count) if i % span != span - 1]
    backward = [(j, i) for i, j in onward]
    hidden_w = gate_up.shape[2]
    gate_w = mixer_in.shape[2]
    query_w = query_in.shape[1]
    shared_w = shared_in.shape[1]
    attn_w = AH * HD
    ff = hidden_w * tensor_count
    steps = len(high_bits())

    def finish_dp(parts, got, deps):
        for i in range(2, steps):
            parts = collect_add(parts, got, deps)
            got = collect_move(parts, i)
        return collect_end([(parts, got)], deps)

    def finish_tensor(joined):
        total = lax.psum_scatter(joined, "tensor", scatter_dimension=0, tiled=False)
        return total.astype(f32)

    before_rows = lax.ppermute(residual[rows - HALO :], "tensor", onward)
    ext_low = permute_features(jnp.concatenate([before_rows, residual], axis=0))
    cot = permute_features(cotangent)
    gain_first = permute_features(norm_gain)
    gain_second = permute_features(mlp_gain)
    ext_normed, ext_inv = norm_of(ext_low.astype(f32))
    ext_in = (ext_normed * gain_first).astype(bf16)
    normed_first = ext_normed[HALO:]
    inv_first = ext_inv[HALO:]
    normed_in = ext_in[HALO:]
    group_rows = ext_low[HALO:].astype(f32)
    wide_f32 = shape((rows, model), f32)
    wide_low = shape((rows, model), bf16)
    second_row = gain_second[None, :]

    half = HD // 2
    frequency = rope_base ** (-2.0 * jnp.arange(half, dtype=f32) / HD)
    place = (part * rows + jnp.arange(rows, dtype=jnp.int32)).astype(f32)
    angles = place[:, None] * frequency[None, :]
    cosine = jnp.cos(angles)
    sine = jnp.sin(angles)
    ones = jnp.ones((rows, HD), f32)
    cos_q = jnp.concatenate([cosine] * 4, axis=1)
    sin_q = jnp.concatenate([-sine, sine] * 2, axis=1)
    cos_kv = jnp.concatenate([cosine, cosine, ones], axis=1)
    sin_kv = jnp.concatenate([-sine, sine, 0.0 * ones], axis=1)

    def padded(parts):
        width = sum(p.shape[1] for p in parts)
        return jnp.concatenate(parts + [jnp.zeros((depth, -width % 128), bf16)], axis=1)

    val_in = padded([mixer_in[:, 1], shared_in, step_in])
    gate_in = padded([mixer_in[:, 0], query_in, keyval_in])
    val_w = val_in.shape[1]
    out_in = jnp.concatenate([mixer_proj, attn_proj], axis=0).T
    out_w = out_in.shape[1]
    in_z = over_tensor(jnp.concatenate([val_in, gate_in], axis=1))
    back_z = over_tensor(jnp.concatenate([out_in, down_proj.T], axis=1))
    tables = (cos_q, sin_q, cos_kv, sin_kv)
    (val_held,) = cut_pieces(in_z, [(0, val_w)], (ext_in, tables, cot, group_rows))
    val_got = spread_send(val_held, 0)
    val_held = join(val_held, val_got)
    val_got = spread_send(val_held, 1)
    (gate_held,) = cut_pieces(in_z, [(val_w, in_z.shape[2])], val_held)
    gate_got = spread_send(gate_held, 0)
    for i in range(1, steps - 1):
        val_held = join(val_held, val_got, gate_held)
        val_got = spread_send(val_held, i + 1)
    val_held, gate_held = join_all(
        [(val_held, val_got, True), (gate_held, gate_got, False)], gate_held
    )
    in_b = spread_end(val_held)
    gate_got = spread_send(gate_held, 1)
    ff_in = slice_one(gate_up.reshape(1, depth, 2 * hidden_w), 0, 2 * hidden_w, val_held)
    ff_z = over_tensor(ff_in[0])

    (out_held,) = cut_pieces(back_z, [(0, out_w)], gate_held)
    out_got = spread_send(out_held, 0)
    (proj_b,) = times(
        ext_in,
        in_b,
        [shape((rows + HALO, val_w * tensor_count), f32)],
        store,
        deps=(gate_held, out_held),
    )
    for i in range(1, steps - 1):
        gate_held = join(gate_held, gate_got, proj_b)
        gate_got = spread_send(gate_held, i + 1)
    gate_held, out_held = join_all(
        [(gate_held, gate_got, True), (out_held, out_got, False)], proj_b
    )
    in_a = spread_end(gate_held)
    out_got = spread_send(out_held, 1)

    ext = rows + HALO
    whole = lambda *dims: spec(dims, lambda i: (0,) * len(dims))
    tail = lambda count, t: (lambda i: (0, count * t + count - 1))
    per_val = val_w // 128
    bias_row = jnp.pad(step_bias, (0, 128 - heads))[None, :]
    rate_row = jnp.pad(jnp.exp(decay_log), (0, 128 - heads))[None, :]
    shr, step_lin, cols, cum_rows, grow = call(
        prepare_kernel,
        (1,),
        [spec((ext, 128), tail(per_val, t)) for t in range(4)] + [whole(1, 128)] * 2,
        [
            whole(ext, 2 * NS),
            whole(rows, 128),
            whole(groups, rows, 2 * SLOT),
            whole(groups, SLOT, rows),
            whole(rows, 128),
        ],
        [
            shape((ext, 2 * NS), f32),
            shape((rows, 128), f32),
            shape((groups, rows, 2 * SLOT), f32),
            shape((groups, SLOT, rows), f32),
            shape((rows, 128), f32),
        ],
        moved=rows * 128 * 40,
    )(proj_b, proj_b, proj_b, proj_b, bias_row, rate_row)
    skip_lanes = jnp.repeat(skip_gain, PH)[None, :]

    val_spec = spec((ext, val_w), lambda g: (0, g))
    shr_spec = whole(ext, 2 * NS)
    tapv_spec = spec((KC, GW), lambda g: (0, g))
    taps_spec = spec((KC, 2 * NS), lambda g: (0, ssm // (2 * NS)))
    col_spec = spec((1, rows, 2 * SLOT), lambda g: (g, 0, 0))
    row_spec = spec((1, SLOT, rows), lambda g: (g, 0, 0))
    lane_spec = spec((1, GW), lambda g: (0, g))
    bc_spec = whole(rows, 2 * NS)
    grp_spec = spec((rows, GW), lambda g: (0, g))
    state_spec = spec((NS, GW), lambda g: (0, g))
    y_local, state_local, bc_act = call(
        mixer_kernel,
        (groups,),
        [val_spec, shr_spec, tapv_spec, taps_spec, col_spec, row_spec, lane_spec],
        [grp_spec, state_spec, bc_spec],
        [shape((rows, ssm), f32), shape((NS, ssm), bf16), shape((rows, 2 * NS), bf16)],
        [pltpu.VMEM((chunks, CHUNK, CHUNK), f32)],
        flops=2 * rows * ssm * 512,
        moved=rows * ssm * 8,
        deps=(gate_held, out_held),
    )(proj_b, shr, conv_filter, conv_filter, cols, cum_rows, skip_lanes)
    entering = lax.ppermute(state_local, "tensor", onward)
    per_gate = gate_held[0].shape[2] // 128
    out_held = spread_rest(out_held, out_got, 1, y_local)
    out_full = spread_end(out_held)
    (ff_held,) = cut_pieces(ff_z, [(0, 2 * hidden_w)], out_held)
    ff_got = spread_send(ff_held, 0)
    (proj_a,) = times(
        normed_in,
        in_a,
        [shape((rows, per_gate * 128 * tensor_count), f32)],
        store,
        deps=(out_held, ff_held),
    )
    ff_held = join(ff_held, ff_got, (proj_a, entering))
    ff_got = spread_send(ff_held, 1)

    kv_w = 2 * KVH * HD
    own_kv = call(
        rotate_kernel,
        (1,),
        [spec((rows, 128), tail(per_gate, t)) for t in range(4)] + [whole(rows, 2 * HD)] * 2,
        whole(rows, kv_w),
        shape((rows, kv_w), bf16),
        moved=rows * kv_w * 12,
    )(proj_a, proj_a, proj_a, proj_a, cos_kv, sin_kv)
    before_kv = lax.ppermute(own_kv, "tensor", onward)
    part_arg = part.astype(jnp.int32).reshape(1)
    pairs = AH // 2
    per_kv = AH // KVH // 2
    smem = pl.BlockSpec(memory_space=pltpu.SMEM)
    q_spec = spec((rows, 2 * HD), lambda i: (0, per_gate * i + GW // 128))
    table_spec = spec((rows, 2 * HD), lambda i: (0, 0))
    kv_spec = spec((rows, 2 * HD), lambda i: (0, i // per_kv))
    pair_spec = spec((rows, 2 * HD), lambda i: (0, i))
    attn_heads = call(
        attend_kernel,
        (pairs,),
        [smem, q_spec, table_spec, table_spec, kv_spec, kv_spec],
        pair_spec,
        shape((rows, attn_w), bf16),
        flops=2 * AH * rows * LEN * 256,
        moved=rows * attn_w * 8,
        deps=ff_held,
    )(part_arg, proj_a, cos_q, sin_q, before_kv, own_kv)

    (down_held,) = cut_pieces(back_z, [(out_w, back_z.shape[2])], (attn_heads, out_full))
    down_got = spread_send(down_held, 0)
    block_rows = CHUNK
    wide = spec((block_rows, ssm), lambda i: (i, 0))
    gate_block = spec((block_rows, proj_a.shape[1]), lambda i: (i, 0))
    heads_block = spec((block_rows, ssm + attn_w), lambda i: (i, 0))
    attn_block = spec((block_rows, attn_w), lambda i: (i, 0))
    bc_block = spec((block_rows, 2 * NS), lambda i: (i, 0))
    grow_block = spec((block_rows, 128), lambda i: (i, 0))
    state_whole = whole(NS, ssm)
    gain_whole = whole(1, ssm)
    gated_row = gated_gain[None, :]
    scanned, heads_all = call(
        finish_kernel,
        (rows // block_rows,),
        [wide, gate_block, bc_block, grow_block, state_whole, gain_whole, attn_block],
        [wide, heads_block],
        [shape((rows, ssm), f32), shape((rows, ssm + attn_w), bf16)],
        flops=2 * rows * ssm * NS,
        moved=rows * ssm * 14,
        deps=down_held,
    )(y_local, proj_a, bc_act, grow, entering, gated_row, attn_heads)

    ff_held = spread_rest(ff_held, ff_got, 1, heads_all)
    ff_full = spread_end(ff_held)
    middle, mlp_rows = times_transposed(
        [heads_all],
        out_full,
        [wide_f32, wide_low],
        middle_finish,
        (group_rows, second_row),
        deps=ff_held,
    )
    down_held = join(down_held, down_got, middle)
    down_got = spread_send(down_held, 1)
    unit = spec((rows, hidden_w), lambda i: (0, i))
    ff_low = shape((rows, ff), bf16)
    hidden, by_gate, by_up = times(
        mlp_rows, ff_full, [ff_low] * 3, unit_finish, out_specs=[unit] * 3, deps=down_held
    )
    down_held = spread_rest(down_held, down_got, 1, hidden)
    down_full = spread_end(down_held)
    down_send, down_got = collect_send(cot, hidden, down_held)
    (both_grad,) = times(
        cot,
        down_full,
        [shape((rows, 2 * ff), bf16)],
        unit_back_finish,
        (by_gate, by_up),
        (unit, unit),
        [spec((rows, 2 * hidden_w), lambda i: (0, i))],
        deps=down_send,
    )
    down_sum = collect_keep(cot, hidden, down_got, both_grad)
    down_got = collect_move(down_sum, 0)
    ff_send, ff_got = collect_send(mlp_rows, both_grad, down_sum)
    middle_grad, branch_grad, mlp_gain_part = times_transposed(
        [both_grad],
        ff_full,
        [wide_f32, wide_low, shape((1, model), f32)],
        middle_back_finish,
        (middle, cot, second_row),
        deps=(ff_send, down_sum),
    )

    down_sum = collect_add(down_sum, down_got, branch_grad)
    down_got = collect_move(down_sum, 1)
    (heads_grad,) = times(
        branch_grad, out_full, [shape((rows, ssm + attn_w), f32)], store, deps=down_sum
    )
    out_send, out_got = collect_send(branch_grad, heads_all, heads_grad)
    ff_sum = collect_keep(mlp_rows, both_grad, ff_got, out_send)
    ff_got = collect_move(ff_sum, 0)
    dgate, dscan, gated_gain_part, dstate_local = call(
        ungate_kernel,
        (rows // block_rows,),
        [heads_block, wide, gate_block, bc_block, grow_block, gain_whole],
        [wide, wide, gain_whole, state_whole],
        [
            shape((rows, ssm), bf16),
            shape((rows, ssm), f32),
            shape((1, ssm), f32),
            shape((NS, ssm), f32),
        ],
        flops=2 * rows * ssm * NS,
        moved=rows * ssm * 18,
        deps=(out_send, ff_sum),
    )(heads_grad, scanned, proj_a, bc_act, grow, gated_row)
    leaving_grad = lax.ppermute(dstate_local.astype(bf16), "tensor", backward)
    down_z = finish_dp(down_sum, down_got, dgate)
    down_t = finish_tensor(down_z)
    gate_send, gate_got = collect_send(normed_in, dgate, down_z)
    out_sum = collect_keep(branch_grad, heads_all, out_got, gate_send, 0)
    out_got = move_one(out_sum, 0, 0)
    (output,) = times_transposed(
        [hidden], down_full, [wide_f32], add_store, (middle,), deps=out_sum
    )
    gate_sum = collect_keep(normed_in, dgate, gate_got, (output, leaving_grad), 1)
    gate_got = move_one(gate_sum, 1, 0)
    (output,) = restore_all([output], gate_sum)

    dout_spec = spec((rows, 2 * HD), lambda i: (0, 4 * i + 3))
    qk_low, before_grad, own_grad = call(
        unattend_kernel,
        (pairs,),
        [smem, q_spec, table_spec, table_spec, kv_spec, kv_spec, dout_spec],
        [spec((rows, 2 * HD), lambda i: (0, 2 * i)), kv_spec, kv_spec],
        [shape((rows, 4 * HD * pairs), bf16), shape((rows, kv_w), f32), shape((rows, kv_w), f32)],
        flops=2 * AH * rows * LEN * 640,
        moved=rows * attn_w * 16,
        deps=(out_sum, gate_sum, output),
    )(part_arg, proj_a, cos_q, sin_q, before_kv, own_kv, heads_grad)
    late_grad = lax.ppermute(before_grad.astype(bf16), "tensor", backward)

    ff_sum = collect_add(ff_sum, ff_got, before_grad)
    ff_got = collect_move(ff_sum, 1)
    out_sum = add_one(out_sum, out_got, 0, 0, ff_sum)
    out_got = move_one(out_sum, 0, 1)
    gate_sum = add_one(gate_sum, gate_got, 1, 0, out_sum)
    gate_got = move_one(gate_sum, 1, 1)
    half_spec = spec((rows, 2 * HD), lambda t: (0, t // 2))
    qk_low = call(
        unrotate_kernel,
        (tensor_count,),
        [pl.BlockSpec(memory_space=pl.ANY), half_spec, half_spec] + [whole(rows, 2 * HD)] * 2,
        spec((rows, 2 * HD), lambda t: (0, 2 * t + 1)),
        shape(qk_low.shape, bf16),
        moved=rows * kv_w * 16,
        aliases={0: 0},
        deps=(ff_sum, out_sum, gate_sum),
    )(qk_low, own_grad, late_grad, cos_kv, sin_kv)

    qk_send, qk_got = collect_send(normed_in, qk_low)

    low_v, dshr, dcols, drows, dlast, dtapv, dtaps, dskip = call(
        unmix_kernel,
        (groups,),
        [
            val_spec, shr_spec, tapv_spec, taps_spec, col_spec, row_spec, lane_spec,
            bc_spec, grp_spec, state_spec, state_spec,
        ],
        [
            val_spec,
            shr_spec,
            spec((1, rows, 128), lambda g: (g, 0, 0)),
            row_spec,
            spec((chunks, GW), lambda g: (0, g)),
            tapv_spec,
            whole(KC, 2 * NS),
            lane_spec,
        ],
        [
            shape((ext, val_w * tensor_count), bf16),
            shape((ext, 2 * NS), f32),
            shape((groups, rows, 128), f32),
            shape((groups, SLOT, rows), f32),
            shape((chunks, ssm), f32),
            shape((KC, ssm), f32),
            shape((KC, 2 * NS), f32),
            shape((1, ssm), f32),
        ],
        [
            pltpu.VMEM((chunks, CHUNK, CHUNK), f32),
            pltpu.VMEM((rows, 2 * NS), f32),
            pltpu.VMEM((chunks, CHUNK, CHUNK), f32),
            pltpu.VMEM((rows, GW), f32),
            pltpu.VMEM((chunks, NS, GW), f32),
            pltpu.VMEM((rows + HALO + 16, GW), f32),
        ],
        flops=2 * rows * ssm * 1280,
        moved=rows * ssm * 12,
        deps=(ff_sum, out_sum, gate_sum, qk_send),
    )(
        proj_b, shr, conv_filter, conv_filter, cols, cum_rows, skip_lanes,
        bc_act, dscan, entering, leaving_grad,
    )
    def rest_dp(parts, got, deps=()):
        for i in range(2, steps):
            parts = collect_add(parts, got, deps)
            got = collect_move(parts, i)
        return parts, got

    def rest_one_way(parts, got, route, deps):
        for i in range(2, steps):
            parts = add_one(parts, got, route, i - 1, deps)
            got = move_one(parts, route, i)
        return parts, got

    ends = collect_end(
        [
            rest_dp(ff_sum, ff_got, low_v),
            rest_one_way(out_sum, out_got, 0, low_v),
            rest_one_way(gate_sum, gate_got, 1, low_v),
        ],
        low_v,
    )
    ends_t = finish_tensor(ends)
    ff_t = ends_t[:, : 2 * hidden_w]
    out_t = ends_t[:, 2 * hidden_w : 2 * hidden_w + out_w]
    gate_t = ends_t[:, 2 * hidden_w + out_w :]
    low_v, decay_part, bias_part = call(
        settle_kernel,
        (tensor_count,),
        [
            pl.BlockSpec(memory_space=pl.ANY),
            shr_spec,
            whole(groups, rows, 128),
            whole(groups, SLOT, rows),
            whole(chunks, ssm),
            whole(rows, 128),
            whole(1, 128),
        ],
        [
            spec((ext, 128), lambda t: (0, per_val * t + per_val - 1)),
            whole(1, 128),
            whole(1, 128),
        ],
        [shape(low_v.shape, bf16), shape((1, 128), f32), shape((1, 128), f32)],
        [pltpu.VMEM((rows, 128), f32)],
        moved=rows * 128 * 60,
        aliases={0: 0},
        deps=ends,
    )(low_v, dshr, dcols, drows, dlast, step_lin, rate_row)
    qk_sum = collect_keep(normed_in, qk_low, qk_got, ends)
    qk_got = collect_move(qk_sum, 0)
    val_send, val_got = collect_send(ext_in, low_v, qk_sum)
    (grad_a,) = times_transposed([dgate, qk_low], in_a, [wide_f32], store, deps=val_send)
    val_sum = collect_keep(ext_in, low_v, val_got, grad_a)
    val_got = collect_move(val_sum, 0)
    qk_sum = collect_add(qk_sum, qk_got, val_sum)
    qk_got = collect_move(qk_sum, 1)
    (grad_b,) = times_transposed(
        [low_v], in_b, [shape((ext, model), f32)], store, deps=(val_sum, qk_sum)
    )
    val_sum = collect_add(val_sum, val_got, grad_b)
    val_got = collect_move(val_sum, 1)
    late_rows = lax.ppermute(grad_b[:HALO], "tensor", backward)
    residual_grad, gain_sums = call(
        first_back_kernel,
        (1,),
        [
            whole(rows, model), whole(ext, model), whole(HALO, model), whole(rows, model),
            whole(rows, model), whole(1, model), whole(1, model),
        ],
        [whole(rows, model), whole(8, model)],
        [wide_f32, shape((8, model), f32)],
        deps=val_sum,
    )(
        grad_a, grad_b, late_rows, ext_low[HALO:], middle_grad, gain_first[None, :], mlp_gain_part
    )
    residual_grad, gain_sums = restore_all([residual_grad, gain_sums])
    last_t = finish_tensor(collect_end([rest_dp(val_sum, val_got), rest_dp(qk_sum, qk_got)]))
    gate_up_sum = ff_t.reshape(depth, 2, hidden_w)
    val_t = last_t[:, :val_w]
    qk_t = last_t[:, val_w:]
    skip_part = dskip.reshape(heads, PH).sum(axis=-1)

    small = [
        gain_sums[0],
        gain_sums[1],
        jnp.concatenate([dtapv, dtaps], axis=1).reshape(-1),
        decay_part[0, :heads],
        skip_part,
        bias_part[0, :heads],
        gated_gain_part[0],
    ]
    sizes = [item.shape[0] for item in small]
    total = sum_all(jnp.concatenate(small))
    marks = [sum(sizes[:i]) for i in range(len(sizes) + 1)]
    sums = [total[marks[i] : marks[i + 1]] for i in range(len(sizes))]
    return (
        output,
        residual_grad,
        jnp.stack([gate_t, val_t[:, :gate_w]], axis=1),
        val_t[:, gate_w + shared_w : gate_w + shared_w + step_in.shape[1]],
        val_t[:, gate_w : gate_w + shared_w],
        qk_t[:, :query_w],
        qk_t[:, query_w : query_w + keyval_in.shape[1]],
        out_t[:, :gate_w].T,
        out_t[:, gate_w:].T,
        gate_up_sum,
        down_t.T,
        sums[0],
        sums[1],
        sums[2].reshape(conv_filter.shape),
        sums[3],
        sums[4],
        sums[5],
        sums[6],
    )


def solution(mesh):
    rows_spec = P(("dp", "tensor"), None)
    into = P("dp", "tensor")
    out_of = P("tensor", "dp")
    double = P("dp", None, "tensor")
    weights = (double, into, into, into, into, out_of, out_of, double, out_of)
    return jax.shard_map(
        shards,
        mesh=mesh,
        in_specs=(rows_spec,) + weights + (P(),) * 7 + (rows_spec,),
        out_specs=(rows_spec, rows_spec) + weights + (P(),) * 7,
        check_vma=False,
    )
```

time: 748 us -> 574 us (0.77)
  Pallas kernels: 98.1 us -> 313 us
  matrix products: 102 us -> 0 us
  local copies, waits for them, and re-layouts: 146 us -> 61.5 us
  other arithmetic: 88.2 us -> 9.71 us
  blocking collectives: 77.8 us -> 0 us
  waiting for transfers between devices: 161 us -> 99.8 us
  starting transfers between devices: 53 us -> 64.2 us
    pallas_call x8 -> x58, Pallas kernels: 98.1 us -> 313 us  [the longest x56 298 us: call(): return lambda *args: run(*args, *late)]
    ppermute x48 -> x51, waiting for transfers between devices: 128 us -> 23.9 us  [partner(): return lax.ppermute(value, 'dp', [(i, i ^ 1 << bit) for i in range(count)])]
    dot_general x34 -> x0, matrix products: 102 us -> none  [the longest x32 101 us: dot(): lax.dot_general(left, right, ((dims[:1], dims[1:]), ((), ())), preferred_...]
    concatenate x28 -> x2, other arithmetic: 56.5 us -> 1.2 us  [the longest x1 0.72 us: shards(): back_z = over_tensor(jnp.concatenate([out_in, down_proj.T], axis=1))]
    all_gather x2 -> x3, waiting for transfers between devices: 0.01 us -> 43.8 us  [over_tensor(): return lax.all_gather(piece, 'tensor', axis=0)]
    concatenate x15 -> x4, local copies, waits for them, and re-layouts: 43.9 us -> 1.84 us  [the longest x1 1.61 us: shards(): in_z = over_tensor(jnp.concatenate([val_in, gate_in], axis=1))]
    psum x1 -> x0, blocking collectives: 40 us -> none  [shards(): total = lax.psum(jnp.concatenate(small), ('dp', 'tensor'))]
    all_gather x2 -> x0, blocking collectives: 37.8 us -> none  [over_tensor(): return lax.all_gather(piece, 'tensor', axis=0)]
  transfers between devices with their start and end apart: 60 -> 68, of which waited for: 24 -> 22; matrix products, arithmetic and copies ran while one was open for 37% -> 7% of each run, Pallas kernels for 10% -> 50%
where the time goes in v2:
time: 574 us; the launch traced here: 564 us
  Pallas kernels  313 us (55%)
  waiting for transfers between devices  99.8 us (17%)
  starting transfers between devices  64.2 us (11%)
  local copies, waits for them, and re-layouts  61.5 us (11%)
  between operations  16 us (3%)
  other arithmetic  9.71 us (2%)
    pallas_call x56, Pallas kernels, call(): return lambda *args: run(*args, *late)  298 us
    all_gather x3, waiting for transfers between devices, over_tensor(): return lax.all_gather(piece, 'tensor', axis=0)  43.8 us
    ppermute x51, starting transfers between devices, partner(): return lax.ppermute(value, 'dp', [(i, i ^ 1 << bit) for i in range(count)])  41.6 us
    unnamed x233, local copies, waits for them, and re-layouts  33.9 us
    ppermute x51, waiting for transfers between devices, partner(): return lax.ppermute(value, 'dp', [(i, i ^ 1 << bit) for i in range(count)])  23.9 us
    reduce_scatter x3, waiting for transfers between devices, finish_tensor(): total = lax.psum_scatter(joined, 'tensor', scatter_dimension=0, tiled=False)  15.8 us
    pallas_call x2, Pallas kernels, restore_all(): pl.pallas_call(kernel, grid_spec=pltpu.PrefetchScalarGridSpec(num_scalar_...  14.5 us
  transfers between devices with their start and end apart: 68, of which 22 were waited for; matrix products, arithmetic and copies ran while one was open for 7% of the time, Pallas kernels for 50%

profile of v2, /device:TPU:0, one launch (start us, length us, event | category | flops | bytes accessed | tf_op | source)
XLA Modules:
  0.0 563.8 jit_solution(1593300818898709494)
XLA Ops:
  8.7 5.5 collective-permute-start
  38.0 12.6 %all-gather.8.cloned.1.call-done = bf16[512,1152]{1,0:T(8,128)(2,1)} async-done(((bf16[128,1152]{1,0:T(8,128)(2,1)}), bf16[512,1152]{1,0:T(8,128)(2,1)}) %all-gather.8.cloned.1.call-update) | async-done | bytes 1179664 | tf_op jit(solution)/shard_map/all_gather | solution.py:1161
  55.7 4.5 collective-permute-done.1.refs_1_
  70.1 13.0 %collective-permute-done.5.refs_5_ = bf16[4,64,640]{2,1,0:T(8,128)(2,1)S(1)} collective-permute-done((bf16[4,64,640]{2,1,0:T(8,128)(2,1)S(1)}, bf16[4,64,640]{2,1,0:T(8,128)(2,1)S(1)}, u32[]{:S(2)}, u32[]{:S(2)}) %collective-permute-start.5) | collective-permute-done | bytes 327712 | tf_op jit(solution)/shard_map/ppermute | solution.py:723
  90.8 28.1 %all-gather.10.cloned.1.call-done = bf16[512,1024]{0,1:T(8,128)(2,1)} async-done(((bf16[128,1024]{0,1:T(8,128)(2,1)}), bf16[512,1024]{0,1:T(8,128)(2,1)}) %all-gather.10.cloned.1.call-update) | async-done | bytes 1048592 | tf_op jit(solution)/shard_map/all_gather | solution.py:1161
  125.2 6.4 %shard_map.336.refs_0_.refs_1_.refs_2_.refs_3_.refs_8_ = f32[528,2048]{1,0:T(8,128)} custom-call(bf16[528,1024]{1,0:T(8,128)(2,1)} %fusion.2.refs_1_.refs_0_, bf16[4,512,512]{2,1,0:T(8,128)(2,1)} %get-tuple-element.126.refs_1_, bf16[4,512,512]{2,1,0:T(8,128)(2,1)} %collective-permute-done.7.refs_2_, bf16[4,128,640]{2,1,0:T(8,128)(2,1)S(1)} %copy-done.11, ...), custom_call_target="tpu_custom_call" | custom-call | flops 1 | bytes 1 | tf_op jit(solution)/shard_map/pallas_call | solution.py:54
  132.6 4.1 shard_map.338
  145.1 13.3 %shard_map.339 = (f32[512,1536]{1,0:T(8,128)}, bf16[128,1536]{1,0:T(8,128)(2,1)S(1)}, bf16[512,256]{1,0:T(8,128)(2,1)S(1)}) custom-call(f32[528,2048]{1,0:T(8,128)} %shard_map.336.refs_0_.refs_1_.refs_2_.refs_3_.refs_8_, f32[528,256]{1,0:T(8,128)} %copy-done.28, f32[4,1792]{1,0:T(4,128)S(1)} %copy-done.44, f32[4,1792]{1,0:T(4,128)S(1)} %copy-done.44, ...), custom_call_target="tpu_custom_call" | custom-call | flops 1 | bytes 1 | tf_op jit(solution)/shard_map/pallas_call | solution.py:54
  174.7 7.6 %shard_map.343.refs_0_.refs_1_.refs_2_.refs_3_.refs_4_ = f32[512,2560]{1,0:T(8,128)} custom-call(bf16[512,1024]{1,0:T(8,128)(2,1)} %slice.118.refs_0_, bf16[4,512,640]{2,1,0:T(8,128)(2,1)} %get-tuple-element.134.refs_7_.refs_1_.refs_2_, bf16[4,512,640]{2,1,0:T(8,128)(2,1)} %collective-permute-done.12.refs_2_.refs_3_, ...), custom_call_target="tpu_custom_call" | custom-call | flops 1 | bytes 1 | tf_op jit(solution)/shard_map/pallas_call | solution.py:54
  197.3 9.5 %shard_map.346.refs_1_.refs_6_ = bf16[512,512]{1,0:T(8,128)(2,1)S(1)} custom-call(s32[1]{0:T(128)} %bitcast.9.refs_0_, f32[512,2560]{1,0:T(8,128)} %shard_map.343.refs_0_.refs_1_.refs_2_.refs_3_.refs_4_, f32[512,128]{1,0:T(8,128)S(1)} %get-tuple-element.317.refs_2_, f32[512,128]{1,0:T(8,128)S(1)} %get-tuple-element.380.refs_3_, ...), custom_call_target="tpu_custom_call" | custom-call | flops 1 | bytes 1 | tf_op jit(solution)/shard_map/pallas_call | solution.py:54
  208.8 7.1 %shard_map.348 = (f32[512,1536]{1,0:T(8,128)}, bf16[512,2048]{1,0:T(8,128)(2,1)}) custom-call(f32[512,1536]{1,0:T(8,128)} %get-tuple-element.137.refs_4_.refs_0_, f32[512,2560]{1,0:T(8,128)} %shard_map.343.refs_0_.refs_1_.refs_2_.refs_3_.refs_4_, bf16[512,256]{1,0:T(8,128)(2,1)S(1)} %get-tuple-element.140.refs_2_.refs_3_.refs_7_, ...), custom_call_target="tpu_custom_call" | custom-call | flops 1 | bytes 1 | tf_op jit(solution)/shard_map/pallas_call | solution.py:54
  217.5 4.4 shard_map.349.refs_5_.refs_1_
  224.4 8.2 %shard_map.350 = (f32[512,1024]{1,0:T(8,128)}, bf16[512,1024]{1,0:T(8,128)(2,1)S(1)}) custom-call(bf16[512,2048]{1,0:T(8,128)(2,1)} %get-tuple-element.147.refs_4_.refs_0_.refs_1_, bf16[4,512,512]{2,1,0:T(8,128)(2,1)} %shard_map.340.refs_1_.refs_3_.refs_2_, bf16[4,512,512]{2,1,0:T(8,128)(2,1)} %collective-permute-done.19.refs_3_.refs_2_, ...), custom_call_target="tpu_custom_call" | custom-call | flops 1 | bytes 1 | tf_op jit(solution)/shard_map/pallas_call | solution.py:54
  237.8 9.8 %shard_map.352 = (bf16[512,2048]{1,0:T(8,128)(2,1)}, bf16[512,2048]{1,0:T(8,128)(2,1)}, bf16[512,2048]{1,0:T(8,128)(2,1)}) custom-call(bf16[512,1024]{1,0:T(8,128)(2,1)} %copy-done.5, bf16[4,512,1024]{2,1,0:T(8,128)(2,1)} %shard_map.349.refs_5_.refs_1_, bf16[4,512,1024]{2,1,0:T(8,128)(2,1)} %collective-permute-done.22.refs_2_, ...), custom_call_target="tpu_custom_call" | custom-call | flops 1 | bytes 1 | tf_op jit(solution)/shard_map/pallas_call | solution.py:54
  260.0 7.2 %shard_map.355.refs_3_.refs_1_.refs_0_ = bf16[512,4096]{1,0:T(8,128)(2,1)} custom-call(bf16[512,1024]{1,0:T(8,128)(2,1)S(1)} %copy-done.1, bf16[4,512,512]{2,1,0:T(8,128)(2,1)} %shard_map.353.refs_2_.refs_1_, bf16[4,512,512]{2,1,0:T(8,128)(2,1)} %copy-done.61, bf16[512,2048]{1,0:T(8,128)(2,1)} %get-tuple-element.153.refs_3_, ...), custom_call_target="tpu_custom_call" | custom-call | flops 1 | bytes 1 | tf_op jit(solution)/shard_map/pallas_call | solution.py:54
  272.5 6.5 %shard_map.357.refs_6_ = bf16[512,4096]{1,0:T(8,128)(2,1)} custom-call(bf16[512,1024]{1,0:T(8,128)(2,1)} %copy-done.5, bf16[512,4096]{1,0:T(8,128)(2,1)} %shard_map.355.refs_3_.refs_1_.refs_0_, bf16[128,2048]{1,0:T(8,128)(2,1)S(1)} %get-tuple-element.155.refs_2_.refs_7_.refs_0_, bf16[128,2048]{1,0:T(8,128)(2,1)S(1)} %get-tuple-element.156.refs_3_.refs_8_, ...), custom_call_target="tpu_custom_call" | custom-call | flops 1 | bytes 1 | tf_op jit(solution)/shard_map/pallas_call | solution.py:54
  280.5 12.2 %shard_map.358 = (f32[512,1024]{1,0:T(8,128)}, bf16[512,1024]{1,0:T(8,128)(2,1)}, f32[1,1024]{1,0:T(1,128)S(1)}) custom-call(bf16[512,4096]{1,0:T(8,128)(2,1)} %shard_map.355.refs_3_.refs_1_.refs_0_, bf16[4,512,1024]{2,1,0:T(8,128)(2,1)} %shard_map.349.refs_5_.refs_1_, bf16[4,512,1024]{2,1,0:T(8,128)(2,1)} %collective-permute-done.22.refs_2_, ...), custom_call_target="tpu_custom_call" | custom-call | flops 1 | bytes 1 | tf_op jit(solution)/shard_map/pallas_call | solution.py:54
  296.3 6.4 %shard_map.360.refs_2_.refs_0_.refs_6_ = f32[512,2048]{1,0:T(8,128)} custom-call(bf16[512,1024]{1,0:T(8,128)(2,1)} %get-tuple-element.159.refs_4_.refs_0_, bf16[4,512,512]{2,1,0:T(8,128)(2,1)} %shard_map.340.refs_1_.refs_3_.refs_2_, bf16[4,512,512]{2,1,0:T(8,128)(2,1)} %collective-permute-done.19.refs_3_.refs_2_, ...), custom_call_target="tpu_custom_call" | custom-call | flops 1 | bytes 1 | tf_op jit(solution)/shard_map/pallas_call | solution.py:54
  310.3 7.0 %shard_map.362 = (bf16[128,4096]{1,0:T(8,128)(2,1)S(1)}, bf16[128,4096]{1,0:T(8,128)(2,1)}, bf16[128,4096]{1,0:T(8,128)(2,1)}, bf16[128,4096]{1,0:T(8,128)(2,1)}) custom-call(bf16[512,1024]{1,0:T(8,128)(2,1)} %copy-done.5, bf16[512,4096]{1,0:T(8,128)(2,1)} %shard_map.355.refs_3_.refs_1_.refs_0_, bf16[512,4096]{1,0:T(8,128)(2,1)} %copy-done.64, ...), custom_call_target="tpu_custom_call" | custom-call | flops 1 | bytes 1 | tf_op jit(solution)/shard_map/pallas_call | solution.py:54
  318.3 9.4 %shard_map.363 = (bf16[512,1536]{1,0:T(8,128)(2,1)}, f32[512,1536]{1,0:T(8,128)}, f32[1,1536]{1,0:T(1,128)S(1)}, f32[128,1536]{1,0:T(8,128)S(1)}) custom-call(f32[512,2048]{1,0:T(8,128)} %shard_map.360.refs_2_.refs_0_.refs_6_, f32[512,1536]{1,0:T(8,128)} %get-tuple-element.164.refs_1_, f32[512,2560]{1,0:T(8,128)} %shard_map.343.refs_0_.refs_1_.refs_2_.refs_3_.refs_4_, ...), custom_call_target="tpu_custom_call" | custom-call | flops 1 | bytes 1 | tf_op jit(solution)/shard_map/pallas_call | solution.py:54
  342.1 8.0 %shard_map.367.refs_3_.refs_0_.refs_1_ = f32[512,1024]{1,0:T(8,128)} custom-call(bf16[512,2048]{1,0:T(8,128)(2,1)} %get-tuple-element.152.refs_4_.refs_1_.refs_0_, bf16[4,512,512]{2,1,0:T(8,128)(2,1)} %shard_map.353.refs_2_.refs_1_, bf16[4,512,512]{2,1,0:T(8,128)(2,1)} %copy-done.61, f32[512,1024]{1,0:T(8,128)} %get-tuple-element.149.refs_4_.refs_3_, ...), custom_call_target="tpu_custom_call" | custom-call | flops 1 | bytes 1 | tf_op jit(solution)/shard_map/pallas_call | solution.py:54
  359.0 7.3 %shard_map.369.refs_11_ = f32[512,1024]{1,0:T(8,128)} custom-call(s32[32]{0:T(128)S(1)} %reshape.101.table_ref, f32[512,1024]{1,0:T(8,128)} %shard_map.367.refs_3_.refs_0_.refs_1_, f32[512,1024]{1,0:T(8,128)} %shard_map.367.refs_3_.refs_0_.refs_1_, bf16[256,1536]{1,0:T(8,128)(2,1)S(1)} %get-tuple-element.173.refs_2_.refs_9_.refs_0_, ...), custom_call_target="tpu_custom_call" | custom-call | flops 1 | bytes 1 | tf_op jit(solution)/shard_map/pallas_call | solution.py:1128
  366.3 18.7 %shard_map.370 = (bf16[512,1024]{1,0:T(8,128)(2,1)}, f32[512,256]{1,0:T(8,128)S(1)}, f32[512,256]{1,0:T(8,128)}) custom-call(s32[1]{0:T(128)} %bitcast.9.refs_0_, f32[512,2560]{1,0:T(8,128)} %shard_map.343.refs_0_.refs_1_.refs_2_.refs_3_.refs_4_, f32[512,128]{1,0:T(8,128)S(1)} %get-tuple-element.317.refs_2_, f32[512,128]{1,0:T(8,128)S(1)} %get-tuple-element.380.refs_3_, ...), custom_call_target="tpu_custom_call" | custom-call | flops 1 | bytes 1 | tf_op jit(solution)/shard_map/pallas_call | solution.py:54
  386.4 4.3 shard_map.371
  406.7 36.6 %shard_map.376 = (bf16[528,2048]{1,0:T(8,128)(2,1)}, f32[528,256]{1,0:T(8,128)}, f32[4,512,128]{2,1,0:T(8,128)}, f32[4,8,512]{2,1,0:T(8,128)S(1)}, f32[4,1536]{1...) custom-call(f32[528,2048]{1,0:T(8,128)} %shard_map.336.refs_0_.refs_1_.refs_2_.refs_3_.refs_8_, ...), custom_call_target="tpu_custom_call" | custom-call | flops 1 | bytes 1 | tf_op jit(solution)/shard_map/pallas_call | solution.py:54
  455.5 4.5 shard_map.380.refs_4_
  463.0 7.9 %shard_map.381.refs_3_.refs_0_ = f32[512,1024]{1,0:T(8,128)} custom-call(bf16[512,1536]{1,0:T(8,128)(2,1)} %get-tuple-element.169.refs_4_.refs_1_.refs_0_, bf16[512,1024]{1,0:T(8,128)(2,1)S(1)} %copy-done.2, bf16[4,512,640]{2,1,0:T(8,128)(2,1)} %get-tuple-element.134.refs_7_.refs_1_.refs_2_, bf16[4,512,640]{2,1,0:T(8,128)(2,1)} %collective-permute-done.12.refs_2_.refs_3_, ...), custom_call_target="tpu_custom_call" | custom-call | flops 1 | bytes 1 | tf_op jit(solution)/shard_map/pallas_call | solution.py:54
  470.9 4.6 shard_map.382
  481.3 7.2 %shard_map.384.refs_4_.refs_1_ = f32[528,1024]{1,0:T(8,128)} custom-call(bf16[528,2048]{1,0:T(8,128)(2,1)} %get-tuple-element.193.refs_1_.refs_0_, bf16[4,512,512]{2,1,0:T(8,128)(2,1)} %get-tuple-element.126.refs_1_, bf16[4,512,512]{2,1,0:T(8,128)(2,1)} %collective-permute-done.7.refs_2_, bf16[128,2048]{1,0:T(8,128)(2,1)S(1)} %copy-done.18, ...), custom_call_target="tpu_custom_call" | custom-call | flops 1 | bytes 1 | tf_op jit(solution)/shard_map/pallas_call | solution.py:54
  495.8 5.7 %shard_map.386 = (f32[512,1024]{1,0:T(8,128)}, f32[8,1024]{1,0:T(8,128)S(1)}) custom-call(f32[512,1024]{1,0:T(8,128)} %shard_map.381.refs_3_.refs_0_, f32[528,1024]{1,0:T(8,128)} %shard_map.384.refs_4_.refs_1_, f32[16,1024]{1,0:T(8,128)S(1)} %collective-permute-done.50.refs_2_, bf16[512,1024]{1,0:T(8,128)(2,1)} %get-tuple-element.276.refs_3_, ...), custom_call_target="tpu_custom_call" | custom-call | flops 1 | bytes 1 | tf_op jit(solution)/shard_map/pallas_call | solution.py:54
  501.5 7.3 %shard_map.387 = (f32[512,1024]{1,0:T(8,128)}, f32[8,1024]{1,0:T(8,128)S(1)}) custom-call(s32[32]{0:T(128)S(1)} %reshape.101.table_ref, f32[512,1024]{1,0:T(8,128)} %get-tuple-element.212.refs_0_.refs_1_, f32[512,1024]{1,0:T(8,128)} %get-tuple-element.212.refs_0_.refs_1_, f32[8,1024]{1,0:T(8,128)S(1)} %get-tuple-element.213.refs_2_.refs_3_, ...), custom_call_target="tpu_custom_call" | custom-call | flops 1 | bytes 1 | tf_op jit(solution)/shard_map/pallas_call | solution.py:1128
  535.9 15.8 %reduce-scatter.6.cloned.1.call-done = bf16[1,128,768]{2,1,0:T(8,128)(2,1)} async-done(((bf16[4,128,768]{2,1,0:T(8,128)(2,1)}), bf16[1,128,768]{2,1,0:T(8,128)(2,1)}) %reduce-scatter.6.cloned.1.call-update) | async-done | bytes 196624 | tf_op jit(solution)/shard_map/reduce_scatter | solution.py:1210
  (476 shorter events, 237.1 us)
Async XLA Ops:
  7.2 43.4 %all-gather.8.cloned.1.call-start = ((), (), s32[]{:S(2)}) async-start(), calls=%async_computation.7 | async-start | bytes 1474560 | tf_op jit(solution)/shard_map/all_gather | solution.py:1161
  8.7 19.9 %collective-permute-start = (bf16[16,1024]{1,0:T(8,128)(2,1)}, bf16[16,1024]{1,0:T(8,128)(2,1)}, u32[]{:S(2)}, u32[]{:S(2)}) collective-permute-start(bf16[16,1024]{1,0:T(8,128)(2,1)} %slice.89), channel_id=1, source_target_pairs={{0,1},{2,3},{4,5},{6,7},{8,9},{10,11},{12,13},{14,15},{16,17},{18,... | collective-permute-start | bytes 98312 | tf_op jit(solution)/shard_map/ppermute | solution.py:1213
  19.8 99.1 %all-gather.10.cloned.1.call-start = ((), (), s32[]{:S(2)}) async-start(), calls=%async_computation.8 | async-start | bytes 1310720 | tf_op jit(solution)/shard_map/all_gather | solution.py:1161
  62.8 20.3 %collective-permute-start.3 = (bf16[4,128,512]{2,1,0:T(8,128)(2,1)S(1)}, bf16[4,128,512]{2,1,0:T(8,128)(2,1)S(1)}, u32[]{:S(2)}, u32[]{:S(2)}) collective-permute-start(bf16[4,128,512]{2,1,0:T(8,128)(2,1)S(1)} %get-tuple-element.122.refs_1_.refs_0_), channel_id=1, source_target_pairs={{0,16},{4,20},{8,24},{12,28},{16,0},{20,4},{24,8},{28,12},{1,17},{... | collective-permute-start | bytes 1572872 | tf_op jit(solution)/shard_map/ppermute | solution.py:723
  88.7 36.5 %collective-permute-start.7 = (bf16[4,512,512]{2,1,0:T(8,128)(2,1)}, bf16[4,512,512]{2,1,0:T(8,128)(2,1)}, u32[]{:S(2)}, u32[]{:S(2)}) collective-permute-start(bf16[4,512,512]{2,1,0:T(8,128)(2,1)} %get-tuple-element.126.refs_1_), channel_id=1, source_target_pairs={{0,4},{4,0},{8,12},{12,8},{16,20},{20,16},{24,28},{28,24},{1,5},{5... | collective-permute-start | bytes 6291464 | tf_op jit(solution)/shard_map/ppermute | solution.py:723
  89.6 75.6 %all-gather.6.cloned.1.call-start = ((), (), s32[]{:S(2)}) async-start(), calls=%async_computation.3 | async-start | bytes 1310720 | tf_op jit(solution)/shard_map/all_gather | solution.py:1161
  89.7 42.1 %collective-permute-start.8 = (bf16[4,128,640]{2,1,0:T(8,128)(2,1)}, bf16[4,128,640]{2,1,0:T(8,128)(2,1)S(1)}, u32[]{:S(2)}, u32[]{:S(2)}) collective-permute-start(bf16[4,128,640]{2,1,0:T(8,128)(2,1)} %get-tuple-element.127.refs_1_.refs_3_.refs_0_), channel_id=1, source_target_pairs={{0,16},{4,20},{8,24},{12,28},{16,0},{20,4},{24,8},{28,12},{1,17},{... | collective-permute-start | bytes 1966088 | tf_op jit(solution)/shard_map/ppermute | solution.py:723
  90.3 41.5 %collective-permute-start.9 = (bf16[4,128,640]{2,1,0:T(8,128)(2,1)}, bf16[4,128,640]{2,1,0:T(8,128)(2,1)}, u32[]{:S(2)}, u32[]{:S(2)}) collective-permute-start(bf16[4,128,640]{2,1,0:T(8,128)(2,1)} %get-tuple-element.128.refs_2_.refs_4_), channel_id=1, source_target_pairs={{0,8},{4,12},{8,0},{12,4},{16,24},{20,28},{24,16},{28,20},{1,9},{5... | collective-permute-start | bytes 1966088 | tf_op jit(solution)/shard_map/ppermute | solution.py:723
  136.8 38.0 %collective-permute-start.12 = (bf16[4,512,640]{2,1,0:T(8,128)(2,1)}, bf16[4,512,640]{2,1,0:T(8,128)(2,1)}, u32[]{:S(2)}, u32[]{:S(2)}) collective-permute-start(bf16[4,512,640]{2,1,0:T(8,128)(2,1)} %get-tuple-element.134.refs_7_.refs_1_.refs_2_), channel_id=1, source_target_pairs={{0,4},{4,0},{8,12},{12,8},{16,20},{20,16},{24,28},{28,24},{1,5},{5... | collective-permute-start | bytes 7864328 | tf_op jit(solution)/shard_map/ppermute | solution.py:723
  137.8 389.8 %reduce-scatter.8.cloned.1.call-start = ((), (), s32[]{:S(2)}) async-start(), calls=%async_computation.6 | async-start | bytes 655360 | tf_op jit(solution)/shard_map/reduce_scatter | solution.py:1210
  138.0 20.4 %collective-permute-start.13 = (bf16[4,128,512]{2,1,0:T(8,128)(2,1)S(1)}, bf16[4,128,512]{2,1,0:T(8,128)(2,1)S(1)}, u32[]{:S(2)}, u32[]{:S(2)}) collective-permute-start(bf16[4,128,512]{2,1,0:T(8,128)(2,1)S(1)} %get-tuple-element.135.refs_8_.refs_0_), channel_id=1, source_target_pairs={{0,16},{4,20},{8,24},{12,28},{16,0},{20,4},{24,8},{28,12},{1,17},{... | collective-permute-start | bytes 1572872 | tf_op jit(solution)/shard_map/ppermute | solution.py:723
  162.1 44.6 %collective-permute-start.19 = (bf16[4,512,512]{2,1,0:T(8,128)(2,1)}, bf16[4,512,512]{2,1,0:T(8,128)(2,1)}, u32[]{:S(2)}, u32[]{:S(2)}) collective-permute-start(bf16[4,512,512]{2,1,0:T(8,128)(2,1)} %shard_map.340.refs_1_.refs_3_.refs_2_), channel_id=1, source_target_pairs={{0,4},{4,0},{8,12},{12,8},{16,20},{20,16},{24,28},{28,24},{1,5},{5... | collective-permute-start | bytes 6291464 | tf_op jit(solution)/shard_map/ppermute | solution.py:723
  186.6 29.3 %collective-permute-start.20 = (bf16[4,128,1024]{2,1,0:T(8,128)(2,1)}, bf16[4,128,1024]{2,1,0:T(8,128)(2,1)S(1)}, u32[]{:S(2)}, u32[]{:S(2)}) collective-permute-start(bf16[4,128,1024]{2,1,0:T(8,128)(2,1)} %get-tuple-element.143.refs_6_.refs_0_), channel_id=1, source_target_pairs={{0,16},{4,20},{8,24},{12,28},{16,0},{20,4},{24,8},{28,12},{1,17},{... | collective-permute-start | bytes 3145736 | tf_op jit(solution)/shard_map/ppermute | solution.py:723
  187.9 28.1 %collective-permute-start.21 = (bf16[4,128,1024]{2,1,0:T(8,128)(2,1)}, bf16[4,128,1024]{2,1,0:T(8,128)(2,1)S(1)}, u32[]{:S(2)}, u32[]{:S(2)}) collective-permute-start(bf16[4,128,1024]{2,1,0:T(8,128)(2,1)} %get-tuple-element.144.refs_7_.refs_2_), channel_id=1, source_target_pairs={{0,8},{4,12},{8,0},{12,4},{16,24},{20,28},{24,16},{28,20},{1,9},{5... | collective-permute-start | bytes 3145736 | tf_op jit(solution)/shard_map/ppermute | solution.py:723
  279.0 29.4 %collective-permute-start.32 = (bf16[512,4096]{1,0:T(8,128)(2,1)}, bf16[512,4096]{1,0:T(8,128)(2,1)S(1)}, u32[]{:S(2)}, u32[]{:S(2)}) collective-permute-start(bf16[512,4096]{1,0:T(8,128)(2,1)} %shard_map.357.refs_6_), channel_id=1, source_target_pairs={{0,4},{4,0},{8,12},{12,8},{16,20},{20,16},{24,28},{28,24},{1,5},{5... | collective-permute-start | bytes 12582920 | tf_op jit(solution)/shard_map/ppermute | solution.py:723
  306.6 28.9 %collective-permute-start.31 = (bf16[512,2048]{1,0:T(8,128)(2,1)}, bf16[512,2048]{1,0:T(8,128)(2,1)}, u32[]{:S(2)}, u32[]{:S(2)}) collective-permute-start(bf16[512,2048]{1,0:T(8,128)(2,1)} %shard_map.361.refs_3_.refs_6_), channel_id=1, source_target_pairs={{0,4},{4,0},{8,12},{12,8},{16,20},{20,16},{24,28},{28,24},{1,5},{5... | collective-permute-start | bytes 6291464 | tf_op jit(solution)/shard_map/ppermute | solution.py:723
  306.6 21.7 %collective-permute-start.33 = (bf16[64,2048]{1,0:T(8,128)(2,1)S(1)}, bf16[64,2048]{1,0:T(8,128)(2,1)S(1)}, u32[]{:S(2)}, u32[]{:S(2)}) collective-permute-start(bf16[64,2048]{1,0:T(8,128)(2,1)S(1)} %get-tuple-element.161.refs_4_), channel_id=1, source_target_pairs={{0,8},{4,12},{8,0},{12,4},{16,24},{20,28},{24,16},{28,20},{1,9},{5... | collective-permute-start | bytes 786440 | tf_op jit(solution)/shard_map/ppermute | solution.py:723
  307.2 21.2 %collective-permute-start.34 = (bf16[64,2048]{1,0:T(8,128)(2,1)S(1)}, bf16[64,2048]{1,0:T(8,128)(2,1)S(1)}, u32[]{:S(2)}, u32[]{:S(2)}) collective-permute-start(bf16[64,2048]{1,0:T(8,128)(2,1)S(1)} %get-tuple-element.163.refs_6_), channel_id=1, source_target_pairs={{0,16},{4,20},{8,24},{12,28},{16,0},{20,4},{24,8},{28,12},{1,17},{... | collective-permute-start | bytes 786440 | tf_op jit(solution)/shard_map/ppermute | solution.py:723
  333.2 20.3 %collective-permute-start.35 = (bf16[512,1536]{1,0:T(8,128)(2,1)}, bf16[512,1536]{1,0:T(8,128)(2,1)S(1)}, u32[]{:S(2)}, u32[]{:S(2)}) collective-permute-start(bf16[512,1536]{1,0:T(8,128)(2,1)} %shard_map.365.refs_3_), channel_id=1, source_target_pairs={{0,4},{4,0},{8,12},{12,8},{16,20},{20,16},{24,28},{28,24},{1,5},{5... | collective-permute-start | bytes 4718600 | tf_op jit(solution)/shard_map/ppermute | solution.py:723
  333.2 53.2 %collective-permute-start.38 = (bf16[128,4096]{1,0:T(8,128)(2,1)}, bf16[128,4096]{1,0:T(8,128)(2,1)}, u32[]{:S(2)}, u32[]{:S(2)}) collective-permute-start(bf16[128,4096]{1,0:T(8,128)(2,1)} %get-tuple-element.166.refs_8_), channel_id=1, source_target_pairs={{0,16},{4,20},{8,24},{12,28},{16,0},{20,4},{24,8},{28,12},{1,17},{... | collective-permute-start | bytes 3145736 | tf_op jit(solution)/shard_map/ppermute | solution.py:723
  334.1 52.4 %collective-permute-start.39 = (bf16[128,4096]{1,0:T(8,128)(2,1)}, bf16[128,4096]{1,0:T(8,128)(2,1)}, u32[]{:S(2)}, u32[]{:S(2)}) collective-permute-start(bf16[128,4096]{1,0:T(8,128)(2,1)} %get-tuple-element.168.refs_10_), channel_id=1, source_target_pairs={{0,8},{4,12},{8,0},{12,4},{16,24},{20,28},{24,16},{28,20},{1,9},{5... | collective-permute-start | bytes 3145736 | tf_op jit(solution)/shard_map/ppermute | solution.py:723
  339.6 52.8 %collective-permute-start.40 = (bf16[256,2048]{1,0:T(8,128)(2,1)}, bf16[256,2048]{1,0:T(8,128)(2,1)}, u32[]{:S(2)}, u32[]{:S(2)}) collective-permute-start(bf16[256,2048]{1,0:T(8,128)(2,1)} %get-tuple-element.171.refs_5_.refs_8_), channel_id=1, source_target_pairs={{0,16},{4,20},{8,24},{12,28},{16,0},{20,4},{24,8},{28,12},{1,17},{... | collective-permute-start | bytes 3145736 | tf_op jit(solution)/shard_map/ppermute | solution.py:723
  357.6 39.6 %collective-permute-start.41 = (bf16[256,1536]{1,0:T(8,128)(2,1)S(1)}, bf16[256,1536]{1,0:T(8,128)(2,1)}, u32[]{:S(2)}, u32[]{:S(2)}) collective-permute-start(bf16[256,1536]{1,0:T(8,128)(2,1)S(1)} %get-tuple-element.174.refs_3_.refs_10_), channel_id=1, source_target_pairs={{0,8},{4,12},{8,0},{12,4},{16,24},{20,28},{24,16},{28,20},{1,9},{5... | collective-permute-start | bytes 2359304 | tf_op jit(solution)/shard_map/ppermute | solution.py:723
  358.3 173.6 %reduce-scatter.4.cloned.1.call-start = ((), (), s32[]{:S(2)}) async-start(), calls=%async_computation.4 | async-start | bytes 2457600 | tf_op jit(solution)/shard_map/reduce_scatter | solution.py:1210
  394.3 49.0 %collective-permute-start.44 = (bf16[128,2048]{1,0:T(8,128)(2,1)S(1)}, bf16[128,2048]{1,0:T(8,128)(2,1)S(1)}, u32[]{:S(2)}, u32[]{:S(2)}) collective-permute-start(bf16[128,2048]{1,0:T(8,128)(2,1)S(1)} %get-tuple-element.183.refs_3_.refs_10_.refs_16_), channel_id=1, source_target_pairs={{0,8},{4,12},{8,0},{12,4},{16,24},{20,28},{24,16},{28,20},{1,9},{5... | collective-permute-start | bytes 1572872 | tf_op jit(solution)/shard_map/ppermute | solution.py:723
  395.8 47.5 %collective-permute-start.42 = (bf16[64,4096]{1,0:T(8,128)(2,1)S(1)}, bf16[64,4096]{1,0:T(8,128)(2,1)S(1)}, u32[]{:S(2)}, u32[]{:S(2)}) collective-permute-start(bf16[64,4096]{1,0:T(8,128)(2,1)S(1)} %copy-done.15), channel_id=1, source_target_pairs={{0,8},{4,12},{8,0},{12,4},{16,24},{20,28},{24,16},{28,20},{1,9},{5... | collective-permute-start | bytes 1572872 | tf_op jit(solution)/shard_map/ppermute | solution.py:723
  396.4 47.0 %collective-permute-start.43 = (bf16[64,4096]{1,0:T(8,128)(2,1)S(1)}, bf16[64,4096]{1,0:T(8,128)(2,1)S(1)}, u32[]{:S(2)}, u32[]{:S(2)}) collective-permute-start(bf16[64,4096]{1,0:T(8,128)(2,1)S(1)} %copy-done.62), channel_id=1, source_target_pairs={{0,16},{4,20},{8,24},{12,28},{16,0},{20,4},{24,8},{28,12},{1,17},{... | collective-permute-start | bytes 1572872 | tf_op jit(solution)/shard_map/ppermute | solution.py:723
  398.7 44.6 %collective-permute-start.45 = (bf16[128,1536]{1,0:T(8,128)(2,1)S(1)}, bf16[128,1536]{1,0:T(8,128)(2,1)S(1)}, u32[]{:S(2)}, u32[]{:S(2)}) collective-permute-start(bf16[128,1536]{1,0:T(8,128)(2,1)S(1)} %get-tuple-element.185.refs_12_.refs_18_), channel_id=1, source_target_pairs={{0,16},{4,20},{8,24},{12,28},{16,0},{20,4},{24,8},{28,12},{1,17},{... | collective-permute-start | bytes 1179656 | tf_op jit(solution)/shard_map/ppermute | solution.py:723
  405.8 47.3 %collective-permute-start.46 = (bf16[512,1024]{1,0:T(8,128)(2,1)S(1)}, bf16[512,1024]{1,0:T(8,128)(2,1)}, u32[]{:S(2)}, u32[]{:S(2)}) collective-permute-start(bf16[512,1024]{1,0:T(8,128)(2,1)S(1)} %shard_map.375.refs_19_), channel_id=1, source_target_pairs={{0,4},{4,0},{8,12},{12,8},{16,20},{20,16},{24,28},{28,24},{1,5},{5... | collective-permute-start | bytes 3145736 | tf_op jit(solution)/shard_map/ppermute | solution.py:723
  448.3 103.3 %reduce-scatter.6.cloned.1.call-start = ((), (), s32[]{:S(2)}) async-start(), calls=%async_computation.5 | async-start | bytes 983040 | tf_op jit(solution)/shard_map/reduce_scatter | solution.py:1210
  493.6 32.2 %collective-permute-start.53 = (bf16[64,2048]{1,0:T(8,128)(2,1)S(1)}, bf16[64,2048]{1,0:T(8,128)(2,1)S(1)}, u32[]{:S(2)}, u32[]{:S(2)}) collective-permute-start(bf16[64,2048]{1,0:T(8,128)(2,1)S(1)} %get-tuple-element.209.refs_8_), channel_id=1, source_target_pairs={{0,8},{4,12},{8,0},{12,4},{16,24},{20,28},{24,16},{28,20},{1,9},{5... | collective-permute-start | bytes 786440 | tf_op jit(solution)/shard_map/ppermute | solution.py:723
  494.6 31.2 %collective-permute-start.54 = (bf16[64,2048]{1,0:T(8,128)(2,1)S(1)}, bf16[64,2048]{1,0:T(8,128)(2,1)S(1)}, u32[]{:S(2)}, u32[]{:S(2)}) collective-permute-start(bf16[64,2048]{1,0:T(8,128)(2,1)S(1)} %get-tuple-element.211.refs_10_), channel_id=1, source_target_pairs={{0,16},{4,20},{8,24},{12,28},{16,0},{20,4},{24,8},{28,12},{1,17},{... | collective-permute-start | bytes 786440 | tf_op jit(solution)/shard_map/ppermute | solution.py:723
  (147 other events, 1288.8 us)
Sparse Core Ops, SparseCore 0:
  19.9 30.6 all-gather.7
  89.7 29.1 all-gather.9
  137.9 27.2 all-gather.5
  358.4 19.7 reduce-scatter.7
  448.5 41.8 reduce-scatter.3
  527.7 23.9 reduce-scatter.5

commit v3 on v2

--- a/solution.py
+++ b/solution.py
@@ -761,6 +761,38 @@
     return [(outs[2 * i], outs[2 * i + 1]) for i in range(len(ranges))]
 
 
+def cut_exchanged(own, deps=()):
+    count = lax.axis_size("tensor")
+    pieces = [own]
+    for far in range(1, count):
+        pieces.append(lax.ppermute(own, "tensor", [(i, i ^ far) for i in range(count)]))
+    rows, width = own.shape
+    half = rows // 2
+
+    def kernel(me_ref, *refs):
+        upper_ref, lower_ref = refs[-2:]
+        source = jnp.bitwise_xor(pl.program_id(0), me_ref[0])
+        for i in range(count):
+
+            @pl.when(source == i)
+            def _(i=i):
+                part = refs[i][...]
+                if half % 16:
+                    part = part.astype(f32)
+                upper_ref[0] = part[:half].astype(bf16)
+                lower_ref[0] = part[half:].astype(bf16)
+
+    return call(
+        kernel,
+        (count,),
+        [pl.BlockSpec(memory_space=pltpu.SMEM)] + [spec((rows, width), lambda t: (0, 0))] * count,
+        [spec((1, half, width), lambda t: (t, 0, 0))] * 2,
+        [shape((count, half, width), bf16)] * 2,
+        moved=count * rows * width * 4,
+        deps=deps,
+    )(lax.axis_index("tensor").astype(jnp.int32).reshape(1), *pieces)
+
+
 def spread_send(held, step):
     bits = high_bits()
     return partner(held[0], bits[step]), partner(held[1], bits[-1 - step])
@@ -1246,43 +1278,25 @@
     val_w = val_in.shape[1]
     out_in = jnp.concatenate([mixer_proj, attn_proj], axis=0).T
     out_w = out_in.shape[1]
-    in_z = over_tensor(jnp.concatenate([val_in, gate_in], axis=1))
-    back_z = over_tensor(jnp.concatenate([out_in, down_proj.T], axis=1))
+    back_in = jnp.concatenate([out_in, down_proj.T], axis=1)
+    gate_in_w = gate_in.shape[1]
+    rest_z = over_tensor(
+        jnp.concatenate([gate_in, gate_up.reshape(depth, 2 * hidden_w), back_in], axis=1)
+    )
+    ff_at = gate_in_w
+    out_at = ff_at + 2 * hidden_w
+    down_at = out_at + out_w
     tables = (cos_q, sin_q, cos_kv, sin_kv)
-    (val_held,) = cut_pieces(in_z, [(0, val_w)], (ext_in, tables, cot, group_rows))
-    val_got = spread_send(val_held, 0)
-    val_held = join(val_held, val_got)
-    val_got = spread_send(val_held, 1)
-    (gate_held,) = cut_pieces(in_z, [(val_w, in_z.shape[2])], val_held)
-    gate_got = spread_send(gate_held, 0)
-    for i in range(1, steps - 1):
-        val_held = join(val_held, val_got, gate_held)
-        val_got = spread_send(val_held, i + 1)
-    val_held, gate_held = join_all(
-        [(val_held, val_got, True), (gate_held, gate_got, False)], gate_held
-    )
+    val_held = cut_exchanged(val_in, (ext_in, tables, cot, group_rows))
+    val_held = spread_rest(val_held, spread_send(val_held, 0), 0)
     in_b = spread_end(val_held)
-    gate_got = spread_send(gate_held, 1)
-    ff_in = slice_one(gate_up.reshape(1, depth, 2 * hidden_w), 0, 2 * hidden_w, val_held)
-    ff_z = over_tensor(ff_in[0])
-
-    (out_held,) = cut_pieces(back_z, [(0, out_w)], gate_held)
-    out_got = spread_send(out_held, 0)
+
     (proj_b,) = times(
         ext_in,
         in_b,
         [shape((rows + HALO, val_w * tensor_count), f32)],
         store,
-        deps=(gate_held, out_held),
-    )
-    for i in range(1, steps - 1):
-        gate_held = join(gate_held, gate_got, proj_b)
-        gate_got = spread_send(gate_held, i + 1)
-    gate_held, out_held = join_all(
-        [(gate_held, gate_got, True), (out_held, out_got, False)], proj_b
-    )
-    in_a = spread_end(gate_held)
-    out_got = spread_send(out_held, 1)
+    )
 
     ext = rows + HALO
     whole = lambda *dims: spec(dims, lambda i: (0,) * len(dims))
@@ -1311,6 +1325,11 @@
         moved=rows * 128 * 40,
     )(proj_b, proj_b, proj_b, proj_b, bias_row, rate_row)
     skip_lanes = jnp.repeat(skip_gain, PH)[None, :]
+    (gate_held,) = cut_pieces(rest_z, [(0, gate_in_w)], cols)
+    gate_held = join(gate_held, spread_send(gate_held, 0))
+    gate_got = spread_send(gate_held, 1)
+    (out_held,) = cut_pieces(rest_z, [(out_at, down_at)], gate_held)
+    out_got = spread_send(out_held, 0)
 
     val_spec = spec((ext, val_w), lambda g: (0, g))
     shr_spec = whole(ext, 2 * NS)
@@ -1335,18 +1354,30 @@
     )(proj_b, shr, conv_filter, conv_filter, cols, cum_rows, skip_lanes)
     entering = lax.ppermute(state_local, "tensor", onward)
     per_gate = gate_held[0].shape[2] // 128
-    out_held = spread_rest(out_held, out_got, 1, y_local)
-    out_full = spread_end(out_held)
-    (ff_held,) = cut_pieces(ff_z, [(0, 2 * hidden_w)], out_held)
+    for i in range(1, steps - 1):
+        gate_held = join(gate_held, gate_got, y_local)
+        gate_got = spread_send(gate_held, i + 1)
+    gate_held, out_held = join_all(
+        [(gate_held, gate_got, True), (out_held, out_got, False)], y_local
+    )
+    in_a = spread_end(gate_held)
+    out_got = spread_send(out_held, 1)
+    (ff_held,) = cut_pieces(rest_z, [(ff_at, out_at)], gate_held)
     ff_got = spread_send(ff_held, 0)
     (proj_a,) = times(
         normed_in,
         in_a,
         [shape((rows, per_gate * 128 * tensor_count), f32)],
         store,
-        deps=(out_held, ff_held),
-    )
-    ff_held = join(ff_held, ff_got, (proj_a, entering))
+        deps=ff_held,
+    )
+    for i in range(1, steps - 1):
+        out_held = join(out_held, out_got, proj_a)
+        out_got = spread_send(out_held, i + 1)
+    out_held, ff_held = join_all(
+        [(out_held, out_got, True), (ff_held, ff_got, False)], (proj_a, entering)
+    )
+    out_full = spread_end(out_held)
     ff_got = spread_send(ff_held, 1)
 
     kv_w = 2 * KVH * HD
@@ -1378,7 +1409,7 @@
         deps=ff_held,
     )(part_arg, proj_a, cos_q, sin_q, before_kv, own_kv)
 
-    (down_held,) = cut_pieces(back_z, [(out_w, back_z.shape[2])], (attn_heads, out_full))
+    (down_held,) = cut_pieces(rest_z, [(down_at, rest_z.shape[2])], (attn_heads, out_full))
     down_got = spread_send(down_held, 0)
     block_rows = CHUNK
     wide = spec((block_rows, ssm), lambda i: (i, 0))
@@ -1628,8 +1659,11 @@
     )(
         grad_a, grad_b, late_rows, ext_low[HALO:], middle_grad, gain_first[None, :], mlp_gain_part
     )
-    residual_grad, gain_sums = restore_all([residual_grad, gain_sums])
-    last_t = finish_tensor(collect_end([rest_dp(val_sum, val_got), rest_dp(qk_sum, qk_got)]))
+    last_z = collect_end(
+        [rest_dp(val_sum, val_got), rest_dp(qk_sum, qk_got)], residual_grad
+    )
+    residual_grad, gain_sums = restore_all([residual_grad, gain_sums], last_z)
+    last_t = finish_tensor(last_z)
     gate_up_sum = ff_t.reshape(depth, 2, hidden_w)
     val_t = last_t[:, :val_w]
     qk_t = last_t[:, val_w:]

time: 574 us -> 561 us (0.977)
  waiting for transfers between devices: 99.8 us -> 91.5 us
    all_gather x3 -> x1, waiting for transfers between devices: 43.8 us -> 0.01 us  [over_tensor(): return lax.all_gather(piece, 'tensor', axis=0)]
    ppermute x51, waiting for transfers between devices: 23.9 us -> 60.2 us  [partner(): return lax.ppermute(value, 'dp', [(i, i ^ 1 << bit) for i in range(count)])]
    reduce_scatter x3, waiting for transfers between devices: 15.8 us -> 7.77 us  [finish_tensor(): total = lax.psum_scatter(joined, 'tensor', scatter_dimension=0, tiled=False)]
    unnamed x233 -> x244, local copies, waits for them, and re-layouts: 33.9 us -> 39.6 us
    pallas_call x56 -> x55, Pallas kernels: 298 us -> 295 us  [call(): return lambda *args: run(*args, *late)]
  transfers between devices with their start and end apart: 68 -> 69, of which waited for: 22 -> 25; matrix products, arithmetic and copies ran while one was open for 7% -> 6% of each run, Pallas kernels for 50% -> 50%
where the time goes in v3:
time: 561 us; the launch traced here: 554 us
  Pallas kernels  310 us (55%)
  waiting for transfers between devices  91.5 us (16%)
  local copies, waits for them, and re-layouts  64 us (11%)
  starting transfers between devices  63.8 us (11%)
  between operations  15.7 us (3%)
  other arithmetic  9.17 us (2%)
    pallas_call x55, Pallas kernels, call(): return lambda *args: run(*args, *late)  295 us
    ppermute x51, waiting for transfers between devices, partner(): return lax.ppermute(value, 'dp', [(i, i ^ 1 << bit) for i in range(count)])  60.2 us
    ppermute x51, starting transfers between devices, partner(): return lax.ppermute(value, 'dp', [(i, i ^ 1 << bit) for i in range(count)])  42.9 us
    unnamed x244, local copies, waits for them, and re-layouts  39.6 us
    pallas_call x2, Pallas kernels, restore_all(): pl.pallas_call(kernel, grid_spec=pltpu.PrefetchScalarGridSpec(num_scalar_...  14.5 us
    ppermute x5, waiting for transfers between devices, sum_all(): lax.ppermute(value, axis, [(i, i ^ 1 << bit) for i in range(count)])  12.9 us
  transfers between devices with their start and end apart: 69, of which 25 were waited for; matrix products, arithmetic and copies ran while one was open for 6% of the time, Pallas kernels for 50%

profile of v3, /device:TPU:0, one launch (start us, length us, event | category | flops | bytes accessed | tf_op | source)
XLA Modules:
  0.0 554.1 jit_solution(7843660323403792271)
XLA Ops:
  53.5 9.4 %collective-permute-done.6.refs_1_ = bf16[4,128,512]{2,1,0:T(8,128)(2,1)S(1)} collective-permute-done((bf16[4,128,512]{2,1,0:T(8,128)(2,1)S(1)}, bf16[4,128,512]{2,1,0:T(8,128)(2,1)S(1)}, u32[]{:S(2)}, u32[]{:S(2)}) %collective-permute-start.6) | collective-permute-done | bytes 524320 | tf_op jit(solution)/shard_map/ppermute | solution.py:723
  75.4 6.0 %shard_map.334.refs_0_.refs_1_.refs_2_.refs_3_ = f32[528,2048]{1,0:T(8,128)} custom-call(bf16[528,1024]{1,0:T(8,128)(2,1)S(1)} %copy-done, bf16[4,512,512]{2,1,0:T(8,128)(2,1)} %shard_map.333.refs_1_, bf16[4,512,512]{2,1,0:T(8,128)(2,1)} %copy-done.69), custom_call_target="tpu_custom_call" | custom-call | flops 1 | bytes 1 | tf_op jit(solution)/shard_map/pallas_call | solution.py:54
  91.2 8.7 %collective-permute-done.10.refs_3_ = bf16[4,64,640]{2,1,0:T(8,128)(2,1)S(1)} collective-permute-done((bf16[4,64,640]{2,1,0:T(8,128)(2,1)S(1)}, bf16[4,64,640]{2,1,0:T(8,128)(2,1)S(1)}, u32[]{:S(2)}, u32[]{:S(2)}) %collective-permute-start.10) | collective-permute-done | bytes 327712 | tf_op jit(solution)/shard_map/ppermute | solution.py:723
  110.5 12.9 %shard_map.339 = (f32[512,1536]{1,0:T(8,128)}, bf16[128,1536]{1,0:T(8,128)(2,1)S(1)}, bf16[512,256]{1,0:T(8,128)(2,1)S(1)}) custom-call(f32[528,2048]{1,0:T(8,128)} %shard_map.334.refs_0_.refs_1_.refs_2_.refs_3_, f32[528,256]{1,0:T(8,128)S(1)} %copy-done.34, f32[4,1792]{1,0:T(4,128)S(1)} %copy-done.52, f32[4,1792]{1,0:T(4,128)S(1)} %copy-done.52, ...), custom_call_target="tpu_custom_call" | custom-call | flops 1 | bytes 1 | tf_op jit(solution)/shard_map/pallas_call | solution.py:54
  138.2 7.6 %shard_map.342.refs_0_.refs_1_.refs_2_.refs_3_.refs_8_ = f32[512,2560]{1,0:T(8,128)} custom-call(bf16[512,1024]{1,0:T(8,128)(2,1)} %slice.118.refs_0_, bf16[4,512,640]{2,1,0:T(8,128)(2,1)} %get-tuple-element.134.refs_1_.refs_2_, bf16[4,512,640]{2,1,0:T(8,128)(2,1)} %copy-done.67, bf16[4,64,1024]{2,1,0:T(8,128)(2,1)S(1)} %get-tuple-element.135.refs_3_.refs_4_, ...), custom_call_target="tpu_custom_call" | custom-call | flops 1 | bytes 1 | tf_op jit(solution)/shard_map/pallas_call | solution.py:54
  146.6 10.5 %collective-permute-done.18.refs_1_ = bf16[4,128,512]{2,1,0:T(8,128)(2,1)S(1)} collective-permute-done((bf16[4,128,512]{2,1,0:T(8,128)(2,1)S(1)}, bf16[4,128,512]{2,1,0:T(8,128)(2,1)S(1)}, u32[]{:S(2)}, u32[]{:S(2)}) %collective-permute-start.18) | collective-permute-done | bytes 524320 | tf_op jit(solution)/shard_map/ppermute | solution.py:723
  157.9 4.4 shard_map.344
  167.9 5.6 %collective-permute-done.17.refs_4_ = bf16[512,256]{1,0:T(8,128)(2,1)S(1)} collective-permute-done((bf16[512,256]{1,0:T(8,128)(2,1)S(1)}, bf16[512,256]{1,0:T(8,128)(2,1)S(1)}, u32[]{:S(2)}, u32[]{:S(2)}) %collective-permute-start.17) | collective-permute-done | bytes 262176 | tf_op jit(solution)/shard_map/ppermute | solution.py:1392
  173.5 9.8 %shard_map.345.refs_1_.refs_6_ = bf16[512,512]{1,0:T(8,128)(2,1)S(1)} custom-call(s32[1]{0:T(128)} %bitcast.9.refs_0_, f32[512,2560]{1,0:T(8,128)} %shard_map.342.refs_0_.refs_1_.refs_2_.refs_3_.refs_8_, f32[512,128]{1,0:T(8,128)S(1)} %get-tuple-element.299.refs_6_.refs_2_, f32[512,128]{1,0:T(8,128)S(1)} %get-tuple-element.360.refs_7_.refs_3_, ...), custom_call_target="tpu_custom_call" | custom-call | flops 1 | bytes 1 | tf_op jit(solution)/shard_map/pallas_call | solution.py:54
  187.2 7.1 %shard_map.347 = (f32[512,1536]{1,0:T(8,128)}, bf16[512,2048]{1,0:T(8,128)(2,1)}) custom-call(f32[512,1536]{1,0:T(8,128)} %get-tuple-element.133.refs_8_.refs_0_, f32[512,2560]{1,0:T(8,128)} %shard_map.342.refs_0_.refs_1_.refs_2_.refs_3_.refs_8_, bf16[512,256]{1,0:T(8,128)(2,1)S(1)} %get-tuple-element.137.refs_2_.refs_3_.refs_7_, f32[512,128]{1,0:T(8,128)S(1)} %copy-done.48, ...), custom_call_target="tpu_custom_call" | custom-call | flops 1 | bytes 1 | tf_op jit(solution)/shard_map/pallas_call | solution.py:54
  195.8 4.4 shard_map.348.refs_5_.refs_1_
  202.4 8.2 %shard_map.349 = (f32[512,1024]{1,0:T(8,128)}, bf16[512,1024]{1,0:T(8,128)(2,1)S(1)}) custom-call(bf16[512,2048]{1,0:T(8,128)(2,1)} %get-tuple-element.147.refs_4_.refs_0_.refs_1_, bf16[4,512,512]{2,1,0:T(8,128)(2,1)} %get-tuple-element.144.refs_2_.refs_1_, bf16[4,512,512]{2,1,0:T(8,128)(2,1)} %copy-done.66, ...), custom_call_target="tpu_custom_call" | custom-call | flops 1 | bytes 1 | tf_op jit(solution)/shard_map/pallas_call | solution.py:54
  216.1 9.8 %shard_map.351 = (bf16[512,2048]{1,0:T(8,128)(2,1)}, bf16[512,2048]{1,0:T(8,128)(2,1)}, bf16[512,2048]{1,0:T(8,128)(2,1)}) custom-call(bf16[512,1024]{1,0:T(8,128)(2,1)} %copy-done.7, bf16[4,512,1024]{2,1,0:T(8,128)(2,1)} %shard_map.348.refs_5_.refs_1_, bf16[4,512,1024]{2,1,0:T(8,128)(2,1)} %collective-permute-done.25.refs_2_, ...), custom_call_target="tpu_custom_call" | custom-call | flops 1 | bytes 1 | tf_op jit(solution)/shard_map/pallas_call | solution.py:54
  237.5 7.2 %shard_map.354.refs_3_.refs_1_.refs_0_ = bf16[512,4096]{1,0:T(8,128)(2,1)} custom-call(bf16[512,1024]{1,0:T(8,128)(2,1)S(1)} %copy-done.2, bf16[4,512,512]{2,1,0:T(8,128)(2,1)} %shard_map.352.refs_2_.refs_1_, bf16[4,512,512]{2,1,0:T(8,128)(2,1)} %copy-done.68, bf16[512,2048]{1,0:T(8,128)(2,1)} %get-tuple-element.153.refs_3_, ...), custom_call_target="tpu_custom_call" | custom-call | flops 1 | bytes 1 | tf_op jit(solution)/shard_map/pallas_call | solution.py:54
  250.0 6.5 %shard_map.356.refs_6_ = bf16[512,4096]{1,0:T(8,128)(2,1)} custom-call(bf16[512,1024]{1,0:T(8,128)(2,1)} %copy-done.7, bf16[512,4096]{1,0:T(8,128)(2,1)} %shard_map.354.refs_3_.refs_1_.refs_0_, bf16[128,2048]{1,0:T(8,128)(2,1)S(1)} %get-tuple-element.155.refs_2_.refs_7_.refs_0_, bf16[128,2048]{1,0:T(8,128)(2,1)S(1)} %get-tuple-element.156.refs_3_.refs_8_, ...), custom_call_target="tpu_custom_call" | custom-call | flops 1 | bytes 1 | tf_op jit(solution)/shard_map/pallas_call | solution.py:54
  259.3 12.1 %shard_map.357 = (f32[512,1024]{1,0:T(8,128)}, bf16[512,1024]{1,0:T(8,128)(2,1)}, f32[1,1024]{1,0:T(1,128)S(1)}) custom-call(bf16[512,4096]{1,0:T(8,128)(2,1)} %shard_map.354.refs_3_.refs_1_.refs_0_, bf16[4,512,1024]{2,1,0:T(8,128)(2,1)} %shard_map.348.refs_5_.refs_1_, bf16[4,512,1024]{2,1,0:T(8,128)(2,1)} %collective-permute-done.25.refs_2_, ...), custom_call_target="tpu_custom_call" | custom-call | flops 1 | bytes 1 | tf_op jit(solution)/shard_map/pallas_call | solution.py:54
  274.2 6.4 %shard_map.359.refs_2_.refs_0_.refs_6_ = f32[512,2048]{1,0:T(8,128)} custom-call(bf16[512,1024]{1,0:T(8,128)(2,1)} %get-tuple-element.159.refs_4_.refs_0_, bf16[4,512,512]{2,1,0:T(8,128)(2,1)} %get-tuple-element.144.refs_2_.refs_1_, bf16[4,512,512]{2,1,0:T(8,128)(2,1)} %copy-done.66, bf16[64,2048]{1,0:T(8,128)(2,1)S(1)} %get-tuple-element.160.refs_3_.refs_0_, ...), custom_call_target="tpu_custom_call" | custom-call | flops 1 | bytes 1 | tf_op jit(solution)/shard_map/pallas_call | solution.py:54
  288.6 7.0 %shard_map.361 = (bf16[128,4096]{1,0:T(8,128)(2,1)S(1)}, bf16[128,4096]{1,0:T(8,128)(2,1)}, bf16[128,4096]{1,0:T(8,128)(2,1)}, bf16[128,4096]{1,0:T(8,128)(2,1)}) custom-call(bf16[512,1024]{1,0:T(8,128)(2,1)} %copy-done.7, bf16[512,4096]{1,0:T(8,128)(2,1)} %shard_map.354.refs_3_.refs_1_.refs_0_, bf16[512,4096]{1,0:T(8,128)(2,1)} %copy-done.72, ...), custom_call_target="tpu_custom_call" | custom-call | flops 1 | bytes 1 | tf_op jit(solution)/shard_map/pallas_call | solution.py:54
  296.6 9.4 %shard_map.362 = (bf16[512,1536]{1,0:T(8,128)(2,1)}, f32[512,1536]{1,0:T(8,128)}, f32[1,1536]{1,0:T(1,128)S(1)}, f32[128,1536]{1,0:T(8,128)S(1)}) custom-call(f32[512,2048]{1,0:T(8,128)} %shard_map.359.refs_2_.refs_0_.refs_6_, f32[512,1536]{1,0:T(8,128)} %get-tuple-element.164.refs_1_, f32[512,2560]{1,0:T(8,128)} %shard_map.342.refs_0_.refs_1_.refs_2_.refs_3_.refs_8_, ...), custom_call_target="tpu_custom_call" | custom-call | flops 1 | bytes 1 | tf_op jit(solution)/shard_map/pallas_call | solution.py:54
  319.6 8.0 %shard_map.366.refs_3_.refs_0_.refs_1_ = f32[512,1024]{1,0:T(8,128)} custom-call(bf16[512,2048]{1,0:T(8,128)(2,1)} %get-tuple-element.152.refs_4_.refs_1_.refs_0_, bf16[4,512,512]{2,1,0:T(8,128)(2,1)} %shard_map.352.refs_2_.refs_1_, bf16[4,512,512]{2,1,0:T(8,128)(2,1)} %copy-done.68, f32[512,1024]{1,0:T(8,128)} %get-tuple-element.149.refs_4_.refs_3_, ...), custom_call_target="tpu_custom_call" | custom-call | flops 1 | bytes 1 | tf_op jit(solution)/shard_map/pallas_call | solution.py:54
  333.9 7.3 %shard_map.368.refs_11_ = f32[512,1024]{1,0:T(8,128)} custom-call(s32[32]{0:T(128)S(1)} %reshape.104.table_ref, f32[512,1024]{1,0:T(8,128)} %shard_map.366.refs_3_.refs_0_.refs_1_, f32[512,1024]{1,0:T(8,128)} %shard_map.366.refs_3_.refs_0_.refs_1_, bf16[256,1536]{1,0:T(8,128)(2,1)S(1)} %get-tuple-element.173.refs_2_.refs_9_.refs_0_, ...), custom_call_target="tpu_custom_call" | custom-call | flops 1 | bytes 1 | tf_op jit(solution)/shard_map/pallas_call | solution.py:1160
  341.2 18.7 %shard_map.369 = (bf16[512,1024]{1,0:T(8,128)(2,1)}, f32[512,256]{1,0:T(8,128)S(1)}, f32[512,256]{1,0:T(8,128)}) custom-call(s32[1]{0:T(128)} %bitcast.9.refs_0_, f32[512,2560]{1,0:T(8,128)} %shard_map.342.refs_0_.refs_1_.refs_2_.refs_3_.refs_8_, f32[512,128]{1,0:T(8,128)S(1)} %get-tuple-element.299.refs_6_.refs_2_, ...), custom_call_target="tpu_custom_call" | custom-call | flops 1 | bytes 1 | tf_op jit(solution)/shard_map/pallas_call | solution.py:54
  381.3 36.6 %shard_map.375 = (bf16[528,2048]{1,0:T(8,128)(2,1)}, f32[528,256]{1,0:T(8,128)}, f32[4,512,128]{2,1,0:T(8,128)}, f32[4,8,512]{2,1,0:T(8,128)S(1)}, f32[4,1536]{1...) custom-call(f32[528,2048]{1,0:T(8,128)} %shard_map.334.refs_0_.refs_1_.refs_2_.refs_3_, ...), custom_call_target="tpu_custom_call" | custom-call | flops 1 | bytes 1 | tf_op jit(solution)/shard_map/pallas_call | solution.py:54
  430.0 4.6 shard_map.379.refs_4_
  434.7 7.9 %shard_map.380.refs_3_.refs_0_ = f32[512,1024]{1,0:T(8,128)} custom-call(bf16[512,1536]{1,0:T(8,128)(2,1)} %get-tuple-element.169.refs_4_.refs_1_.refs_0_, bf16[512,1024]{1,0:T(8,128)(2,1)S(1)} %copy-done.3, bf16[4,512,640]{2,1,0:T(8,128)(2,1)} %get-tuple-element.134.refs_1_.refs_2_, bf16[4,512,640]{2,1,0:T(8,128)(2,1)} %copy-done.67, ...), custom_call_target="tpu_custom_call" | custom-call | flops 1 | bytes 1 | tf_op jit(solution)/shard_map/pallas_call | solution.py:54
  443.9 4.5 shard_map.381
  454.4 15.6 %collective-permute-done.51.refs_1_ = bf16[128,1024]{1,0:T(8,128)(2,1)S(1)} collective-permute-done((bf16[128,1024]{1,0:T(8,128)(2,1)S(1)}, bf16[128,1024]{1,0:T(8,128)(2,1)S(1)}, u32[]{:S(2)}, u32[]{:S(2)}) %collective-permute-start.51) | collective-permute-done | bytes 262176 | tf_op jit(solution)/shard_map/ppermute | solution.py:723
  472.3 7.1 %shard_map.383.refs_4_.refs_1_ = f32[528,1024]{1,0:T(8,128)} custom-call(bf16[528,2048]{1,0:T(8,128)(2,1)} %get-tuple-element.193.refs_1_.refs_0_, bf16[4,512,512]{2,1,0:T(8,128)(2,1)} %shard_map.333.refs_1_, bf16[4,512,512]{2,1,0:T(8,128)(2,1)} %copy-done.69, bf16[128,2048]{1,0:T(8,128)(2,1)S(1)} %copy-done.22, bf16[128,2048]{1,0:T(8,128)(2,1)S(1)} %copy-done.40, ...), custom_call_target="tpu_custom_call" | custom-call | flops 1 | bytes 1 | tf_op jit(solution)/shard_map/pallas_call | solution.py:54
  487.3 5.1 collective-permute-done.53.refs_2_
  492.4 5.7 %shard_map.385 = (f32[512,1024]{1,0:T(8,128)}, f32[8,1024]{1,0:T(8,128)S(1)}) custom-call(f32[512,1024]{1,0:T(8,128)} %shard_map.380.refs_3_.refs_0_, f32[528,1024]{1,0:T(8,128)} %shard_map.383.refs_4_.refs_1_, f32[16,1024]{1,0:T(8,128)S(1)} %collective-permute-done.53.refs_2_, bf16[512,1024]{1,0:T(8,128)(2,1)} %get-tuple-element.258.refs_3_, ...), custom_call_target="tpu_custom_call" | custom-call | flops 1 | bytes 1 | tf_op jit(solution)/shard_map/pallas_call | solution.py:54
  501.0 7.3 %shard_map.387 = (f32[512,1024]{1,0:T(8,128)}, f32[8,1024]{1,0:T(8,128)S(1)}) custom-call(s32[32]{0:T(128)S(1)} %reshape.104.table_ref, f32[512,1024]{1,0:T(8,128)} %get-tuple-element.212.refs_8_.refs_0_.refs_1_, f32[512,1024]{1,0:T(8,128)} %get-tuple-element.212.refs_8_.refs_0_.refs_1_, f32[8,1024]{1,0:T(8,128)S(1)} %get-tuple-element.213.refs_2_.refs_3_, ...), custom_call_target="tpu_custom_call" | custom-call | flops 1 | bytes 1 | tf_op jit(solution)/shard_map/pallas_call | solution.py:1160
  534.5 7.8 %reduce-scatter.6.cloned.1.call-done = bf16[1,128,768]{2,1,0:T(8,128)(2,1)} async-done(((bf16[4,128,768]{2,1,0:T(8,128)(2,1)}), bf16[1,128,768]{2,1,0:T(8,128)(2,1)}) %reduce-scatter.6.cloned.1.call-update) | async-done | bytes 196624 | tf_op jit(solution)/shard_map/reduce_scatter | solution.py:1242
  (486 shorter events, 249.3 us)
Async XLA Ops:
  7.2 78.8 %all-gather.3.cloned.1.call-start = ((), (), s32[]{:S(2)}) async-start(), calls=%async_computation.6 | async-start | bytes 3440640 | tf_op jit(solution)/shard_map/all_gather | solution.py:1193
  10.6 31.0 %collective-permute-start.1 = (bf16[128,512]{1,0:T(8,128)(2,1)S(1)}, bf16[128,512]{1,0:T(8,128)(2,1)S(1)}, u32[]{:S(2)}, u32[]{:S(2)}) collective-permute-start(bf16[128,512]{1,0:T(8,128)(2,1)S(1)} %maximum_maximum_fusion.refs_1_), channel_id=1, source_target_pairs={{0,1},{1,0},{2,3},{3,2},{4,5},{5,4},{6,7},{7,6},{8,9},{9,8},{10,11... | collective-permute-start | bytes 393224 | tf_op jit(solution)/shard_map/ppermute | solution.py:768
  13.7 27.9 %collective-permute-start.2 = (bf16[128,512]{1,0:T(8,128)(2,1)S(1)}, bf16[128,512]{1,0:T(8,128)(2,1)S(1)}, u32[]{:S(2)}, u32[]{:S(2)}) collective-permute-start(bf16[128,512]{1,0:T(8,128)(2,1)S(1)} %maximum_maximum_fusion.refs_1_), channel_id=1, source_target_pairs={{0,2},{1,3},{2,0},{3,1},{4,6},{5,7},{6,4},{7,5},{8,10},{9,11},{10,... | collective-permute-start | bytes 393224 | tf_op jit(solution)/shard_map/ppermute | solution.py:768
  16.2 25.4 %collective-permute-start.3 = (bf16[128,512]{1,0:T(8,128)(2,1)S(1)}, bf16[128,512]{1,0:T(8,128)(2,1)S(1)}, u32[]{:S(2)}, u32[]{:S(2)}) collective-permute-start(bf16[128,512]{1,0:T(8,128)(2,1)S(1)} %maximum_maximum_fusion.refs_1_), channel_id=1, source_target_pairs={{0,3},{1,2},{2,1},{3,0},{4,7},{5,6},{6,5},{7,4},{8,11},{9,10},{10,... | collective-permute-start | bytes 393224 | tf_op jit(solution)/shard_map/ppermute | solution.py:768
  22.9 502.7 %reduce-scatter.8.cloned.1.call-start = ((), (), s32[]{:S(2)}) async-start(), calls=%async_computation.5 | async-start | bytes 655360 | tf_op jit(solution)/shard_map/reduce_scatter | solution.py:1242
  101.5 22.8 %collective-permute-start.11 = (bf16[4,128,640]{2,1,0:T(8,128)(2,1)S(1)}, bf16[4,128,640]{2,1,0:T(8,128)(2,1)}, u32[]{:S(2)}, u32[]{:S(2)}) collective-permute-start(bf16[4,128,640]{2,1,0:T(8,128)(2,1)S(1)} %get-tuple-element.129.refs_1_.refs_7_.refs_0_), channel_id=1, source_target_pairs={{0,16},{4,20},{8,24},{12,28},{16,0},{20,4},{24,8},{28,12},{1,17},{... | collective-permute-start | bytes 1966088 | tf_op jit(solution)/shard_map/ppermute | solution.py:723
  103.1 21.3 %collective-permute-start.12 = (bf16[4,128,640]{2,1,0:T(8,128)(2,1)}, bf16[4,128,640]{2,1,0:T(8,128)(2,1)}, u32[]{:S(2)}, u32[]{:S(2)}) collective-permute-start(bf16[4,128,640]{2,1,0:T(8,128)(2,1)} %get-tuple-element.130.refs_2_.refs_8_), channel_id=1, source_target_pairs={{0,8},{4,12},{8,0},{12,4},{16,24},{20,28},{24,16},{28,20},{1,9},{5... | collective-permute-start | bytes 1966088 | tf_op jit(solution)/shard_map/ppermute | solution.py:723
  107.3 17.1 %collective-permute-start.13 = (bf16[4,64,512]{2,1,0:T(8,128)(2,1)S(1)}, bf16[4,64,512]{2,1,0:T(8,128)(2,1)}, u32[]{:S(2)}, u32[]{:S(2)}) collective-permute-start(bf16[4,64,512]{2,1,0:T(8,128)(2,1)S(1)} %get-tuple-element.131.refs_9_.refs_4_), channel_id=1, source_target_pairs={{0,8},{4,12},{8,0},{12,4},{16,24},{20,28},{24,16},{28,20},{1,9},{5... | collective-permute-start | bytes 786440 | tf_op jit(solution)/shard_map/ppermute | solution.py:723
  132.6 24.5 %collective-permute-start.18 = (bf16[4,128,512]{2,1,0:T(8,128)(2,1)S(1)}, bf16[4,128,512]{2,1,0:T(8,128)(2,1)S(1)}, u32[]{:S(2)}, u32[]{:S(2)}) collective-permute-start(bf16[4,128,512]{2,1,0:T(8,128)(2,1)S(1)} %get-tuple-element.140.refs_0_), channel_id=1, source_target_pairs={{0,16},{4,20},{8,24},{12,28},{16,0},{20,4},{24,8},{28,12},{1,17},{... | collective-permute-start | bytes 1572872 | tf_op jit(solution)/shard_map/ppermute | solution.py:723
  133.9 23.2 %collective-permute-start.19 = (bf16[4,128,512]{2,1,0:T(8,128)(2,1)S(1)}, bf16[4,128,512]{2,1,0:T(8,128)(2,1)S(1)}, u32[]{:S(2)}, u32[]{:S(2)}) collective-permute-start(bf16[4,128,512]{2,1,0:T(8,128)(2,1)S(1)} %copy-done.50), channel_id=1, source_target_pairs={{0,8},{4,12},{8,0},{12,4},{16,24},{20,28},{24,16},{28,20},{1,9},{5... | collective-permute-start | bytes 1572872 | tf_op jit(solution)/shard_map/ppermute | solution.py:723
  162.3 21.0 %collective-permute-start.22 = (bf16[4,512,512]{2,1,0:T(8,128)(2,1)}, bf16[4,512,512]{2,1,0:T(8,128)(2,1)S(1)}, u32[]{:S(2)}, u32[]{:S(2)}) collective-permute-start(bf16[4,512,512]{2,1,0:T(8,128)(2,1)} %get-tuple-element.144.refs_2_.refs_1_), channel_id=1, source_target_pairs={{0,4},{4,0},{8,12},{12,8},{16,20},{20,16},{24,28},{28,24},{1,5},{5... | collective-permute-start | bytes 6291464 | tf_op jit(solution)/shard_map/ppermute | solution.py:723
  162.3 32.0 %collective-permute-start.23 = (bf16[4,128,1024]{2,1,0:T(8,128)(2,1)}, bf16[4,128,1024]{2,1,0:T(8,128)(2,1)S(1)}, u32[]{:S(2)}, u32[]{:S(2)}) collective-permute-start(bf16[4,128,1024]{2,1,0:T(8,128)(2,1)} %get-tuple-element.142.refs_6_.refs_0_), channel_id=1, source_target_pairs={{0,16},{4,20},{8,24},{12,28},{16,0},{20,4},{24,8},{28,12},{1,17},{... | collective-permute-start | bytes 3145736 | tf_op jit(solution)/shard_map/ppermute | solution.py:723
  163.0 31.2 %collective-permute-start.24 = (bf16[4,128,1024]{2,1,0:T(8,128)(2,1)}, bf16[4,128,1024]{2,1,0:T(8,128)(2,1)S(1)}, u32[]{:S(2)}, u32[]{:S(2)}) collective-permute-start(bf16[4,128,1024]{2,1,0:T(8,128)(2,1)} %get-tuple-element.143.refs_7_.refs_2_), channel_id=1, source_target_pairs={{0,8},{4,12},{8,0},{12,4},{16,24},{20,28},{24,16},{28,20},{1,9},{5... | collective-permute-start | bytes 3145736 | tf_op jit(solution)/shard_map/ppermute | solution.py:723
  256.5 30.2 %collective-permute-start.35 = (bf16[512,4096]{1,0:T(8,128)(2,1)}, bf16[512,4096]{1,0:T(8,128)(2,1)S(1)}, u32[]{:S(2)}, u32[]{:S(2)}) collective-permute-start(bf16[512,4096]{1,0:T(8,128)(2,1)} %shard_map.356.refs_6_), channel_id=1, source_target_pairs={{0,4},{4,0},{8,12},{12,8},{16,20},{20,16},{24,28},{28,24},{1,5},{5... | collective-permute-start | bytes 12582920 | tf_op jit(solution)/shard_map/ppermute | solution.py:723
  284.6 30.3 %collective-permute-start.34 = (bf16[512,2048]{1,0:T(8,128)(2,1)}, bf16[512,2048]{1,0:T(8,128)(2,1)}, u32[]{:S(2)}, u32[]{:S(2)}) collective-permute-start(bf16[512,2048]{1,0:T(8,128)(2,1)} %shard_map.360.refs_3_.refs_6_), channel_id=1, source_target_pairs={{0,4},{4,0},{8,12},{12,8},{16,20},{20,16},{24,28},{28,24},{1,5},{5... | collective-permute-start | bytes 6291464 | tf_op jit(solution)/shard_map/ppermute | solution.py:723
  284.6 22.0 %collective-permute-start.36 = (bf16[64,2048]{1,0:T(8,128)(2,1)S(1)}, bf16[64,2048]{1,0:T(8,128)(2,1)S(1)}, u32[]{:S(2)}, u32[]{:S(2)}) collective-permute-start(bf16[64,2048]{1,0:T(8,128)(2,1)S(1)} %get-tuple-element.161.refs_4_), channel_id=1, source_target_pairs={{0,8},{4,12},{8,0},{12,4},{16,24},{20,28},{24,16},{28,20},{1,9},{5... | collective-permute-start | bytes 786440 | tf_op jit(solution)/shard_map/ppermute | solution.py:723
  285.9 20.6 %collective-permute-start.37 = (bf16[64,2048]{1,0:T(8,128)(2,1)S(1)}, bf16[64,2048]{1,0:T(8,128)(2,1)S(1)}, u32[]{:S(2)}, u32[]{:S(2)}) collective-permute-start(bf16[64,2048]{1,0:T(8,128)(2,1)S(1)} %get-tuple-element.163.refs_6_), channel_id=1, source_target_pairs={{0,16},{4,20},{8,24},{12,28},{16,0},{20,4},{24,8},{28,12},{1,17},{... | collective-permute-start | bytes 786440 | tf_op jit(solution)/shard_map/ppermute | solution.py:723
  312.8 48.5 %collective-permute-start.41 = (bf16[128,4096]{1,0:T(8,128)(2,1)}, bf16[128,4096]{1,0:T(8,128)(2,1)}, u32[]{:S(2)}, u32[]{:S(2)}) collective-permute-start(bf16[128,4096]{1,0:T(8,128)(2,1)} %get-tuple-element.166.refs_8_), channel_id=1, source_target_pairs={{0,16},{4,20},{8,24},{12,28},{16,0},{20,4},{24,8},{28,12},{1,17},{... | collective-permute-start | bytes 3145736 | tf_op jit(solution)/shard_map/ppermute | solution.py:723
  314.2 47.1 %collective-permute-start.42 = (bf16[128,4096]{1,0:T(8,128)(2,1)}, bf16[128,4096]{1,0:T(8,128)(2,1)}, u32[]{:S(2)}, u32[]{:S(2)}) collective-permute-start(bf16[128,4096]{1,0:T(8,128)(2,1)} %get-tuple-element.168.refs_10_), channel_id=1, source_target_pairs={{0,8},{4,12},{8,0},{12,4},{16,24},{20,28},{24,16},{28,20},{1,9},{5... | collective-permute-start | bytes 3145736 | tf_op jit(solution)/shard_map/ppermute | solution.py:723
  318.9 48.3 %collective-permute-start.43 = (bf16[256,2048]{1,0:T(8,128)(2,1)}, bf16[256,2048]{1,0:T(8,128)(2,1)}, u32[]{:S(2)}, u32[]{:S(2)}) collective-permute-start(bf16[256,2048]{1,0:T(8,128)(2,1)} %get-tuple-element.171.refs_5_.refs_8_), channel_id=1, source_target_pairs={{0,16},{4,20},{8,24},{12,28},{16,0},{20,4},{24,8},{28,12},{1,17},{... | collective-permute-start | bytes 3145736 | tf_op jit(solution)/shard_map/ppermute | solution.py:723
  331.7 37.4 %collective-permute-start.44 = (bf16[256,1536]{1,0:T(8,128)(2,1)S(1)}, bf16[256,1536]{1,0:T(8,128)(2,1)}, u32[]{:S(2)}, u32[]{:S(2)}) collective-permute-start(bf16[256,1536]{1,0:T(8,128)(2,1)S(1)} %get-tuple-element.174.refs_3_.refs_10_), channel_id=1, source_target_pairs={{0,8},{4,12},{8,0},{12,4},{16,24},{20,28},{24,16},{28,20},{1,9},{5... | collective-permute-start | bytes 2359304 | tf_op jit(solution)/shard_map/ppermute | solution.py:723
  333.2 197.4 %reduce-scatter.4.cloned.1.call-start = ((), (), s32[]{:S(2)}) async-start(), calls=%async_computation.3 | async-start | bytes 2457600 | tf_op jit(solution)/shard_map/reduce_scatter | solution.py:1242
  377.0 50.5 %collective-permute-start.49 = (bf16[512,1024]{1,0:T(8,128)(2,1)S(1)}, bf16[512,1024]{1,0:T(8,128)(2,1)}, u32[]{:S(2)}, u32[]{:S(2)}) collective-permute-start(bf16[512,1024]{1,0:T(8,128)(2,1)S(1)} %shard_map.374.refs_19_), channel_id=1, source_target_pairs={{0,4},{4,0},{8,12},{12,8},{16,20},{20,16},{24,28},{28,24},{1,5},{5... | collective-permute-start | bytes 3145736 | tf_op jit(solution)/shard_map/ppermute | solution.py:723
  377.1 40.7 %collective-permute-start.47 = (bf16[128,2048]{1,0:T(8,128)(2,1)S(1)}, bf16[128,2048]{1,0:T(8,128)(2,1)S(1)}, u32[]{:S(2)}, u32[]{:S(2)}) collective-permute-start(bf16[128,2048]{1,0:T(8,128)(2,1)S(1)} %copy-done.17), channel_id=1, source_target_pairs={{0,8},{4,12},{8,0},{12,4},{16,24},{20,28},{24,16},{28,20},{1,9},{5... | collective-permute-start | bytes 1572872 | tf_op jit(solution)/shard_map/ppermute | solution.py:723
  377.8 40.0 %collective-permute-start.45 = (bf16[64,4096]{1,0:T(8,128)(2,1)S(1)}, bf16[64,4096]{1,0:T(8,128)(2,1)S(1)}, u32[]{:S(2)}, u32[]{:S(2)}) collective-permute-start(bf16[64,4096]{1,0:T(8,128)(2,1)S(1)} %copy-done.19), channel_id=1, source_target_pairs={{0,8},{4,12},{8,0},{12,4},{16,24},{20,28},{24,16},{28,20},{1,9},{5... | collective-permute-start | bytes 1572872 | tf_op jit(solution)/shard_map/ppermute | solution.py:723
  379.2 38.6 %collective-permute-start.46 = (bf16[64,4096]{1,0:T(8,128)(2,1)S(1)}, bf16[64,4096]{1,0:T(8,128)(2,1)S(1)}, u32[]{:S(2)}, u32[]{:S(2)}) collective-permute-start(bf16[64,4096]{1,0:T(8,128)(2,1)S(1)} %copy-done.70), channel_id=1, source_target_pairs={{0,16},{4,20},{8,24},{12,28},{16,0},{20,4},{24,8},{28,12},{1,17},{... | collective-permute-start | bytes 1572872 | tf_op jit(solution)/shard_map/ppermute | solution.py:723
  380.6 37.3 %collective-permute-start.48 = (bf16[128,1536]{1,0:T(8,128)(2,1)S(1)}, bf16[128,1536]{1,0:T(8,128)(2,1)S(1)}, u32[]{:S(2)}, u32[]{:S(2)}) collective-permute-start(bf16[128,1536]{1,0:T(8,128)(2,1)S(1)} %get-tuple-element.185.refs_12_.refs_18_), channel_id=1, source_target_pairs={{0,16},{4,20},{8,24},{12,28},{16,0},{20,4},{24,8},{28,12},{1,17},{... | collective-permute-start | bytes 1179656 | tf_op jit(solution)/shard_map/ppermute | solution.py:723
  422.9 119.4 %reduce-scatter.6.cloned.1.call-start = ((), (), s32[]{:S(2)}) async-start(), calls=%async_computation.4 | async-start | bytes 983040 | tf_op jit(solution)/shard_map/reduce_scatter | solution.py:1242
  450.1 29.4 %collective-permute-start.54 = (bf16[128,2048]{1,0:T(8,128)(2,1)S(1)}, bf16[128,2048]{1,0:T(8,128)(2,1)}, u32[]{:S(2)}, u32[]{:S(2)}) collective-permute-start(bf16[128,2048]{1,0:T(8,128)(2,1)S(1)} %get-tuple-element.199.refs_5_.refs_4_), channel_id=1, source_target_pairs={{0,16},{4,20},{8,24},{12,28},{16,0},{20,4},{24,8},{28,12},{1,17},{... | collective-permute-start | bytes 1572872 | tf_op jit(solution)/shard_map/ppermute | solution.py:723
  451.3 28.2 %collective-permute-start.55 = (bf16[128,2048]{1,0:T(8,128)(2,1)}, bf16[128,2048]{1,0:T(8,128)(2,1)}, u32[]{:S(2)}, u32[]{:S(2)}) collective-permute-start(bf16[128,2048]{1,0:T(8,128)(2,1)} %get-tuple-element.201.refs_7_.refs_6_), channel_id=1, source_target_pairs={{0,8},{4,12},{8,0},{12,4},{16,24},{20,28},{24,16},{28,20},{1,9},{5... | collective-permute-start | bytes 1572872 | tf_op jit(solution)/shard_map/ppermute | solution.py:723
  451.9 18.1 %collective-permute-start.51 = (bf16[128,1024]{1,0:T(8,128)(2,1)S(1)}, bf16[128,1024]{1,0:T(8,128)(2,1)S(1)}, u32[]{:S(2)}, u32[]{:S(2)}) collective-permute-start(bf16[128,1024]{1,0:T(8,128)(2,1)S(1)} %get-tuple-element.195.refs_3_), channel_id=1, source_target_pairs={{0,16},{4,20},{8,24},{12,28},{16,0},{20,4},{24,8},{28,12},{1,17},{... | collective-permute-start | bytes 786440 | tf_op jit(solution)/shard_map/ppermute | solution.py:723
  452.6 18.5 %collective-permute-start.52 = (bf16[128,1024]{1,0:T(8,128)(2,1)S(1)}, bf16[128,1024]{1,0:T(8,128)(2,1)S(1)}, u32[]{:S(2)}, u32[]{:S(2)}) collective-permute-start(bf16[128,1024]{1,0:T(8,128)(2,1)S(1)} %get-tuple-element.197.refs_5_), channel_id=1, source_target_pairs={{0,8},{4,12},{8,0},{12,4},{16,24},{20,28},{24,16},{28,20},{1,9},{5... | collective-permute-start | bytes 786440 | tf_op jit(solution)/shard_map/ppermute | solution.py:723
  (152 other events, 1220.1 us)
Sparse Core Ops, SparseCore 0:
  23.0 58.1 all-gather.2
  333.3 23.9 reduce-scatter.7
  423.0 43.7 reduce-scatter.3
  518.0 24.2 reduce-scatter.5

commit v4 on v3

--- a/solution.py
+++ b/solution.py
@@ -1638,13 +1638,13 @@
     (grad_a,) = times_transposed([dgate, qk_low], in_a, [wide_f32], store, deps=val_send)
     val_sum = collect_keep(ext_in, low_v, val_got, grad_a)
     val_got = collect_move(val_sum, 0)
+    (grad_b,) = times_transposed(
+        [low_v], in_b, [shape((ext, model), f32)], store, deps=val_sum
+    )
+    val_sum = collect_add(val_sum, val_got, grad_b)
+    val_got = collect_move(val_sum, 1)
     qk_sum = collect_add(qk_sum, qk_got, val_sum)
     qk_got = collect_move(qk_sum, 1)
-    (grad_b,) = times_transposed(
-        [low_v], in_b, [shape((ext, model), f32)], store, deps=(val_sum, qk_sum)
-    )
-    val_sum = collect_add(val_sum, val_got, grad_b)
-    val_got = collect_move(val_sum, 1)
     late_rows = lax.ppermute(grad_b[:HALO], "tensor", backward)
     residual_grad, gain_sums = call(
         first_back_kernel,
@@ -1655,7 +1655,7 @@
         ],
         [whole(rows, model), whole(8, model)],
         [wide_f32, shape((8, model), f32)],
-        deps=val_sum,
+        deps=(val_sum, qk_sum),
     )(
         grad_a, grad_b, late_rows, ext_low[HALO:], middle_grad, gain_first[None, :], mlp_gain_part
     )

time: 561 us -> 547 us (0.975)
  waiting for transfers between devices: 91.5 us -> 75.9 us
    ppermute x51, waiting for transfers between devices: 60.2 us -> 48.2 us  [partner(): return lax.ppermute(value, 'dp', [(i, i ^ 1 << bit) for i in range(count)])]
    unnamed x244 -> x252, local copies, waits for them, and re-layouts: 39.6 us -> 38.3 us
  transfers between devices with their start and end apart: 69 -> 69, of which waited for: 25 -> 25; matrix products, arithmetic and copies ran while one was open for 6% -> 6% of each run, Pallas kernels for 50% -> 52%
where the time goes in v4:
time: 547 us; the launch traced here: 540 us
  Pallas kernels  311 us (57%)
  waiting for transfers between devices  75.9 us (14%)
  starting transfers between devices  66.1 us (12%)
  local copies, waits for them, and re-layouts  62.7 us (11%)
  between operations  15.7 us (3%)
  other arithmetic  9.16 us (2%)
    pallas_call x55, Pallas kernels, call(): return lambda *args: run(*args, *late)  296 us
    ppermute x51, waiting for transfers between devices, partner(): return lax.ppermute(value, 'dp', [(i, i ^ 1 << bit) for i in range(count)])  48.2 us
    ppermute x51, starting transfers between devices, partner(): return lax.ppermute(value, 'dp', [(i, i ^ 1 << bit) for i in range(count)])  42.9 us
    unnamed x252, local copies, waits for them, and re-layouts  38.3 us
    pallas_call x2, Pallas kernels, restore_all(): pl.pallas_call(kernel, grid_spec=pltpu.PrefetchScalarGridSpec(num_scalar_...  14.5 us
  transfers between devices with their start and end apart: 69, of which 25 were waited for; matrix products, arithmetic and copies ran while one was open for 6% of the time, Pallas kernels for 52%

profile of v4, /device:TPU:0, one launch (start us, length us, event | category | flops | bytes accessed | tf_op | source)
XLA Modules:
  0.0 540.1 jit_solution(17088303984605099314)
XLA Ops:
  53.5 9.4 %collective-permute-done.6.refs_1_ = bf16[4,128,512]{2,1,0:T(8,128)(2,1)S(1)} collective-permute-done((bf16[4,128,512]{2,1,0:T(8,128)(2,1)S(1)}, bf16[4,128,512]{2,1,0:T(8,128)(2,1)S(1)}, u32[]{:S(2)}, u32[]{:S(2)}) %collective-permute-start.6) | collective-permute-done | bytes 524320 | tf_op jit(solution)/shard_map/ppermute | solution.py:723
  69.7 4.3 collective-permute-done.8.refs_2_
  75.4 6.0 %shard_map.334.refs_0_.refs_1_.refs_2_.refs_3_ = f32[528,2048]{1,0:T(8,128)} custom-call(bf16[528,1024]{1,0:T(8,128)(2,1)S(1)} %copy-done, bf16[4,512,512]{2,1,0:T(8,128)(2,1)} %shard_map.333.refs_1_, bf16[4,512,512]{2,1,0:T(8,128)(2,1)} %copy-done.73), custom_call_target="tpu_custom_call" | custom-call | flops 1 | bytes 1 | tf_op jit(solution)/shard_map/pallas_call | solution.py:54
  91.1 8.7 %collective-permute-done.10.refs_3_ = bf16[4,64,640]{2,1,0:T(8,128)(2,1)S(1)} collective-permute-done((bf16[4,64,640]{2,1,0:T(8,128)(2,1)S(1)}, bf16[4,64,640]{2,1,0:T(8,128)(2,1)S(1)}, u32[]{:S(2)}, u32[]{:S(2)}) %collective-permute-start.10) | collective-permute-done | bytes 327712 | tf_op jit(solution)/shard_map/ppermute | solution.py:723
  110.5 12.9 %shard_map.339 = (f32[512,1536]{1,0:T(8,128)}, bf16[128,1536]{1,0:T(8,128)(2,1)S(1)}, bf16[512,256]{1,0:T(8,128)(2,1)S(1)}) custom-call(f32[528,2048]{1,0:T(8,128)} %shard_map.334.refs_0_.refs_1_.refs_2_.refs_3_, f32[528,256]{1,0:T(8,128)S(1)} %copy-done.33, f32[4,1792]{1,0:T(4,128)S(1)} %copy-done.50, f32[4,1792]{1,0:T(4,128)S(1)} %copy-done.50, ...), custom_call_target="tpu_custom_call" | custom-call | flops 1 | bytes 1 | tf_op jit(solution)/shard_map/pallas_call | solution.py:54
  138.2 7.6 %shard_map.342.refs_0_.refs_1_.refs_2_.refs_3_.refs_8_ = f32[512,2560]{1,0:T(8,128)} custom-call(bf16[512,1024]{1,0:T(8,128)(2,1)} %slice.118.refs_0_, bf16[4,512,640]{2,1,0:T(8,128)(2,1)} %get-tuple-element.134.refs_1_.refs_2_, bf16[4,512,640]{2,1,0:T(8,128)(2,1)} %copy-done.71, bf16[4,64,1024]{2,1,0:T(8,128)(2,1)S(1)} %get-tuple-element.135.refs_3_.refs_4_, ...), custom_call_target="tpu_custom_call" | custom-call | flops 1 | bytes 1 | tf_op jit(solution)/shard_map/pallas_call | solution.py:54
  146.6 10.5 %collective-permute-done.18.refs_1_ = bf16[4,128,512]{2,1,0:T(8,128)(2,1)S(1)} collective-permute-done((bf16[4,128,512]{2,1,0:T(8,128)(2,1)S(1)}, bf16[4,128,512]{2,1,0:T(8,128)(2,1)S(1)}, u32[]{:S(2)}, u32[]{:S(2)}) %collective-permute-start.18) | collective-permute-done | bytes 524320 | tf_op jit(solution)/shard_map/ppermute | solution.py:723
  157.9 4.4 shard_map.344
  167.9 5.6 %collective-permute-done.17.refs_4_ = bf16[512,256]{1,0:T(8,128)(2,1)S(1)} collective-permute-done((bf16[512,256]{1,0:T(8,128)(2,1)S(1)}, bf16[512,256]{1,0:T(8,128)(2,1)S(1)}, u32[]{:S(2)}, u32[]{:S(2)}) %collective-permute-start.17) | collective-permute-done | bytes 262176 | tf_op jit(solution)/shard_map/ppermute | solution.py:1392
  173.5 9.8 %shard_map.345.refs_1_.refs_6_ = bf16[512,512]{1,0:T(8,128)(2,1)S(1)} custom-call(s32[1]{0:T(128)} %bitcast.9.refs_0_, f32[512,2560]{1,0:T(8,128)} %shard_map.342.refs_0_.refs_1_.refs_2_.refs_3_.refs_8_, f32[512,128]{1,0:T(8,128)S(1)} %get-tuple-element.299.refs_6_.refs_2_, f32[512,128]{1,0:T(8,128)S(1)} %get-tuple-element.360.refs_7_.refs_3_, ...), custom_call_target="tpu_custom_call" | custom-call | flops 1 | bytes 1 | tf_op jit(solution)/shard_map/pallas_call | solution.py:54
  187.1 7.1 %shard_map.347 = (f32[512,1536]{1,0:T(8,128)}, bf16[512,2048]{1,0:T(8,128)(2,1)}) custom-call(f32[512,1536]{1,0:T(8,128)} %get-tuple-element.133.refs_8_.refs_0_, f32[512,2560]{1,0:T(8,128)} %shard_map.342.refs_0_.refs_1_.refs_2_.refs_3_.refs_8_, bf16[512,256]{1,0:T(8,128)(2,1)S(1)} %get-tuple-element.137.refs_2_.refs_3_.refs_7_, f32[512,128]{1,0:T(8,128)S(1)} %copy-done.46, ...), custom_call_target="tpu_custom_call" | custom-call | flops 1 | bytes 1 | tf_op jit(solution)/shard_map/pallas_call | solution.py:54
  195.7 4.4 shard_map.348.refs_5_.refs_1_
  202.3 8.2 %shard_map.349 = (f32[512,1024]{1,0:T(8,128)}, bf16[512,1024]{1,0:T(8,128)(2,1)S(1)}) custom-call(bf16[512,2048]{1,0:T(8,128)(2,1)} %get-tuple-element.147.refs_4_.refs_0_.refs_1_, bf16[4,512,512]{2,1,0:T(8,128)(2,1)} %get-tuple-element.144.refs_2_.refs_1_, bf16[4,512,512]{2,1,0:T(8,128)(2,1)} %copy-done.70, ...), custom_call_target="tpu_custom_call" | custom-call | flops 1 | bytes 1 | tf_op jit(solution)/shard_map/pallas_call | solution.py:54
  216.1 9.8 %shard_map.351 = (bf16[512,2048]{1,0:T(8,128)(2,1)}, bf16[512,2048]{1,0:T(8,128)(2,1)}, bf16[512,2048]{1,0:T(8,128)(2,1)}) custom-call(bf16[512,1024]{1,0:T(8,128)(2,1)} %copy-done.7, bf16[4,512,1024]{2,1,0:T(8,128)(2,1)} %shard_map.348.refs_5_.refs_1_, bf16[4,512,1024]{2,1,0:T(8,128)(2,1)} %collective-permute-done.25.refs_2_, ...), custom_call_target="tpu_custom_call" | custom-call | flops 1 | bytes 1 | tf_op jit(solution)/shard_map/pallas_call | solution.py:54
  237.4 7.2 %shard_map.354.refs_3_.refs_1_.refs_0_ = bf16[512,4096]{1,0:T(8,128)(2,1)} custom-call(bf16[512,1024]{1,0:T(8,128)(2,1)S(1)} %copy-done.2, bf16[4,512,512]{2,1,0:T(8,128)(2,1)} %shard_map.352.refs_2_.refs_1_, bf16[4,512,512]{2,1,0:T(8,128)(2,1)} %copy-done.72, bf16[512,2048]{1,0:T(8,128)(2,1)} %get-tuple-element.153.refs_3_, ...), custom_call_target="tpu_custom_call" | custom-call | flops 1 | bytes 1 | tf_op jit(solution)/shard_map/pallas_call | solution.py:54
  250.0 6.5 %shard_map.356.refs_6_ = bf16[512,4096]{1,0:T(8,128)(2,1)} custom-call(bf16[512,1024]{1,0:T(8,128)(2,1)} %copy-done.7, bf16[512,4096]{1,0:T(8,128)(2,1)} %shard_map.354.refs_3_.refs_1_.refs_0_, bf16[128,2048]{1,0:T(8,128)(2,1)S(1)} %get-tuple-element.155.refs_2_.refs_7_.refs_0_, bf16[128,2048]{1,0:T(8,128)(2,1)S(1)} %get-tuple-element.156.refs_3_.refs_8_, ...), custom_call_target="tpu_custom_call" | custom-call | flops 1 | bytes 1 | tf_op jit(solution)/shard_map/pallas_call | solution.py:54
  259.3 12.1 %shard_map.357 = (f32[512,1024]{1,0:T(8,128)}, bf16[512,1024]{1,0:T(8,128)(2,1)}, f32[1,1024]{1,0:T(1,128)S(1)}) custom-call(bf16[512,4096]{1,0:T(8,128)(2,1)} %shard_map.354.refs_3_.refs_1_.refs_0_, bf16[4,512,1024]{2,1,0:T(8,128)(2,1)} %shard_map.348.refs_5_.refs_1_, bf16[4,512,1024]{2,1,0:T(8,128)(2,1)} %collective-permute-done.25.refs_2_, ...), custom_call_target="tpu_custom_call" | custom-call | flops 1 | bytes 1 | tf_op jit(solution)/shard_map/pallas_call | solution.py:54
  274.3 6.5 %shard_map.359.refs_2_.refs_0_.refs_6_ = f32[512,2048]{1,0:T(8,128)} custom-call(bf16[512,1024]{1,0:T(8,128)(2,1)} %get-tuple-element.159.refs_4_.refs_0_, bf16[4,512,512]{2,1,0:T(8,128)(2,1)} %get-tuple-element.144.refs_2_.refs_1_, bf16[4,512,512]{2,1,0:T(8,128)(2,1)} %copy-done.70, bf16[64,2048]{1,0:T(8,128)(2,1)S(1)} %get-tuple-element.160.refs_3_.refs_0_, ...), custom_call_target="tpu_custom_call" | custom-call | flops 1 | bytes 1 | tf_op jit(solution)/shard_map/pallas_call | solution.py:54
  288.6 7.0 %shard_map.361 = (bf16[128,4096]{1,0:T(8,128)(2,1)S(1)}, bf16[128,4096]{1,0:T(8,128)(2,1)}, bf16[128,4096]{1,0:T(8,128)(2,1)}, bf16[128,4096]{1,0:T(8,128)(2,1)}) custom-call(bf16[512,1024]{1,0:T(8,128)(2,1)} %copy-done.7, bf16[512,4096]{1,0:T(8,128)(2,1)} %shard_map.354.refs_3_.refs_1_.refs_0_, bf16[512,4096]{1,0:T(8,128)(2,1)} %copy-done.76, ...), custom_call_target="tpu_custom_call" | custom-call | flops 1 | bytes 1 | tf_op jit(solution)/shard_map/pallas_call | solution.py:54
  296.6 9.3 %shard_map.362 = (bf16[512,1536]{1,0:T(8,128)(2,1)}, f32[512,1536]{1,0:T(8,128)}, f32[1,1536]{1,0:T(1,128)S(1)}, f32[128,1536]{1,0:T(8,128)S(1)}) custom-call(f32[512,2048]{1,0:T(8,128)} %shard_map.359.refs_2_.refs_0_.refs_6_, f32[512,1536]{1,0:T(8,128)} %get-tuple-element.164.refs_1_, f32[512,2560]{1,0:T(8,128)} %shard_map.342.refs_0_.refs_1_.refs_2_.refs_3_.refs_8_, ...), custom_call_target="tpu_custom_call" | custom-call | flops 1 | bytes 1 | tf_op jit(solution)/shard_map/pallas_call | solution.py:54
  319.6 8.0 %shard_map.366.refs_3_.refs_0_.refs_1_ = f32[512,1024]{1,0:T(8,128)} custom-call(bf16[512,2048]{1,0:T(8,128)(2,1)} %get-tuple-element.152.refs_4_.refs_1_.refs_0_, bf16[4,512,512]{2,1,0:T(8,128)(2,1)} %shard_map.352.refs_2_.refs_1_, bf16[4,512,512]{2,1,0:T(8,128)(2,1)} %copy-done.72, f32[512,1024]{1,0:T(8,128)} %get-tuple-element.149.refs_4_.refs_3_, ...), custom_call_target="tpu_custom_call" | custom-call | flops 1 | bytes 1 | tf_op jit(solution)/shard_map/pallas_call | solution.py:54
  333.9 7.3 %shard_map.368.refs_11_ = f32[512,1024]{1,0:T(8,128)} custom-call(s32[32]{0:T(128)S(1)} %reshape.104.table_ref, f32[512,1024]{1,0:T(8,128)} %shard_map.366.refs_3_.refs_0_.refs_1_, f32[512,1024]{1,0:T(8,128)} %shard_map.366.refs_3_.refs_0_.refs_1_, bf16[256,1536]{1,0:T(8,128)(2,1)S(1)} %get-tuple-element.173.refs_2_.refs_9_.refs_0_, ...), custom_call_target="tpu_custom_call" | custom-call | flops 1 | bytes 1 | tf_op jit(solution)/shard_map/pallas_call | solution.py:1160
  341.3 18.7 %shard_map.369 = (bf16[512,1024]{1,0:T(8,128)(2,1)}, f32[512,256]{1,0:T(8,128)S(1)}, f32[512,256]{1,0:T(8,128)}) custom-call(s32[1]{0:T(128)} %bitcast.9.refs_0_, f32[512,2560]{1,0:T(8,128)} %shard_map.342.refs_0_.refs_1_.refs_2_.refs_3_.refs_8_, f32[512,128]{1,0:T(8,128)S(1)} %get-tuple-element.299.refs_6_.refs_2_, ...), custom_call_target="tpu_custom_call" | custom-call | flops 1 | bytes 1 | tf_op jit(solution)/shard_map/pallas_call | solution.py:54
  361.4 4.3 shard_map.370
  381.3 36.6 %shard_map.375 = (bf16[528,2048]{1,0:T(8,128)(2,1)}, f32[528,256]{1,0:T(8,128)}, f32[4,512,128]{2,1,0:T(8,128)}, f32[4,8,512]{2,1,0:T(8,128)S(1)}, f32[4,1536]{1...) custom-call(f32[528,2048]{1,0:T(8,128)} %shard_map.334.refs_0_.refs_1_.refs_2_.refs_3_, ...), custom_call_target="tpu_custom_call" | custom-call | flops 1 | bytes 1 | tf_op jit(solution)/shard_map/pallas_call | solution.py:54
  430.6 4.6 shard_map.379.refs_4_
  435.2 7.9 %shard_map.380.refs_3_.refs_0_ = f32[512,1024]{1,0:T(8,128)} custom-call(bf16[512,1536]{1,0:T(8,128)(2,1)} %get-tuple-element.169.refs_4_.refs_1_.refs_0_, bf16[512,1024]{1,0:T(8,128)(2,1)S(1)} %copy-done.3, bf16[4,512,640]{2,1,0:T(8,128)(2,1)} %get-tuple-element.134.refs_1_.refs_2_, bf16[4,512,640]{2,1,0:T(8,128)(2,1)} %copy-done.71, ...), custom_call_target="tpu_custom_call" | custom-call | flops 1 | bytes 1 | tf_op jit(solution)/shard_map/pallas_call | solution.py:54
  444.5 4.6 shard_map.381
  453.4 7.2 %shard_map.382.refs_4_.refs_1_ = f32[528,1024]{1,0:T(8,128)} custom-call(bf16[528,2048]{1,0:T(8,128)(2,1)} %get-tuple-element.193.refs_1_.refs_0_, bf16[4,512,512]{2,1,0:T(8,128)(2,1)} %shard_map.333.refs_1_, bf16[4,512,512]{2,1,0:T(8,128)(2,1)} %copy-done.73, bf16[128,2048]{1,0:T(8,128)(2,1)S(1)} %get-tuple-element.198.refs_3_.refs_0_, ...), custom_call_target="tpu_custom_call" | custom-call | flops 1 | bytes 1 | tf_op jit(solution)/shard_map/pallas_call | solution.py:54
  476.8 5.7 %shard_map.385 = (f32[512,1024]{1,0:T(8,128)}, f32[8,1024]{1,0:T(8,128)S(1)}) custom-call(f32[512,1024]{1,0:T(8,128)} %shard_map.380.refs_3_.refs_0_, f32[528,1024]{1,0:T(8,128)} %shard_map.382.refs_4_.refs_1_, f32[16,1024]{1,0:T(8,128)S(1)} %collective-permute-done.51.refs_2_, bf16[512,1024]{1,0:T(8,128)(2,1)} %get-tuple-element.258.refs_3_, ...), custom_call_target="tpu_custom_call" | custom-call | flops 1 | bytes 1 | tf_op jit(solution)/shard_map/pallas_call | solution.py:54
  485.4 7.3 %shard_map.387 = (f32[512,1024]{1,0:T(8,128)}, f32[8,1024]{1,0:T(8,128)S(1)}) custom-call(s32[32]{0:T(128)S(1)} %copy-done.65, f32[512,1024]{1,0:T(8,128)} %get-tuple-element.212.refs_8_.refs_0_.refs_1_, f32[512,1024]{1,0:T(8,128)} %get-tuple-element.212.refs_8_.refs_0_.refs_1_, f32[8,1024]{1,0:T(8,128)S(1)} %get-tuple-element.213.refs_2_.refs_3_, ...), custom_call_target="tpu_custom_call" | custom-call | flops 1 | bytes 1 | tf_op jit(solution)/shard_map/pallas_call | solution.py:1160
  518.8 9.4 %reduce-scatter.6.cloned.1.call-done = bf16[1,128,768]{2,1,0:T(8,128)(2,1)} async-done(((bf16[4,128,768]{2,1,0:T(8,128)(2,1)}), bf16[1,128,768]{2,1,0:T(8,128)(2,1)}) %reduce-scatter.6.cloned.1.call-update) | async-done | bytes 196624 | tf_op jit(solution)/shard_map/reduce_scatter | solution.py:1242
  (494 shorter events, 245.7 us)
Async XLA Ops:
  7.2 78.8 %all-gather.3.cloned.1.call-start = ((), (), s32[]{:S(2)}) async-start(), calls=%async_computation.6 | async-start | bytes 3440640 | tf_op jit(solution)/shard_map/all_gather | solution.py:1193
  10.6 31.0 %collective-permute-start.1 = (bf16[128,512]{1,0:T(8,128)(2,1)S(1)}, bf16[128,512]{1,0:T(8,128)(2,1)S(1)}, u32[]{:S(2)}, u32[]{:S(2)}) collective-permute-start(bf16[128,512]{1,0:T(8,128)(2,1)S(1)} %maximum_maximum_fusion.refs_1_), channel_id=1, source_target_pairs={{0,1},{1,0},{2,3},{3,2},{4,5},{5,4},{6,7},{7,6},{8,9},{9,8},{10,11... | collective-permute-start | bytes 393224 | tf_op jit(solution)/shard_map/ppermute | solution.py:768
  13.7 27.9 %collective-permute-start.2 = (bf16[128,512]{1,0:T(8,128)(2,1)S(1)}, bf16[128,512]{1,0:T(8,128)(2,1)S(1)}, u32[]{:S(2)}, u32[]{:S(2)}) collective-permute-start(bf16[128,512]{1,0:T(8,128)(2,1)S(1)} %maximum_maximum_fusion.refs_1_), channel_id=1, source_target_pairs={{0,2},{1,3},{2,0},{3,1},{4,6},{5,7},{6,4},{7,5},{8,10},{9,11},{10,... | collective-permute-start | bytes 393224 | tf_op jit(solution)/shard_map/ppermute | solution.py:768
  16.2 25.3 %collective-permute-start.3 = (bf16[128,512]{1,0:T(8,128)(2,1)S(1)}, bf16[128,512]{1,0:T(8,128)(2,1)S(1)}, u32[]{:S(2)}, u32[]{:S(2)}) collective-permute-start(bf16[128,512]{1,0:T(8,128)(2,1)S(1)} %maximum_maximum_fusion.refs_1_), channel_id=1, source_target_pairs={{0,3},{1,2},{2,1},{3,0},{4,7},{5,6},{6,5},{7,4},{8,11},{9,10},{10,... | collective-permute-start | bytes 393224 | tf_op jit(solution)/shard_map/ppermute | solution.py:768
  22.9 486.9 %reduce-scatter.8.cloned.1.call-start = ((), (), s32[]{:S(2)}) async-start(), calls=%async_computation.5 | async-start | bytes 655360 | tf_op jit(solution)/shard_map/reduce_scatter | solution.py:1242
  101.5 22.8 %collective-permute-start.11 = (bf16[4,128,640]{2,1,0:T(8,128)(2,1)S(1)}, bf16[4,128,640]{2,1,0:T(8,128)(2,1)}, u32[]{:S(2)}, u32[]{:S(2)}) collective-permute-start(bf16[4,128,640]{2,1,0:T(8,128)(2,1)S(1)} %get-tuple-element.129.refs_1_.refs_7_.refs_0_), channel_id=1, source_target_pairs={{0,16},{4,20},{8,24},{12,28},{16,0},{20,4},{24,8},{28,12},{1,17},{... | collective-permute-start | bytes 1966088 | tf_op jit(solution)/shard_map/ppermute | solution.py:723
  103.0 21.3 %collective-permute-start.12 = (bf16[4,128,640]{2,1,0:T(8,128)(2,1)}, bf16[4,128,640]{2,1,0:T(8,128)(2,1)}, u32[]{:S(2)}, u32[]{:S(2)}) collective-permute-start(bf16[4,128,640]{2,1,0:T(8,128)(2,1)} %get-tuple-element.130.refs_2_.refs_8_), channel_id=1, source_target_pairs={{0,8},{4,12},{8,0},{12,4},{16,24},{20,28},{24,16},{28,20},{1,9},{5... | collective-permute-start | bytes 1966088 | tf_op jit(solution)/shard_map/ppermute | solution.py:723
  107.2 17.1 %collective-permute-start.13 = (bf16[4,64,512]{2,1,0:T(8,128)(2,1)S(1)}, bf16[4,64,512]{2,1,0:T(8,128)(2,1)}, u32[]{:S(2)}, u32[]{:S(2)}) collective-permute-start(bf16[4,64,512]{2,1,0:T(8,128)(2,1)S(1)} %get-tuple-element.131.refs_9_.refs_4_), channel_id=1, source_target_pairs={{0,8},{4,12},{8,0},{12,4},{16,24},{20,28},{24,16},{28,20},{1,9},{5... | collective-permute-start | bytes 786440 | tf_op jit(solution)/shard_map/ppermute | solution.py:723
  132.5 24.6 %collective-permute-start.18 = (bf16[4,128,512]{2,1,0:T(8,128)(2,1)S(1)}, bf16[4,128,512]{2,1,0:T(8,128)(2,1)S(1)}, u32[]{:S(2)}, u32[]{:S(2)}) collective-permute-start(bf16[4,128,512]{2,1,0:T(8,128)(2,1)S(1)} %get-tuple-element.140.refs_0_), channel_id=1, source_target_pairs={{0,16},{4,20},{8,24},{12,28},{16,0},{20,4},{24,8},{28,12},{1,17},{... | collective-permute-start | bytes 1572872 | tf_op jit(solution)/shard_map/ppermute | solution.py:723
  133.9 23.2 %collective-permute-start.19 = (bf16[4,128,512]{2,1,0:T(8,128)(2,1)S(1)}, bf16[4,128,512]{2,1,0:T(8,128)(2,1)S(1)}, u32[]{:S(2)}, u32[]{:S(2)}) collective-permute-start(bf16[4,128,512]{2,1,0:T(8,128)(2,1)S(1)} %copy-done.48), channel_id=1, source_target_pairs={{0,8},{4,12},{8,0},{12,4},{16,24},{20,28},{24,16},{28,20},{1,9},{5... | collective-permute-start | bytes 1572872 | tf_op jit(solution)/shard_map/ppermute | solution.py:723
  162.3 21.0 %collective-permute-start.22 = (bf16[4,512,512]{2,1,0:T(8,128)(2,1)}, bf16[4,512,512]{2,1,0:T(8,128)(2,1)S(1)}, u32[]{:S(2)}, u32[]{:S(2)}) collective-permute-start(bf16[4,512,512]{2,1,0:T(8,128)(2,1)} %get-tuple-element.144.refs_2_.refs_1_), channel_id=1, source_target_pairs={{0,4},{4,0},{8,12},{12,8},{16,20},{20,16},{24,28},{28,24},{1,5},{5... | collective-permute-start | bytes 6291464 | tf_op jit(solution)/shard_map/ppermute | solution.py:723
  162.3 31.9 %collective-permute-start.23 = (bf16[4,128,1024]{2,1,0:T(8,128)(2,1)}, bf16[4,128,1024]{2,1,0:T(8,128)(2,1)S(1)}, u32[]{:S(2)}, u32[]{:S(2)}) collective-permute-start(bf16[4,128,1024]{2,1,0:T(8,128)(2,1)} %get-tuple-element.142.refs_6_.refs_0_), channel_id=1, source_target_pairs={{0,16},{4,20},{8,24},{12,28},{16,0},{20,4},{24,8},{28,12},{1,17},{... | collective-permute-start | bytes 3145736 | tf_op jit(solution)/shard_map/ppermute | solution.py:723
  163.0 31.2 %collective-permute-start.24 = (bf16[4,128,1024]{2,1,0:T(8,128)(2,1)}, bf16[4,128,1024]{2,1,0:T(8,128)(2,1)S(1)}, u32[]{:S(2)}, u32[]{:S(2)}) collective-permute-start(bf16[4,128,1024]{2,1,0:T(8,128)(2,1)} %get-tuple-element.143.refs_7_.refs_2_), channel_id=1, source_target_pairs={{0,8},{4,12},{8,0},{12,4},{16,24},{20,28},{24,16},{28,20},{1,9},{5... | collective-permute-start | bytes 3145736 | tf_op jit(solution)/shard_map/ppermute | solution.py:723
  256.5 30.2 %collective-permute-start.35 = (bf16[512,4096]{1,0:T(8,128)(2,1)}, bf16[512,4096]{1,0:T(8,128)(2,1)S(1)}, u32[]{:S(2)}, u32[]{:S(2)}) collective-permute-start(bf16[512,4096]{1,0:T(8,128)(2,1)} %shard_map.356.refs_6_), channel_id=1, source_target_pairs={{0,4},{4,0},{8,12},{12,8},{16,20},{20,16},{24,28},{28,24},{1,5},{5... | collective-permute-start | bytes 12582920 | tf_op jit(solution)/shard_map/ppermute | solution.py:723
  284.6 30.3 %collective-permute-start.34 = (bf16[512,2048]{1,0:T(8,128)(2,1)}, bf16[512,2048]{1,0:T(8,128)(2,1)}, u32[]{:S(2)}, u32[]{:S(2)}) collective-permute-start(bf16[512,2048]{1,0:T(8,128)(2,1)} %shard_map.360.refs_3_.refs_6_), channel_id=1, source_target_pairs={{0,4},{4,0},{8,12},{12,8},{16,20},{20,16},{24,28},{28,24},{1,5},{5... | collective-permute-start | bytes 6291464 | tf_op jit(solution)/shard_map/ppermute | solution.py:723
  284.6 22.0 %collective-permute-start.36 = (bf16[64,2048]{1,0:T(8,128)(2,1)S(1)}, bf16[64,2048]{1,0:T(8,128)(2,1)S(1)}, u32[]{:S(2)}, u32[]{:S(2)}) collective-permute-start(bf16[64,2048]{1,0:T(8,128)(2,1)S(1)} %get-tuple-element.161.refs_4_), channel_id=1, source_target_pairs={{0,8},{4,12},{8,0},{12,4},{16,24},{20,28},{24,16},{28,20},{1,9},{5... | collective-permute-start | bytes 786440 | tf_op jit(solution)/shard_map/ppermute | solution.py:723
  286.0 20.6 %collective-permute-start.37 = (bf16[64,2048]{1,0:T(8,128)(2,1)S(1)}, bf16[64,2048]{1,0:T(8,128)(2,1)S(1)}, u32[]{:S(2)}, u32[]{:S(2)}) collective-permute-start(bf16[64,2048]{1,0:T(8,128)(2,1)S(1)} %get-tuple-element.163.refs_6_), channel_id=1, source_target_pairs={{0,16},{4,20},{8,24},{12,28},{16,0},{20,4},{24,8},{28,12},{1,17},{... | collective-permute-start | bytes 786440 | tf_op jit(solution)/shard_map/ppermute | solution.py:723
  311.5 16.2 %collective-permute-start.38 = (bf16[512,1536]{1,0:T(8,128)(2,1)}, bf16[512,1536]{1,0:T(8,128)(2,1)S(1)}, u32[]{:S(2)}, u32[]{:S(2)}) collective-permute-start(bf16[512,1536]{1,0:T(8,128)(2,1)} %shard_map.364.refs_3_), channel_id=1, source_target_pairs={{0,4},{4,0},{8,12},{12,8},{16,20},{20,16},{24,28},{28,24},{1,5},{5... | collective-permute-start | bytes 4718600 | tf_op jit(solution)/shard_map/ppermute | solution.py:723
  311.5 16.1 %collective-permute-start.39 = (bf16[128,1536]{1,0:T(8,128)(2,1)S(1)}, bf16[128,1536]{1,0:T(8,128)(2,1)S(1)}, u32[]{:S(2)}, u32[]{:S(2)}) collective-permute-start(bf16[128,1536]{1,0:T(8,128)(2,1)S(1)} %convert_element_type.45), channel_id=1, source_target_pairs={{1,0},{3,2},{5,4},{7,6},{9,8},{11,10},{13,12},{15,14},{17,16},{19,... | collective-permute-start | bytes 1179656 | tf_op jit(solution)/shard_map/ppermute | solution.py:1500
  312.8 48.5 %collective-permute-start.41 = (bf16[128,4096]{1,0:T(8,128)(2,1)}, bf16[128,4096]{1,0:T(8,128)(2,1)}, u32[]{:S(2)}, u32[]{:S(2)}) collective-permute-start(bf16[128,4096]{1,0:T(8,128)(2,1)} %get-tuple-element.166.refs_8_), channel_id=1, source_target_pairs={{0,16},{4,20},{8,24},{12,28},{16,0},{20,4},{24,8},{28,12},{1,17},{... | collective-permute-start | bytes 3145736 | tf_op jit(solution)/shard_map/ppermute | solution.py:723
  314.2 47.1 %collective-permute-start.42 = (bf16[128,4096]{1,0:T(8,128)(2,1)}, bf16[128,4096]{1,0:T(8,128)(2,1)}, u32[]{:S(2)}, u32[]{:S(2)}) collective-permute-start(bf16[128,4096]{1,0:T(8,128)(2,1)} %get-tuple-element.168.refs_10_), channel_id=1, source_target_pairs={{0,8},{4,12},{8,0},{12,4},{16,24},{20,28},{24,16},{28,20},{1,9},{5... | collective-permute-start | bytes 3145736 | tf_op jit(solution)/shard_map/ppermute | solution.py:723
  318.9 48.3 %collective-permute-start.43 = (bf16[256,2048]{1,0:T(8,128)(2,1)}, bf16[256,2048]{1,0:T(8,128)(2,1)}, u32[]{:S(2)}, u32[]{:S(2)}) collective-permute-start(bf16[256,2048]{1,0:T(8,128)(2,1)} %get-tuple-element.171.refs_5_.refs_8_), channel_id=1, source_target_pairs={{0,16},{4,20},{8,24},{12,28},{16,0},{20,4},{24,8},{28,12},{1,17},{... | collective-permute-start | bytes 3145736 | tf_op jit(solution)/shard_map/ppermute | solution.py:723
  331.8 37.4 %collective-permute-start.44 = (bf16[256,1536]{1,0:T(8,128)(2,1)S(1)}, bf16[256,1536]{1,0:T(8,128)(2,1)}, u32[]{:S(2)}, u32[]{:S(2)}) collective-permute-start(bf16[256,1536]{1,0:T(8,128)(2,1)S(1)} %get-tuple-element.174.refs_3_.refs_10_), channel_id=1, source_target_pairs={{0,8},{4,12},{8,0},{12,4},{16,24},{20,28},{24,16},{28,20},{1,9},{5... | collective-permute-start | bytes 2359304 | tf_op jit(solution)/shard_map/ppermute | solution.py:723
  333.2 181.7 %reduce-scatter.4.cloned.1.call-start = ((), (), s32[]{:S(2)}) async-start(), calls=%async_computation.3 | async-start | bytes 2457600 | tf_op jit(solution)/shard_map/reduce_scatter | solution.py:1242
  377.0 51.1 %collective-permute-start.49 = (bf16[512,1024]{1,0:T(8,128)(2,1)S(1)}, bf16[512,1024]{1,0:T(8,128)(2,1)}, u32[]{:S(2)}, u32[]{:S(2)}) collective-permute-start(bf16[512,1024]{1,0:T(8,128)(2,1)S(1)} %shard_map.374.refs_19_), channel_id=1, source_target_pairs={{0,4},{4,0},{8,12},{12,8},{16,20},{20,16},{24,28},{28,24},{1,5},{5... | collective-permute-start | bytes 3145736 | tf_op jit(solution)/shard_map/ppermute | solution.py:723
  377.1 41.3 %collective-permute-start.47 = (bf16[128,2048]{1,0:T(8,128)(2,1)S(1)}, bf16[128,2048]{1,0:T(8,128)(2,1)S(1)}, u32[]{:S(2)}, u32[]{:S(2)}) collective-permute-start(bf16[128,2048]{1,0:T(8,128)(2,1)S(1)} %copy-done.17), channel_id=1, source_target_pairs={{0,8},{4,12},{8,0},{12,4},{16,24},{20,28},{24,16},{28,20},{1,9},{5... | collective-permute-start | bytes 1572872 | tf_op jit(solution)/shard_map/ppermute | solution.py:723
  377.9 40.6 %collective-permute-start.45 = (bf16[64,4096]{1,0:T(8,128)(2,1)S(1)}, bf16[64,4096]{1,0:T(8,128)(2,1)S(1)}, u32[]{:S(2)}, u32[]{:S(2)}) collective-permute-start(bf16[64,4096]{1,0:T(8,128)(2,1)S(1)} %copy-done.19), channel_id=1, source_target_pairs={{0,8},{4,12},{8,0},{12,4},{16,24},{20,28},{24,16},{28,20},{1,9},{5... | collective-permute-start | bytes 1572872 | tf_op jit(solution)/shard_map/ppermute | solution.py:723
  379.2 39.2 %collective-permute-start.46 = (bf16[64,4096]{1,0:T(8,128)(2,1)S(1)}, bf16[64,4096]{1,0:T(8,128)(2,1)S(1)}, u32[]{:S(2)}, u32[]{:S(2)}) collective-permute-start(bf16[64,4096]{1,0:T(8,128)(2,1)S(1)} %copy-done.74), channel_id=1, source_target_pairs={{0,16},{4,20},{8,24},{12,28},{16,0},{20,4},{24,8},{28,12},{1,17},{... | collective-permute-start | bytes 1572872 | tf_op jit(solution)/shard_map/ppermute | solution.py:723
  380.6 37.9 %collective-permute-start.48 = (bf16[128,1536]{1,0:T(8,128)(2,1)S(1)}, bf16[128,1536]{1,0:T(8,128)(2,1)S(1)}, u32[]{:S(2)}, u32[]{:S(2)}) collective-permute-start(bf16[128,1536]{1,0:T(8,128)(2,1)S(1)} %get-tuple-element.185.refs_12_.refs_18_), channel_id=1, source_target_pairs={{0,16},{4,20},{8,24},{12,28},{16,0},{20,4},{24,8},{28,12},{1,17},{... | collective-permute-start | bytes 1179656 | tf_op jit(solution)/shard_map/ppermute | solution.py:723
  423.5 104.7 %reduce-scatter.6.cloned.1.call-start = ((), (), s32[]{:S(2)}) async-start(), calls=%async_computation.4 | async-start | bytes 983040 | tf_op jit(solution)/shard_map/reduce_scatter | solution.py:1242
  451.0 20.8 %collective-permute-start.54 = (bf16[128,1024]{1,0:T(8,128)(2,1)S(1)}, bf16[128,1024]{1,0:T(8,128)(2,1)S(1)}, u32[]{:S(2)}, u32[]{:S(2)}) collective-permute-start(bf16[128,1024]{1,0:T(8,128)(2,1)S(1)} %get-tuple-element.195.refs_3_), channel_id=1, source_target_pairs={{0,16},{4,20},{8,24},{12,28},{16,0},{20,4},{24,8},{28,12},{1,17},{... | collective-permute-start | bytes 786440 | tf_op jit(solution)/shard_map/ppermute | solution.py:723
  451.7 20.1 %collective-permute-start.55 = (bf16[128,1024]{1,0:T(8,128)(2,1)S(1)}, bf16[128,1024]{1,0:T(8,128)(2,1)S(1)}, u32[]{:S(2)}, u32[]{:S(2)}) collective-permute-start(bf16[128,1024]{1,0:T(8,128)(2,1)S(1)} %get-tuple-element.197.refs_5_), channel_id=1, source_target_pairs={{0,8},{4,12},{8,0},{12,4},{16,24},{20,28},{24,16},{28,20},{1,9},{5... | collective-permute-start | bytes 786440 | tf_op jit(solution)/shard_map/ppermute | solution.py:723
  (156 other events, 1202.2 us)
Sparse Core Ops, SparseCore 0:
  23.0 58.1 all-gather.2
  333.3 23.8 reduce-scatter.7
  423.6 43.7 reduce-scatter.3
  503.2 24.9 reduce-scatter.5
